TPU v7x, 256 devices: a whole 4x4x8 slice. The times are simulated.
256 devices in a mesh: mom: 32 (over y, z_hi, x), hist: 8 (over z_lo, core).
Axes of the slice: x: 4, y: 4, z: 8 (z_hi: 2, z_lo: 4; z = z_hi * 4 + z_lo), core: 2. Of those that a mesh axis runs over, the one named last changes fastest.
Arguments:
- green_row: float32 [2, 2, 3, 3, 2048, 4096], P(None, None, None, None, 'hist', 'mom'), may hold values from -6 to 6
- time_step: int32 [1], replicated, may hold values from 0 to 8388607
Outputs:
- collision: float32 [2, 3, 3, 4096], P(None, None, None, ('mom', 'hist'))
Inputs may be any that keep to these rules, and one draw needn't show every extreme that they name: History slot j holds the step ((time_step - 1 - j) mod 2048) + 1 steps before the current one.
All inputs are finite; a program needn't handle non-finite values.
Results may differ from a plain program's by a relative error of at most 0.00013.
Values sent between devices are 32-bit elements; how exact they have to be, the bound alone decides.
No kernel may reach another device: no remote copies, remote signals or barrier semaphores. Data moves between devices by JAX's collectives and lax.ppermute only.
A program may use at most 320 MiB of HBM per device.

v0:
```python
import math

import jax
import jax.numpy as jnp
import numpy as np
from jax import lax
from jax.experimental import pallas as pl
from jax.experimental.pallas import tpu as pltpu
from jax.sharding import PartitionSpec as P

NKX = 64
NKY = 64
ORB = 3
PAIRS = ORB * ORB
ROWS = 32
SLOTS = 8
LANES = 128

delta_time = 0.01


def lane_tables():
    index = np.arange(64)
    angle = 2.0 * math.pi * (index[:, None] * index[None, :] % 64) / 64
    sign = np.array([[1.0, 1.0], [1.0, -1.0]])
    cosine = np.kron(sign, np.cos(angle)) / 64
    sine = np.kron(sign, np.sin(angle)) / 64
    table = np.block([[cosine, sine], [-sine, cosine]]).astype(np.float32)
    high = table.astype(jnp.bfloat16)
    low = (table - high.astype(np.float32)).astype(jnp.bfloat16)
    turn = 2.0 * math.pi * np.arange(ROWS)[:, None] * np.repeat([0, 1], 64)[None, :] / 64
    twiddle = np.stack([np.cos(turn), np.sin(turn)], 1).astype(np.float32)
    return high, low, twiddle


def turned(value, step, length):
    real, imag = value
    eighths = step * 8 / length
    if eighths == 0:
        return real, imag
    if eighths == 2:
        return -imag, real
    if eighths == 4:
        return -real, -imag
    if eighths == 6:
        return imag, -real
    root = math.sqrt(0.5)
    if eighths == 1:
        return root * (real - imag), root * (real + imag)
    if eighths == 3:
        return -root * (real + imag), root * (real - imag)
    if eighths == 5:
        return root * (imag - real), -root * (real + imag)
    if eighths == 7:
        return root * (real + imag), root * (imag - real)
    cosine, sine = math.cos(2 * math.pi * step / length), math.sin(2 * math.pi * step / length)
    return real * cosine - imag * sine, real * sine + imag * cosine


def plus(first, second):
    return first[0] + second[0], first[1] + second[1]


def minus(first, second):
    return first[0] - second[0], first[1] - second[1]


def fourier(values):
    length = len(values)
    if length == 1:
        return values
    if length == 2:
        return [plus(*values), minus(*values)]
    quarter = length // 4
    parts = [fourier(values[start::4]) for start in range(4)]
    out = [None] * length
    for m in range(quarter):
        first, second, third, fourth = (turned(parts[p][m], p * m, length) for p in range(4))
        even, odd = plus(first, third), minus(first, third)
        other, cross = plus(second, fourth), minus(second, fourth)
        cross = (-cross[1], cross[0])
        out[m], out[m + 2 * quarter] = plus(even, other), minus(even, other)
        out[m + quarter], out[m + 3 * quarter] = plus(odd, cross), minus(odd, cross)
    return out


def product(values, high, low):
    head = values.astype(jnp.bfloat16)
    tail = (values - head.astype(jnp.float32)).astype(jnp.bfloat16)

    def dot(left, right):
        return jnp.dot(left, right, preferred_element_type=jnp.float32)

    return dot(head, high) + (dot(tail, high) + dot(head, low))


def kernel(green, weight, high_ref, low_ref, twiddle, out, field):
    def spot(part):
        return pl.ds(part * LANES, LANES)

    def twist(n):
        return twiddle[n, 0][None, :], twiddle[n, 1][None, :]

    def times(value, factor):
        return value[0] * factor[0] - value[1] * factor[1], value[0] * factor[1] + value[1] * factor[0]

    @pl.loop(0, 2 * PAIRS)
    def _(s):
        comp, pair = s // PAIRS, s % PAIRS
        at = comp * 2 * PAIRS + pair
        rows = pl.ds(pl.multiple_of(comp * SLOTS, SLOTS), SLOTS)
        values = [(green[m, at], green[m, at + PAIRS]) for m in range(ROWS)]
        for n, value in enumerate(fourier(values)):
            real, imag = times(value, twist(n)) if n else value
            field[n, pair, rows, spot(0)] = real
            field[n, pair, rows, spot(1)] = imag

    block = 4
    size = block * PAIRS * 2 * SLOTS

    @pl.loop(0, ROWS // block)
    def _(b):
        take = pl.ds(b * block, block)
        high, low = high_ref[...], low_ref[...]
        space = product(field[take].reshape(size, 2 * LANES), high, low)
        space = space.reshape(block * PAIRS, 2, SLOTS, 2 * LANES)
        less = space[:, 0, :, :LANES], space[:, 0, :, LANES:]
        great = space[:, 1, :, :LANES], space[:, 1, :, LANES:]

        def bubble(first, other):
            real = first[0] * first[0] - first[1] * first[1]
            imag = 2.0 * first[0] * first[1]
            return -(real * other[0] + imag * other[1]), imag * other[0] - real * other[1]

        sigma = jnp.stack(
            [jnp.concatenate(bubble(less, great), -1), jnp.concatenate(bubble(great, less), -1)], 1
        )
        back = product(sigma.reshape(size, 2 * LANES), high, low)
        field[take] = back.reshape(block, PAIRS, 2 * SLOTS, 2 * LANES)

    @pl.loop(0, 2 * PAIRS)
    def _(s):
        comp, pair = s // PAIRS, s % PAIRS
        rows = pl.ds(pl.multiple_of(comp * SLOTS, SLOTS), SLOTS)
        values = [(field[n, pair, rows, spot(0)], field[n, pair, rows, spot(1)]) for n in range(ROWS)]
        values = [times(value, twist(n)) if n else value for n, value in enumerate(values)]
        for m, (real, imag) in enumerate(fourier(values)):
            field[m, pair, rows, spot(0)] = real
            field[m, pair, rows, spot(1)] = imag

    scale = weight[...]

    @pl.loop(0, ROWS)
    def _(m):
        def sigma(comp, a, c):
            rows = pl.ds(comp * SLOTS, SLOTS)
            return field[m, a * ORB + c, rows, spot(0)], field[m, a * ORB + c, rows, spot(1)]

        def given(comp, b, c):
            at = comp * 2 * PAIRS + b * ORB + c
            return green[m, at], green[m, at + PAIRS]

        def memory(a, b):
            real, imag = 0.0, 0.0
            for c in range(ORB):
                for comp in range(2):
                    left, right = sigma(comp, a, c), given(1 - comp, b, c)
                    term = left[0] * right[0] - left[1] * right[1]
                    cross = left[0] * right[1] + left[1] * right[0] if a != b else 0.0
                    real, imag = (real + term, imag + cross) if comp == 0 else (real - term, imag - cross)
            return real, imag

        results = [2.0 * memory(a, a)[0] for a in range(ORB)]
        for a, b in ((0, 1), (0, 2), (1, 2)):
            one, two = memory(a, b), memory(b, a)
            results += [one[0] + two[0], two[1] - one[1]]
        for i, result in enumerate(results):
            out[i, pl.ds(m, 1), :] = jnp.sum(result * scale, axis=0, keepdims=True)


def collide(green, weights, high, low, twiddle):
    return pl.pallas_call(
        kernel,
        out_shape=jax.ShapeDtypeStruct((PAIRS, ROWS, LANES), jnp.float32),
        in_specs=[pl.BlockSpec(memory_space=pltpu.VMEM)] * 5,
        out_specs=pl.BlockSpec(memory_space=pltpu.VMEM),
        scratch_shapes=[pltpu.VMEM((ROWS, PAIRS, 2 * SLOTS, 2 * LANES), jnp.float32)],
        compiler_params=pltpu.CompilerParams(vmem_limit_bytes=48 * 1024 * 1024),
    )(green, weights, high, low, twiddle)


def per_device(green_row, time_step):
    slot_count = green_row.shape[4]
    hist_count = lax.axis_size("hist")
    history = slot_count * hist_count
    slot_ids = (
        lax.axis_index("hist") * slot_count
        + lax.axis_index("mom") * SLOTS
        + jnp.arange(SLOTS, dtype=jnp.int32)
    )
    slot_age = (time_step[0] - 1 - slot_ids) % history + 1
    decays = jnp.exp2(-(slot_age - 1).astype(jnp.float32) / history)
    weights = delta_time * decays * jnp.where(slot_age == history, 0.5, 1.0).astype(jnp.float32)
    weights = jnp.broadcast_to(weights[:, None], (SLOTS, LANES))
    high, low, twiddle = lane_tables()

    parts = green_row.reshape(4 * PAIRS, ROWS, SLOTS, LANES)
    arrived = lax.all_to_all(parts, "mom", split_axis=1, concat_axis=0)
    partial = collide(arrived, weights, high, low, twiddle)
    flat = partial.reshape(PAIRS, ROWS * LANES)
    summed = lax.psum_scatter(flat, ("mom", "hist"), scatter_dimension=1, tiled=True)
    zero = jnp.zeros_like(summed[0])
    real = [summed[0], summed[3], summed[5], summed[3], summed[1], summed[7], summed[5], summed[7], summed[2]]
    imag = [zero, summed[4], summed[6], -summed[4], zero, summed[8], -summed[6], -summed[8], zero]
    return jnp.stack(real + imag).reshape(2, ORB, ORB, -1)


def solution(mesh):
    placed = (P(None, None, None, None, "hist", "mom"), P())
    return jax.shard_map(
        per_device,
        mesh=mesh,
        in_specs=placed,
        out_specs=P(None, None, None, ("mom", "hist")),
        check_vma=False,
    )
```

profile of v0, /device:TPU:1, one launch (start us, length us, event | category | flops | bytes accessed | tf_op | source)
XLA Modules:
  0.0 1430.9 jit_solution(1405377642638030224)
XLA Ops:
  6.5 5.1 copy.8
  11.6 0.0 copy-start
  11.6 0.0 copy-start.1
  11.6 0.0 copy-start.2
  11.6 14.7 %all-to-all-start = ((f32[1,36,32,8,128]{4,3,1,0,2:T(8,128)}), f32[1,36,32,8,128]{4,3,1,0,2:T(8,128)}, u32[]{:S(2)}, u32[]{:S(2)}) async-start(f32[1,36,32,8,128]{4,3,1,0,2:T(8,128)} %copy.8), calls=%async_computation | async-start | bytes 9437184 | tf_op jit(solution)/shard_map/all_to_all | solution.py:208
  26.4 0.0 reduce-scatter.4.cloned.1.call-start
  27.1 76.1 %all-to-all-done = f32[1,36,32,8,128]{4,3,1,0,2:T(8,128)} async-done(((f32[1,36,32,8,128]{4,3,1,0,2:T(8,128)}), f32[1,36,32,8,128]{4,3,1,0,2:T(8,128)}, u32[]{:S(2)}, u32[]{:S(2)}) %all-to-all-start) | async-done | bytes 4718624 | tf_op jit(solution)/shard_map/all_to_all | solution.py:208
  103.2 0.1 broadcast_in_dim.16.weight
  103.3 0.0 copy-done
  103.3 0.0 copy-done.1
  103.3 0.0 copy-done.2
  103.3 17.4 %shard_map.55 = f32[9,32,128]{2,1,0:T(8,128)S(1)} custom-call(f32[32,36,8,128]{3,2,1,0:T(8,128)} %bitcast.5.green, f32[8,128]{1,0:T(8,128)S(1)} %broadcast_in_dim.16.weight, bf16[256,256]{1,0:T(8,128)(2,1)S(1)} %copy-done, bf16[256,256]{1,0:T(8,128)(2,1)S(1)} %copy-done.1, f32[32,2,128]{2,1,0:T(2,128)S(1)} %copy-done.2), custom_call_target="tpu_custom_call" | custom-call | tf_op jit(solution)/shard_map/pallas_call | solution.py:182
  120.7 2.0 copy.12
  122.7 0.0 reduce-scatter.4.cloned.1.call-update
  122.8 1298.7 %reduce-scatter.4.cloned.1.call-done = f32[16,9]{1,0:T(8,128)} async-done(((f32[4096,9]{1,0:T(8,128)}), f32[16,9]{1,0:T(8,128)}) %reduce-scatter.4.cloned.1.call-update) | async-done | bytes 592
  1421.5 1.1 fusion.2
  1422.6 0.1 copy.13
  1422.7 0.1 copy.14
  1422.8 0.1 copy.15
  1422.8 0.1 copy.16
  1422.9 0.1 copy.17
  1423.0 0.1 copy.18
  1423.1 0.1 copy.19
  1423.1 0.1 copy.20
  1423.2 0.1 copy.21
  1423.3 0.1 stack.2
  1423.4 0.6 copy.9
  (6 shorter events, 0.0 us)
Async XLA Ops:
  11.6 91.7 %copy-start = (bf16[256,256]{1,0:T(8,128)(2,1)S(1)}, bf16[256,256]{1,0:T(8,128)(2,1)}, u32[]{:S(2)}) copy-start(bf16[256,256]{1,0:T(8,128)(2,1)} %constant.56.clone.high_ref) | copy-start | bytes 393220
  11.6 91.7 %copy-start.1 = (bf16[256,256]{1,0:T(8,128)(2,1)S(1)}, bf16[256,256]{1,0:T(8,128)(2,1)}, u32[]{:S(2)}) copy-start(bf16[256,256]{1,0:T(8,128)(2,1)} %constant.57.clone.low_ref) | copy-start | bytes 393220
  11.6 91.7 %copy-start.2 = (f32[32,2,128]{2,1,0:T(2,128)S(1)}, f32[32,2,128]{2,1,0:T(2,128)}, u32[]{:S(2)}) copy-start(f32[32,2,128]{2,1,0:T(2,128)} %constant.58.clone.twiddle) | copy-start | bytes 98308
  11.6 91.6 %all-to-all-start = ((f32[1,36,32,8,128]{4,3,1,0,2:T(8,128)}), f32[1,36,32,8,128]{4,3,1,0,2:T(8,128)}, u32[]{:S(2)}, u32[]{:S(2)}) async-start(f32[1,36,32,8,128]{4,3,1,0,2:T(8,128)} %copy.8), calls=%async_computation | async-start | bytes 9437184 | tf_op jit(solution)/shard_map/all_to_all | solution.py:208
  26.4 1395.1 %reduce-scatter.4.cloned.1.call-start = ((), (), s32[]{:S(2)}) async-start(), calls=%async_computation.2 | async-start | bytes 2105344
Sparse Core Ops, SparseCore 0:
  122.9 1298.5 reduce-scatter.3
where the time goes:
time: 1440 us; the launch traced here: 1430 us
  waiting for transfers between devices  1370 us (95%)
  Pallas kernels  17.4 us (1%)
  starting transfers between devices  14.8 us (1%)
    unnamed x2, waiting for transfers between devices  1300 us
    all_to_all x1, waiting for transfers between devices, per_device(): arrived = lax.all_to_all(parts, 'mom', split_axis=1, concat_axis=0)  76.1 us
  transfers between devices with their start and end apart: 2, of which 2 were waited for; matrix products, arithmetic and copies ran while one was open for 0% of the time, Pallas kernels for 0%

commit v1 on v0

--- a/solution.py
+++ b/solution.py
@@ -94,7 +94,7 @@
     return dot(head, high) + (dot(tail, high) + dot(head, low))
 
 
-def kernel(green, weight, high_ref, low_ref, twiddle, out, field):
+def kernel(green, weight, high_ref, low_ref, twiddle, before, out, field):
     def spot(part):
         return pl.ds(part * LANES, LANES)
 
@@ -104,26 +104,26 @@
     def times(value, factor):
         return value[0] * factor[0] - value[1] * factor[1], value[0] * factor[1] + value[1] * factor[0]
 
-    @pl.loop(0, 2 * PAIRS)
+    @pl.loop(0, 2 * ORB)
     def _(s):
-        comp, pair = s // PAIRS, s % PAIRS
-        at = comp * 2 * PAIRS + pair
+        comp, pair = s // ORB, s % ORB
+        at = comp * 2 * ORB + pair
         rows = pl.ds(pl.multiple_of(comp * SLOTS, SLOTS), SLOTS)
-        values = [(green[m, at], green[m, at + PAIRS]) for m in range(ROWS)]
+        values = [(green[m, at], green[m, at + ORB]) for m in range(ROWS)]
         for n, value in enumerate(fourier(values)):
             real, imag = times(value, twist(n)) if n else value
             field[n, pair, rows, spot(0)] = real
             field[n, pair, rows, spot(1)] = imag
 
-    block = 4
-    size = block * PAIRS * 2 * SLOTS
+    block = 8
+    size = block * ORB * 2 * SLOTS
 
     @pl.loop(0, ROWS // block)
     def _(b):
         take = pl.ds(b * block, block)
         high, low = high_ref[...], low_ref[...]
         space = product(field[take].reshape(size, 2 * LANES), high, low)
-        space = space.reshape(block * PAIRS, 2, SLOTS, 2 * LANES)
+        space = space.reshape(block * ORB, 2, SLOTS, 2 * LANES)
         less = space[:, 0, :, :LANES], space[:, 0, :, LANES:]
         great = space[:, 1, :, :LANES], space[:, 1, :, LANES:]
 
@@ -136,11 +136,11 @@
             [jnp.concatenate(bubble(less, great), -1), jnp.concatenate(bubble(great, less), -1)], 1
         )
         back = product(sigma.reshape(size, 2 * LANES), high, low)
-        field[take] = back.reshape(block, PAIRS, 2 * SLOTS, 2 * LANES)
-
-    @pl.loop(0, 2 * PAIRS)
+        field[take] = back.reshape(block, ORB, 2 * SLOTS, 2 * LANES)
+
+    @pl.loop(0, 2 * ORB)
     def _(s):
-        comp, pair = s // PAIRS, s % PAIRS
+        comp, pair = s // ORB, s % ORB
         rows = pl.ds(pl.multiple_of(comp * SLOTS, SLOTS), SLOTS)
         values = [(field[n, pair, rows, spot(0)], field[n, pair, rows, spot(1)]) for n in range(ROWS)]
         values = [times(value, twist(n)) if n else value for n, value in enumerate(values)]
@@ -152,22 +152,21 @@
 
     @pl.loop(0, ROWS)
     def _(m):
-        def sigma(comp, a, c):
+        def sigma(comp, a):
             rows = pl.ds(comp * SLOTS, SLOTS)
-            return field[m, a * ORB + c, rows, spot(0)], field[m, a * ORB + c, rows, spot(1)]
-
-        def given(comp, b, c):
-            at = comp * 2 * PAIRS + b * ORB + c
-            return green[m, at], green[m, at + PAIRS]
+            return field[m, a, rows, spot(0)], field[m, a, rows, spot(1)]
+
+        def given(comp, b):
+            at = comp * 2 * ORB + b
+            return green[m, at], green[m, at + ORB]
 
         def memory(a, b):
-            real, imag = 0.0, 0.0
-            for c in range(ORB):
-                for comp in range(2):
-                    left, right = sigma(comp, a, c), given(1 - comp, b, c)
-                    term = left[0] * right[0] - left[1] * right[1]
-                    cross = left[0] * right[1] + left[1] * right[0] if a != b else 0.0
-                    real, imag = (real + term, imag + cross) if comp == 0 else (real - term, imag - cross)
+            left, right = sigma(0, a), given(1, b)
+            other, cross = sigma(1, a), given(0, b)
+            real = left[0] * right[0] - left[1] * right[1] - other[0] * cross[0] + other[1] * cross[1]
+            if a == b:
+                return real, None
+            imag = left[0] * right[1] + left[1] * right[0] - other[0] * cross[1] - other[1] * cross[0]
             return real, imag
 
         results = [2.0 * memory(a, a)[0] for a in range(ORB)]
@@ -175,18 +174,20 @@
             one, two = memory(a, b), memory(b, a)
             results += [one[0] + two[0], two[1] - one[1]]
         for i, result in enumerate(results):
-            out[i, pl.ds(m, 1), :] = jnp.sum(result * scale, axis=0, keepdims=True)
-
-
-def collide(green, weights, high, low, twiddle):
+            row = pl.ds(i, 1)
+            out[m, row, :] = before[m, row, :] + jnp.sum(result * scale, axis=0, keepdims=True)
+
+
+def collide(green, weights, high, low, twiddle, before):
     return pl.pallas_call(
         kernel,
-        out_shape=jax.ShapeDtypeStruct((PAIRS, ROWS, LANES), jnp.float32),
-        in_specs=[pl.BlockSpec(memory_space=pltpu.VMEM)] * 5,
+        out_shape=jax.ShapeDtypeStruct((ROWS, PAIRS, LANES), jnp.float32),
+        in_specs=[pl.BlockSpec(memory_space=pltpu.VMEM)] * 6,
         out_specs=pl.BlockSpec(memory_space=pltpu.VMEM),
-        scratch_shapes=[pltpu.VMEM((ROWS, PAIRS, 2 * SLOTS, 2 * LANES), jnp.float32)],
-        compiler_params=pltpu.CompilerParams(vmem_limit_bytes=48 * 1024 * 1024),
-    )(green, weights, high, low, twiddle)
+        scratch_shapes=[pltpu.VMEM((ROWS, ORB, 2 * SLOTS, 2 * LANES), jnp.float32)],
+        compiler_params=pltpu.CompilerParams(vmem_limit_bytes=24 * 1024 * 1024),
+        cost_estimate=pl.CostEstimate(flops=2_000_000_000, bytes_accessed=4_000_000, transcendentals=0),
+    )(green, weights, high, low, twiddle, before)
 
 
 def per_device(green_row, time_step):
@@ -204,11 +205,16 @@
     weights = jnp.broadcast_to(weights[:, None], (SLOTS, LANES))
     high, low, twiddle = lane_tables()
 
-    parts = green_row.reshape(4 * PAIRS, ROWS, SLOTS, LANES)
-    arrived = lax.all_to_all(parts, "mom", split_axis=1, concat_axis=0)
-    partial = collide(arrived, weights, high, low, twiddle)
-    flat = partial.reshape(PAIRS, ROWS * LANES)
-    summed = lax.psum_scatter(flat, ("mom", "hist"), scatter_dimension=1, tiled=True)
+    parts = green_row.reshape(4 * ORB, ORB, ROWS, SLOTS, LANES)
+    arrived = [
+        lax.all_to_all(parts[:, c], "mom", split_axis=1, concat_axis=0) for c in range(ORB)
+    ]
+    partial = jnp.zeros((ROWS, PAIRS, LANES), jnp.float32)
+    for part in arrived:
+        partial = collide(part, weights, high, low, twiddle, partial)
+    owned = jnp.sum(lax.all_to_all(partial, "mom", split_axis=0, concat_axis=0), axis=0)
+    shares = owned.reshape(PAIRS, hist_count, LANES // hist_count).transpose(1, 0, 2)
+    summed = jnp.sum(lax.all_to_all(shares, "hist", split_axis=0, concat_axis=0), axis=0)
     zero = jnp.zeros_like(summed[0])
     real = [summed[0], summed[3], summed[5], summed[3], summed[1], summed[7], summed[5], summed[7], summed[2]]
     imag = [zero, summed[4], summed[6], -summed[4], zero, summed[8], -summed[6], -summed[8], zero]

time: 1440 us -> 182 us (0.13)
  waiting for transfers between devices: 1370 us -> 59.6 us
  blocking collectives: 0 us -> 62.2 us
    unnamed x2 -> x0, waiting for transfers between devices: 1300 us -> none
    all_to_all x0 -> x2, blocking collectives: none -> 62.2 us  [the longest x1 39.4 us: per_device(): lax.all_to_all(shares, 'hist', split_axis=0, concat_axis=0)]
    all_to_all x1 -> x3, waiting for transfers between devices: 76.1 us -> 59.6 us  [per_device(): lax.all_to_all(parts[:, c], 'mom', split_axis=1, concat_axis=0)]
  transfers between devices with their start and end apart: 2 -> 3, of which waited for: 2 -> 3; matrix products, arithmetic and copies ran while one was open for 0% -> 2% of each run, Pallas kernels for 0% -> 6%
where the time goes in v1:
time: 182 us; the launch traced here: 181 us
  blocking collectives  62.2 us (34%)
  waiting for transfers between devices  59.6 us (33%)
  starting transfers between devices  27.9 us (15%)
  Pallas kernels  18.8 us (10%)
  local copies, waits for them, and re-layouts  11 us (6%)
    all_to_all x3, waiting for transfers between devices, per_device(): lax.all_to_all(parts[:, c], 'mom', split_axis=1, concat_axis=0)  59.6 us
    all_to_all x1, blocking collectives, per_device(): lax.all_to_all(shares, 'hist', split_axis=0, concat_axis=0)  39.4 us
    all_to_all x3, starting transfers between devices, per_device(): lax.all_to_all(parts[:, c], 'mom', split_axis=1, concat_axis=0)  27.9 us
    all_to_all x1, blocking collectives, per_device(): lax.all_to_all(partial, 'mom', split_axis=0, concat_axis=0)  22.8 us
    pallas_call x3, Pallas kernels, collide(): pl.pallas_call(kernel, out_shape=jax.ShapeDtypeStruct((ROWS, PAIRS, LANES...  18.8 us
    another operation x4, local copies, waits for them, and re-layouts, per_device(): lax.all_to_all(parts[:, c], 'mom', split_axis=1, concat_axis=0)  9.45 us
  transfers between devices with their start and end apart: 3, of which 3 were waited for; matrix products, arithmetic and copies ran while one was open for 2% of the time, Pallas kernels for 6%

profile of v1, /device:TPU:1, one launch (start us, length us, event | category | flops | bytes accessed | tf_op | source)
XLA Modules:
  0.0 181.0 jit_solution(17817920937106339640)
XLA Ops:
  0.0 4.0 %slice_bitcast_fusion = (f32[1,12,32,8,128]{4,3,2,1,0:T(8,128)S(1)}, f32[1,12,32,8,128]{4,3,2,1,0:T(8,128)S(1)}, f32[1,12,32,8,128]{4,3,2,1,0:T(8,128)}) fusion(f32[12,3,32,8,128]{4,3,2,1,0:T(8,128)} %bitcast.26), kind=kLoop, calls=%fused_computation | loop fusion | bytes 9437184 | tf_op jit(solution)/shard_map/broadcast_in_dim;squeeze | solution.py:210
  4.0 1.4 copy.16
  5.3 14.5 %all-to-all-start.2 = ((f32[1,12,32,8,128]{4,3,1,0,2:T(8,128)}), f32[1,12,32,8,128]{4,3,1,0,2:T(8,128)S(1)}, u32[]{:S(2)}, u32[]{:S(2)}) async-start(f32[1,12,32,8,128]{4,3,1,0,2:T(8,128)} %copy.16), calls=%async_computation.2 | async-start | bytes 3145728 | tf_op jit(solution)/shard_map/all_to_all | solution.py:210
  19.8 1.3 copy.15
  21.2 27.3 %all-to-all-done.2 = f32[1,12,32,8,128]{4,3,1,0,2:T(8,128)S(1)} async-done(((f32[1,12,32,8,128]{4,3,1,0,2:T(8,128)}), f32[1,12,32,8,128]{4,3,1,0,2:T(8,128)S(1)}, u32[]{:S(2)}, u32[]{:S(2)}) %all-to-all-start.2) | async-done | bytes 1572896 | tf_op jit(solution)/shard_map/all_to_all | solution.py:210
  48.5 4.6 %all-to-all-start.1 = ((f32[1,12,32,8,128]{4,3,1,0,2:T(8,128)}), f32[1,12,32,8,128]{4,3,1,0,2:T(8,128)S(1)}, u32[]{:S(2)}, u32[]{:S(2)}) async-start(f32[1,12,32,8,128]{4,3,1,0,2:T(8,128)} %copy.15), calls=%async_computation.1 | async-start | bytes 3145728 | tf_op jit(solution)/shard_map/all_to_all | solution.py:210
  53.1 2.8 %copy.14 = f32[1,12,32,8,128]{4,3,1,0,2:T(8,128)} copy(f32[1,12,32,8,128]{4,3,2,1,0:T(8,128)} %get-tuple-element.7) | data formatting | bytes 3145728 | tf_op jit(solution)/shard_map/broadcast_in_dim;squeeze | solution.py:210
  55.9 0.0 copy-start
  55.9 0.0 copy-start.1
  55.9 0.0 copy-start.2
  55.9 14.9 %all-to-all-done.1 = f32[1,12,32,8,128]{4,3,1,0,2:T(8,128)S(1)} async-done(((f32[1,12,32,8,128]{4,3,1,0,2:T(8,128)}), f32[1,12,32,8,128]{4,3,1,0,2:T(8,128)S(1)}, u32[]{:S(2)}, u32[]{:S(2)}) %all-to-all-start.1) | async-done | bytes 1572896 | tf_op jit(solution)/shard_map/all_to_all | solution.py:210
  70.8 8.8 %all-to-all-start = ((f32[1,12,32,8,128]{4,3,1,0,2:T(8,128)}), f32[1,12,32,8,128]{4,3,1,0,2:T(8,128)}, u32[]{:S(2)}, u32[]{:S(2)}) async-start(f32[1,12,32,8,128]{4,3,1,0,2:T(8,128)} %copy.14), calls=%async_computation | async-start | bytes 3145728 | tf_op jit(solution)/shard_map/all_to_all | solution.py:210
  80.3 0.1 broadcast_in_dim.19.weight
  80.4 0.0 copy-done
  80.4 0.0 copy-done.1
  80.4 0.0 copy-done.2
  80.4 5.8 %shard_map.55.before = f32[32,9,128]{2,1,0:T(8,128)S(1)} custom-call(f32[32,12,8,128]{3,2,1,0:T(8,128)S(1)} %bitcast.24, f32[8,128]{1,0:T(8,128)S(1)} %broadcast_in_dim.19.weight, bf16[256,256]{1,0:T(8,128)(2,1)S(1)} %copy-done, bf16[256,256]{1,0:T(8,128)(2,1)S(1)} %copy-done.1, f32[32,2,128]{2,1,0:T(2,128)S(1)} %copy-done.2, ...), custom_call_target="tpu_custom_call" | custom-call | flops 2000000000 | bytes 4000000 | tf_op jit(solution)/shard_map/pallas_call | solution.py:182
  86.2 5.8 %shard_map.56.before = f32[32,9,128]{2,1,0:T(8,128)S(1)} custom-call(f32[32,12,8,128]{3,2,1,0:T(8,128)S(1)} %bitcast.25, f32[8,128]{1,0:T(8,128)S(1)} %broadcast_in_dim.19.weight, bf16[256,256]{1,0:T(8,128)(2,1)S(1)} %copy-done, bf16[256,256]{1,0:T(8,128)(2,1)S(1)} %copy-done.1, f32[32,2,128]{2,1,0:T(2,128)S(1)} %copy-done.2, f32[32,9,128]{2,1,0:T(8,128)S(1)} %shard_map.55.before), custom_call_target="tpu_custom_call" | custom-call | flops 2000000000 | bytes 4000000 | tf_op jit(solution)/shard_map/pallas_call | solution.py:182
  92.0 17.4 %all-to-all-done = f32[1,12,32,8,128]{4,3,1,0,2:T(8,128)} async-done(((f32[1,12,32,8,128]{4,3,1,0,2:T(8,128)}), f32[1,12,32,8,128]{4,3,1,0,2:T(8,128)}, u32[]{:S(2)}, u32[]{:S(2)}) %all-to-all-start) | async-done | bytes 1572896 | tf_op jit(solution)/shard_map/all_to_all | solution.py:210
  109.4 7.2 %shard_map.57 = f32[32,9,128]{2,1,0:T(8,128)S(1)} custom-call(f32[32,12,8,128]{3,2,1,0:T(8,128)} %bitcast.4.green, f32[8,128]{1,0:T(8,128)S(1)} %broadcast_in_dim.19.weight, bf16[256,256]{1,0:T(8,128)(2,1)S(1)} %copy-done, bf16[256,256]{1,0:T(8,128)(2,1)S(1)} %copy-done.1, f32[32,2,128]{2,1,0:T(2,128)S(1)} %copy-done.2, f32[32,9,128]{2,1,0:T(8,128)S(1)} %shard_map.56.before), custom_call_target="tpu_custom_call" | custom-call | flops 2000000000 | bytes 4000000 | tf_op jit(solution)/shard_map/pallas_call | solution.py:182
  116.6 22.8 %all_to_all.55 = f32[32,9,128]{2,1,0:T(8,128)S(1)} all-to-all(f32[32,9,128]{2,1,0:T(8,128)S(1)} %shard_map.57), channel_id=1, replica_groups=mesh['mom'=32,'hist'=8] {'mom'}, dimensions={0} | all-to-all | bytes 294912 | tf_op jit(solution)/shard_map/all_to_all | solution.py:215
  139.5 0.1 reshape.41
  139.6 0.1 reshape.43
  139.7 39.4 %all_to_all.56 = f32[8,1,144]{2,1,0:T(1,128)S(1)} all-to-all(f32[8,1,144]{2,1,0:T(1,128)S(1)} %reshape.43), channel_id=1, replica_groups=mesh['mom'=32,'hist'=8] {'hist'}, dimensions={0} | all-to-all | bytes 9216 | tf_op jit(solution)/shard_map/all_to_all | solution.py:217
  179.0 0.5 broadcast.84
  179.5 0.7 reduce
  180.2 0.1 reshape.44
  180.3 0.1 stack.2
  180.4 0.6 copy.18
  (8 shorter events, 0.1 us)
Async XLA Ops:
  5.3 43.2 %all-to-all-start.2 = ((f32[1,12,32,8,128]{4,3,1,0,2:T(8,128)}), f32[1,12,32,8,128]{4,3,1,0,2:T(8,128)S(1)}, u32[]{:S(2)}, u32[]{:S(2)}) async-start(f32[1,12,32,8,128]{4,3,1,0,2:T(8,128)} %copy.16), calls=%async_computation.2 | async-start | bytes 3145728 | tf_op jit(solution)/shard_map/all_to_all | solution.py:210
  48.5 22.3 %all-to-all-start.1 = ((f32[1,12,32,8,128]{4,3,1,0,2:T(8,128)}), f32[1,12,32,8,128]{4,3,1,0,2:T(8,128)S(1)}, u32[]{:S(2)}, u32[]{:S(2)}) async-start(f32[1,12,32,8,128]{4,3,1,0,2:T(8,128)} %copy.15), calls=%async_computation.1 | async-start | bytes 3145728 | tf_op jit(solution)/shard_map/all_to_all | solution.py:210
  55.9 24.5 %copy-start = (bf16[256,256]{1,0:T(8,128)(2,1)S(1)}, bf16[256,256]{1,0:T(8,128)(2,1)}, u32[]{:S(2)}) copy-start(bf16[256,256]{1,0:T(8,128)(2,1)} %constant.58.clone.high_ref) | copy-start | bytes 393220
  55.9 24.5 %copy-start.1 = (bf16[256,256]{1,0:T(8,128)(2,1)S(1)}, bf16[256,256]{1,0:T(8,128)(2,1)}, u32[]{:S(2)}) copy-start(bf16[256,256]{1,0:T(8,128)(2,1)} %constant.59.clone.low_ref) | copy-start | bytes 393220
  55.9 24.5 %copy-start.2 = (f32[32,2,128]{2,1,0:T(2,128)S(1)}, f32[32,2,128]{2,1,0:T(2,128)}, u32[]{:S(2)}) copy-start(f32[32,2,128]{2,1,0:T(2,128)} %constant.60.clone.twiddle) | copy-start | bytes 98308
  70.8 38.6 %all-to-all-start = ((f32[1,12,32,8,128]{4,3,1,0,2:T(8,128)}), f32[1,12,32,8,128]{4,3,1,0,2:T(8,128)}, u32[]{:S(2)}, u32[]{:S(2)}) async-start(f32[1,12,32,8,128]{4,3,1,0,2:T(8,128)} %copy.14), calls=%async_computation | async-start | bytes 3145728 | tf_op jit(solution)/shard_map/all_to_all | solution.py:210

commit v2 on v1

--- a/solution.py
+++ b/solution.py
@@ -1,3 +1,4 @@
+import functools
 import math
 
 import jax
@@ -6,6 +7,7 @@
 from jax import lax
 from jax.experimental import pallas as pl
 from jax.experimental.pallas import tpu as pltpu
+from jax.sharding import Mesh
 from jax.sharding import PartitionSpec as P
 
 NKX = 64
@@ -13,6 +15,7 @@
 ORB = 3
 PAIRS = ORB * ORB
 ROWS = 32
+PLANE = 16
 SLOTS = 8
 LANES = 128
 
@@ -94,7 +97,19 @@
     return dot(head, high) + (dot(tail, high) + dot(head, low))
 
 
-def kernel(green, weight, high_ref, low_ref, twiddle, before, out, field):
+def kernel(turn, *refs):
+    *given_refs, weight, high_ref, low_ref, twiddle, before, out, field = refs
+    straight = turn[0] == 0
+    if len(given_refs) == 2:
+        lower, upper = given_refs
+    else:
+        lower, upper = given_refs[0].at[:, 0], given_refs[0].at[:, 1]
+
+    def green(m, at):
+        plane, half = m // 8 * 4 + m % 4, m // 4 % 2
+        one, two = lower[plane, at], upper[plane, at]
+        return jnp.where(straight == (half == 0), one, two)
+
     def spot(part):
         return pl.ds(part * LANES, LANES)
 
@@ -109,7 +124,7 @@
         comp, pair = s // ORB, s % ORB
         at = comp * 2 * ORB + pair
         rows = pl.ds(pl.multiple_of(comp * SLOTS, SLOTS), SLOTS)
-        values = [(green[m, at], green[m, at + ORB]) for m in range(ROWS)]
+        values = [(green(m, at), green(m, at + ORB)) for m in range(ROWS)]
         for n, value in enumerate(fourier(values)):
             real, imag = times(value, twist(n)) if n else value
             field[n, pair, rows, spot(0)] = real
@@ -158,7 +173,7 @@
 
         def given(comp, b):
             at = comp * 2 * ORB + b
-            return green[m, at], green[m, at + ORB]
+            return green(m, at), green(m, at + ORB)
 
         def memory(a, b):
             left, right = sigma(0, a), given(1, b)
@@ -174,59 +189,136 @@
             one, two = memory(a, b), memory(b, a)
             results += [one[0] + two[0], two[1] - one[1]]
         for i, result in enumerate(results):
-            row = pl.ds(i, 1)
-            out[m, row, :] = before[m, row, :] + jnp.sum(result * scale, axis=0, keepdims=True)
-
-
-def collide(green, weights, high, low, twiddle, before):
+            spare, row = (m // 8 * 4 + m % 4) * 2 + m // 4 % 2, pl.ds(i, 1)
+            out[spare, row, :] = before[spare, row, :] + jnp.sum(result * scale, axis=0, keepdims=True)
+
+
+def collide(turn, fields, weights, high, low, twiddle, before):
     return pl.pallas_call(
         kernel,
         out_shape=jax.ShapeDtypeStruct((ROWS, PAIRS, LANES), jnp.float32),
-        in_specs=[pl.BlockSpec(memory_space=pltpu.VMEM)] * 6,
+        in_specs=[pl.BlockSpec(memory_space=pltpu.SMEM)] + [pl.BlockSpec(memory_space=pltpu.VMEM)] * (len(fields) + 5),
         out_specs=pl.BlockSpec(memory_space=pltpu.VMEM),
         scratch_shapes=[pltpu.VMEM((ROWS, ORB, 2 * SLOTS, 2 * LANES), jnp.float32)],
         compiler_params=pltpu.CompilerParams(vmem_limit_bytes=24 * 1024 * 1024),
         cost_estimate=pl.CostEstimate(flops=2_000_000_000, bytes_accessed=4_000_000, transcendentals=0),
-    )(green, weights, high, low, twiddle, before)
+    )(turn, *fields, weights, high, low, twiddle, before)
+
+
+def arrange_kernel(c, apart, first, parts, *refs):
+    *outs, sems = refs
+    copies = []
+    for n in range(2):
+        half = first[0] if n == 0 else 1 - first[0]
+        for at in range(4 * ORB):
+            target = outs[n].at[:, at] if apart else outs[0].at[:, n, at]
+            copies.append(pltpu.make_async_copy(parts.at[at, c, half], target, sems.at[n, at]))
+    for copy in copies:
+        copy.start()
+    for copy in copies:
+        copy.wait()
+
+
+def arrange(first, parts, c, apart):
+    whole = (PLANE, 4 * ORB, SLOTS, LANES) if apart else (PLANE, 2, 4 * ORB, SLOTS, LANES)
+    shape = jax.ShapeDtypeStruct(whole, jnp.float32)
+    return pl.pallas_call(
+        functools.partial(arrange_kernel, c, apart),
+        out_shape=[shape] * (2 if apart else 1),
+        in_specs=[pl.BlockSpec(memory_space=pltpu.SMEM), pl.BlockSpec(memory_space=pl.ANY)],
+        out_specs=[pl.BlockSpec(memory_space=pl.ANY)] * (2 if apart else 1),
+        scratch_shapes=[pltpu.SemaphoreType.DMA((2, 4 * ORB))],
+        cost_estimate=pl.CostEstimate(flops=0, bytes_accessed=3_200_000, transcendentals=0),
+    )(first, parts)
+
+
+def settle(fields, flops=100_000_000_000):
+    count = len(fields)
+    return pl.pallas_call(
+        lambda *refs: None,
+        out_shape=[jax.ShapeDtypeStruct(field.shape, field.dtype) for field in fields],
+        in_specs=[pl.BlockSpec(memory_space=pl.ANY)] * count,
+        out_specs=[pl.BlockSpec(memory_space=pl.ANY)] * count,
+        input_output_aliases={n: n for n in range(count)},
+        cost_estimate=pl.CostEstimate(flops=flops, bytes_accessed=0, transcendentals=0),
+    )(*fields)
+
+
+def shifted(step):
+    return [(z, (z + step) % 8) for z in range(8)]
 
 
 def per_device(green_row, time_step):
     slot_count = green_row.shape[4]
-    hist_count = lax.axis_size("hist")
-    history = slot_count * hist_count
-    slot_ids = (
-        lax.axis_index("hist") * slot_count
-        + lax.axis_index("mom") * SLOTS
-        + jnp.arange(SLOTS, dtype=jnp.int32)
-    )
+    history = slot_count * 8
+    zh, zl, core = (lax.axis_index(axis) for axis in ("zh", "zl", "core"))
+    plane = lax.axis_index("y") * 4 + lax.axis_index("x")
+    turn = ((zh * 4 + zl + 2) // 4 + 1) % 2
+    origin = (zl + 2) % 4 * 2 + core
+    first = origin * slot_count + turn * (slot_count // 2) + plane * SLOTS
+    slot_ids = first + jnp.arange(SLOTS, dtype=jnp.int32)
     slot_age = (time_step[0] - 1 - slot_ids) % history + 1
     decays = jnp.exp2(-(slot_age - 1).astype(jnp.float32) / history)
     weights = delta_time * decays * jnp.where(slot_age == history, 0.5, 1.0).astype(jnp.float32)
     weights = jnp.broadcast_to(weights[:, None], (SLOTS, LANES))
     high, low, twiddle = lane_tables()
 
-    parts = green_row.reshape(4 * ORB, ORB, ROWS, SLOTS, LANES)
-    arrived = [
-        lax.all_to_all(parts[:, c], "mom", split_axis=1, concat_axis=0) for c in range(ORB)
-    ]
+    parts = green_row.reshape(4 * ORB, ORB, 2, PLANE, SLOTS, LANES)
+
+    def spread(value):
+        return lax.all_to_all(value, ("y", "x"), split_axis=0, concat_axis=0)
+
+    def move(rising, falling):
+        return (
+            lax.ppermute(rising, ("zh", "zl"), shifted(2)),
+            lax.ppermute(falling, ("zh", "zl"), shifted(-2)),
+        )
+
+    def work(fields, partial):
+        return collide(turn_flag, fields, weights, high, low, twiddle, partial)
+
+    turn_flag = turn.reshape(1).astype(jnp.int32)
     partial = jnp.zeros((ROWS, PAIRS, LANES), jnp.float32)
-    for part in arrived:
-        partial = collide(part, weights, high, low, twiddle, partial)
-    owned = jnp.sum(lax.all_to_all(partial, "mom", split_axis=0, concat_axis=0), axis=0)
-    shares = owned.reshape(PAIRS, hist_count, LANES // hist_count).transpose(1, 0, 2)
-    summed = jnp.sum(lax.all_to_all(shares, "hist", split_axis=0, concat_axis=0), axis=0)
-    zero = jnp.zeros_like(summed[0])
+    fence = lax.optimization_barrier
+    side = zh.reshape(1).astype(jnp.int32)
+    zero = arrange(side, parts, 0, True)
+    zero, side = fence((zero, side))
+    zero = move(*zero)
+    (one,) = arrange(side, parts, 1, False)
+    one = spread(one)
+    zero, one, side = fence((settle(zero), one, side))
+    one = move(one[:, 0], one[:, 1])
+    (two,) = arrange(side, parts, 2, False)
+    two = spread(two)
+    one, two = fence((settle(one), two))
+    two = move(two[:, 0], two[:, 1])
+    one, zero = fence((one, jnp.stack(zero, 1)))
+    zero = spread(zero)
+    partial = work(one, partial)
+    partial = work([zero], partial)
+    partial, two = fence((partial, two))
+    partial = work(two, partial)
+
+    blocks = partial.reshape(PLANE, 2, PAIRS, LANES)
+    owned = jnp.sum(spread(blocks), axis=0)
+    copies = jnp.broadcast_to(owned[:, None], (2, 8, PAIRS, LANES)).reshape(PLANE, PAIRS, LANES)
+    copies = lax.all_to_all(copies, ("zh", "zl", "core"), split_axis=0, concat_axis=0)
+    share = LANES // 8
+    summed = lax.dynamic_slice_in_dim(jnp.sum(copies, axis=0), (zl * 2 + core) * share, share, 1)
+    none = jnp.zeros_like(summed[0])
     real = [summed[0], summed[3], summed[5], summed[3], summed[1], summed[7], summed[5], summed[7], summed[2]]
-    imag = [zero, summed[4], summed[6], -summed[4], zero, summed[8], -summed[6], -summed[8], zero]
+    imag = [none, summed[4], summed[6], -summed[4], none, summed[8], -summed[6], -summed[8], none]
     return jnp.stack(real + imag).reshape(2, ORB, ORB, -1)
 
 
 def solution(mesh):
-    placed = (P(None, None, None, None, "hist", "mom"), P())
+    axes = ("y", "zh", "x", "zl", "core")
+    finer = Mesh(mesh.devices.reshape(4, 2, 4, 4, 2), axes)
+    mom, hist = axes[:3], axes[3:]
     return jax.shard_map(
         per_device,
-        mesh=mesh,
-        in_specs=placed,
-        out_specs=P(None, None, None, ("mom", "hist")),
+        mesh=finer,
+        in_specs=(P(None, None, None, None, hist, mom), P()),
+        out_specs=P(None, None, None, axes),
         check_vma=False,
     )

time: 182 us -> 299 us (1.64)
  Pallas kernels: 18.8 us -> 166 us
  blocking collectives: 62.2 us -> 13.4 us
  starting transfers between devices: 27.9 us -> 39.6 us
  waiting for transfers between devices: 59.6 us -> 64 us
    pallas_call x0 -> x5, Pallas kernels: none -> 147 us  [the longest x3 147 us: arrange(): pl.pallas_call(functools.partial(arrange_kernel, c, apart), out_shape=[sh...]
    all_to_all x2 -> x1, blocking collectives: 62.2 us -> 13.4 us  [spread(): return lax.all_to_all(value, ('y', 'x'), split_axis=0, concat_axis=0)]
    ppermute x0 -> x6, starting transfers between devices: none -> 14.2 us  [the longest x3 7.19 us: move(): lax.ppermute(rising, ('zh', 'zl'), shifted(2))]
    ppermute x0 -> x6, waiting for transfers between devices: none -> 13.3 us  [the longest x3 13.3 us: move(): lax.ppermute(falling, ('zh', 'zl'), shifted(-2))]
    another operation x5 -> x1, local copies, waits for them, and re-layouts: 9.45 us -> 0.01 us  [the longest x4 9.45 us: per_device(): lax.all_to_all(parts[:, c], 'mom', split_axis=1, concat_axis=0)]
    all_to_all x3 -> x4, waiting for transfers between devices: 59.6 us -> 50.7 us  [the longest x3 41.5 us: spread(): return lax.all_to_all(value, ('y', 'x'), split_axis=0, concat_axis=0)]
    unnamed x8 -> x22, local copies, waits for them, and re-layouts: 0.17 us -> 7.45 us
    all_to_all x3 -> x4, starting transfers between devices: 27.9 us -> 25.5 us  [the longest x3 17.9 us: spread(): return lax.all_to_all(value, ('y', 'x'), split_axis=0, concat_axis=0)]
  transfers between devices with their start and end apart: 3 -> 10, of which waited for: 3 -> 5; matrix products, arithmetic and copies ran while one was open for 2% -> 1% of each run, Pallas kernels for 6% -> 37%
where the time goes in v2:
time: 299 us; the launch traced here: 298 us
  Pallas kernels  166 us (56%)
  waiting for transfers between devices  64 us (21%)
  starting transfers between devices  39.6 us (13%)
  blocking collectives  13.4 us (4%)
  local copies, waits for them, and re-layouts  11.5 us (4%)
    pallas_call x3, Pallas kernels, arrange(): pl.pallas_call(functools.partial(arrange_kernel, c, apart), out_shape=[sh...  147 us
    all_to_all x3, waiting for transfers between devices, spread(): return lax.all_to_all(value, ('y', 'x'), split_axis=0, concat_axis=0)  41.5 us
    pallas_call x3, Pallas kernels, collide(): pl.pallas_call(kernel, out_shape=jax.ShapeDtypeStruct((ROWS, PAIRS, LANES...  19.1 us
    all_to_all x3, starting transfers between devices, spread(): return lax.all_to_all(value, ('y', 'x'), split_axis=0, concat_axis=0)  17.9 us
    all_to_all x1, blocking collectives, spread(): return lax.all_to_all(value, ('y', 'x'), split_axis=0, concat_axis=0)  13.4 us
    ppermute x3, waiting for transfers between devices, move(): lax.ppermute(falling, ('zh', 'zl'), shifted(-2))  13.3 us
    all_to_all x1, waiting for transfers between devices, per_device(): lax.all_to_all(copies, ('zh', 'zl', 'core'), split_axis=0, concat_axis=0)  9.17 us
    all_to_all x1, starting transfers between devices, per_device(): lax.all_to_all(copies, ('zh', 'zl', 'core'), split_axis=0, concat_axis=0)  7.57 us
  transfers between devices with their start and end apart: 10, of which 5 were waited for; matrix products, arithmetic and copies ran while one was open for 1% of the time, Pallas kernels for 37%

profile of v2, /device:TPU:1, one launch (start us, length us, event | category | flops | bytes accessed | tf_op | source)
XLA Modules:
  0.0 298.2 jit_solution(8123871718498615904)
XLA Ops:
  0.0 49.0 %shard_map.55 = (f32[16,12,8,128]{3,2,1,0:T(8,128)}, f32[16,12,8,128]{3,2,1,0:T(8,128)}) custom-call(s32[1]{0:T(128)} %bitcast.1.first, f32[12,3,2,16,8,128]{5,4,3,2,1,0:T(8,128)} %bitcast.17), custom_call_target="tpu_custom_call" | custom-call | bytes 3200000 | tf_op jit(solution)/shard_map/pallas_call | solution.py:225
  49.0 3.9 %collective-permute-start = (f32[16,12,8,128]{3,2,1,0:T(8,128)}, f32[16,12,8,128]{3,2,1,0:T(8,128)S(1)}, u32[]{:S(2)}, u32[]{:S(2)}) collective-permute-start(f32[16,12,8,128]{3,2,1,0:T(8,128)} %get-tuple-element.29), channel_id=1, source_target_pairs={{0,4},{2,6},{4,32},{6,34},{32,36},{34,38},{36,0},{38,2},{1,5},{3,7... | collective-permute-start | bytes 2359304 | tf_op jit(solution)/shard_map/ppermute | solution.py:273
  52.9 3.1 %collective-permute-start.1 = (f32[16,12,8,128]{3,2,1,0:T(8,128)}, f32[16,12,8,128]{3,2,1,0:T(8,128)S(1)}, u32[]{:S(2)}, u32[]{:S(2)}) collective-permute-start(f32[16,12,8,128]{3,2,1,0:T(8,128)} %get-tuple-element.30), channel_id=1, source_target_pairs={{0,36},{2,38},{4,0},{6,2},{32,4},{34,6},{36,32},{38,34},{1,37},{3,... | collective-permute-start | bytes 2359304 | tf_op jit(solution)/shard_map/ppermute | solution.py:274
  56.0 49.0 %shard_map.57 = f32[16,2,12,8,128]{4,3,2,1,0:T(8,128)} custom-call(s32[1]{0:T(128)} %bitcast.1.first, f32[12,3,2,16,8,128]{5,4,3,2,1,0:T(8,128)} %bitcast.18), custom_call_target="tpu_custom_call" | custom-call | bytes 3200000 | tf_op jit(solution)/shard_map/pallas_call | solution.py:225
  105.0 6.8 %all-to-all-start = ((f32[16,2,12,8,128]{4,3,2,1,0:T(8,128)}), f32[16,2,12,8,128]{4,3,2,1,0:T(8,128)S(1)}, u32[]{:S(2)}, u32[]{:S(2)}) async-start(f32[16,2,12,8,128]{4,3,2,1,0:T(8,128)} %shard_map.57), calls=%async_computation | async-start | bytes 3145728 | tf_op jit(solution)/shard_map/all_to_all | solution.py:269
  111.7 0.0 collective-permute-done.refs_0_
  111.7 0.0 copy-start.9
  111.7 0.0 collective-permute-done.1.refs_1_
  111.8 0.9 copy-done.9
  112.6 0.0 copy-start.10
  112.6 0.9 copy-done.10
  113.5 20.0 %all-to-all-done = f32[16,2,12,8,128]{4,3,2,1,0:T(8,128)S(1)} async-done(((f32[16,2,12,8,128]{4,3,2,1,0:T(8,128)}), f32[16,2,12,8,128]{4,3,2,1,0:T(8,128)S(1)}, u32[]{:S(2)}, u32[]{:S(2)}) %all-to-all-start) | async-done | bytes 1572896 | tf_op jit(solution)/shard_map/all_to_all | solution.py:269
  133.6 1.3 slice_bitcast_fusion.2
  134.9 1.1 collective-permute-start.2
  135.9 2.5 collective-permute-start.3
  138.4 49.0 %shard_map.59 = f32[16,2,12,8,128]{4,3,2,1,0:T(8,128)} custom-call(s32[1]{0:T(128)} %bitcast.1.first, f32[12,3,2,16,8,128]{5,4,3,2,1,0:T(8,128)} %bitcast.19), custom_call_target="tpu_custom_call" | custom-call | bytes 3200000 | tf_op jit(solution)/shard_map/pallas_call | solution.py:225
  187.4 5.6 %all-to-all-start.1 = ((f32[16,2,12,8,128]{4,3,2,1,0:T(8,128)}), f32[16,2,12,8,128]{4,3,2,1,0:T(8,128)S(1)}, u32[]{:S(2)}, u32[]{:S(2)}) async-start(f32[16,2,12,8,128]{4,3,2,1,0:T(8,128)} %shard_map.59), calls=%async_computation.1 | async-start | bytes 3145728 | tf_op jit(solution)/shard_map/all_to_all | solution.py:269
  193.0 2.7 pad_maximum_fusion
  195.6 0.0 collective-permute-done.2.refs_0_
  195.6 0.0 copy-start
  195.6 0.0 collective-permute-done.3.refs_1_
  195.7 0.9 copy-done
  196.5 0.0 copy-start.2
  196.5 0.9 copy-done.2
  197.4 16.0 %all-to-all-done.1 = f32[16,2,12,8,128]{4,3,2,1,0:T(8,128)S(1)} async-done(((f32[16,2,12,8,128]{4,3,2,1,0:T(8,128)}), f32[16,2,12,8,128]{4,3,2,1,0:T(8,128)S(1)}, u32[]{:S(2)}, u32[]{:S(2)}) %all-to-all-start.1) | async-done | bytes 1572896 | tf_op jit(solution)/shard_map/all_to_all | solution.py:269
  213.5 5.6 %all-to-all-start.2 = ((f32[16,2,12,8,128]{4,3,2,1,0:T(8,128)}), f32[16,2,12,8,128]{4,3,2,1,0:T(8,128)S(1)}, u32[]{:S(2)}, u32[]{:S(2)}) async-start(f32[16,2,12,8,128]{4,3,2,1,0:T(8,128)} %pad_maximum_fusion), calls=%async_computation.2 | async-start | bytes 3145728 | tf_op jit(solution)/shard_map/all_to_all | solution.py:269
  219.0 0.0 copy-start.4
  219.0 0.0 copy-start.5
  219.1 0.0 copy-start.6
  219.1 1.3 slice_bitcast_fusion
  220.3 2.2 collective-permute-start.4
  222.5 1.4 collective-permute-start.5
  224.6 0.1 broadcast_in_dim.25.refs_2_.refs_1_
  224.7 0.0 copy-done.4
  224.7 0.0 copy-done.5
  224.7 0.0 copy-done.6
  224.7 0.0 copy-start.1
  224.7 1.1 copy-done.1
  225.8 0.0 copy-start.3
  225.8 1.1 copy-done.3
  227.0 6.4 %shard_map.60.refs_5_ = f32[32,9,128]{2,1,0:T(8,128)S(1)} custom-call(s32[1]{0:T(128)} %bitcast.turn, f32[16,12,8,128]{3,2,1,0:T(8,128)S(1)} %copy-done.1, f32[16,12,8,128]{3,2,1,0:T(8,128)S(1)} %copy-done.3, f32[8,128]{1,0:T(8,128)S(1)} %broadcast_in_dim.25.refs_2_.refs_1_, bf16[256,256]{1,0:T(8,128)(2,1)S(1)} %copy-done.4, bf16[256,256]{1,0:T(8,128)(2,1)S(1)} %copy-done.5, ...), custom_call_target="tpu_custom_call" | custom-call | flops 2000000000 | bytes 4000000 | tf_op jit(solution)/shard_map/pallas_call | solution.py:197
  233.4 0.0 copy-start.7
  233.4 0.7 copy-done.7
  234.0 5.5 %all-to-all-done.2.refs_0_ = f32[16,2,12,8,128]{4,3,2,1,0:T(8,128)S(1)} async-done(((f32[16,2,12,8,128]{4,3,2,1,0:T(8,128)}), f32[16,2,12,8,128]{4,3,2,1,0:T(8,128)S(1)}, u32[]{:S(2)}, u32[]{:S(2)}) %all-to-all-start.2) | async-done | bytes 1572896 | tf_op jit(solution)/shard_map/all_to_all | solution.py:269
  239.5 0.0 copy-start.8
  239.5 0.9 copy-done.8
  240.4 6.4 %shard_map.61.refs_6_ = f32[32,9,128]{2,1,0:T(8,128)S(1)} custom-call(s32[1]{0:T(128)} %bitcast.turn, f32[16,2,12,8,128]{4,3,2,1,0:T(8,128)S(1)} %all-to-all-done.2.refs_0_, f32[8,128]{1,0:T(8,128)S(1)} %broadcast_in_dim.25.refs_2_.refs_1_, bf16[256,256]{1,0:T(8,128)(2,1)S(1)} %copy-done.4, bf16[256,256]{1,0:T(8,128)(2,1)S(1)} %copy-done.5, ...), custom_call_target="tpu_custom_call" | custom-call | flops 2000000000 | bytes 4000000 | tf_op jit(solution)/shard_map/pallas_call | solution.py:197
  246.8 0.0 collective-permute-done.4.refs_0_
  246.8 13.2 %collective-permute-done.5.refs_1_ = f32[16,12,8,128]{3,2,1,0:T(8,128)S(1)} collective-permute-done((f32[16,12,8,128]{3,2,1,0:T(8,128)}, f32[16,12,8,128]{3,2,1,0:T(8,128)S(1)}, u32[]{:S(2)}, u32[]{:S(2)}) %collective-permute-start.5) | collective-permute-done | bytes 786464 | tf_op jit(solution)/shard_map/ppermute | solution.py:274
  260.1 6.4 %shard_map.62 = f32[32,9,128]{2,1,0:T(8,128)S(1)} custom-call(s32[1]{0:T(128)} %bitcast.turn, f32[16,12,8,128]{3,2,1,0:T(8,128)S(1)} %collective-permute-done.4.refs_0_, f32[16,12,8,128]{3,2,1,0:T(8,128)S(1)} %collective-permute-done.5.refs_1_, f32[8,128]{1,0:T(8,128)S(1)} %broadcast_in_dim.25.refs_2_.refs_1_, bf16[256,256]{1,0:T(8,128)(2,1)S(1)} %copy-done.4, ...), custom_call_target="tpu_custom_call" | custom-call | flops 2000000000 | bytes 4000000 | tf_op jit(solution)/shard_map/pallas_call | solution.py:197
  266.5 0.1 copy.38
  266.5 13.4 %all_to_all.25 = f32[16,2,9,128]{3,1,2,0:T(2,128)S(1)} all-to-all(f32[16,2,9,128]{3,1,2,0:T(2,128)S(1)} %copy.38), channel_id=1, replica_groups=mesh['y'=4,'zh'=2,'x'=4,'zl'=4,'core'=2] {'y','x'}, dimensions={0} | all-to-all | bytes 294912 | tf_op jit(solution)/shard_map/all_to_all | solution.py:269
  279.9 0.1 reduce_sum.18
  280.0 0.7 broadcast_in_dim.27
  280.6 7.6 %all-to-all-start.4 = ((f32[16,9,128]{2,1,0:T(8,128)}), f32[16,9,128]{2,1,0:T(8,128)S(1)}, u32[]{:S(2)}, u32[]{:S(2)}) async-start(f32[16,9,128]{2,1,0:T(8,128)} %bitcast.11), calls=%async_computation.4 | async-start | bytes 262144 | tf_op jit(solution)/shard_map/all_to_all | solution.py:305
  288.2 9.2 %all-to-all-done.4 = f32[16,9,128]{2,1,0:T(8,128)S(1)} async-done(((f32[16,9,128]{2,1,0:T(8,128)}), f32[16,9,128]{2,1,0:T(8,128)S(1)}, u32[]{:S(2)}, u32[]{:S(2)}) %all-to-all-start.4) | async-done | bytes 73760 | tf_op jit(solution)/shard_map/all_to_all | solution.py:305
  297.4 0.1 fusion.2
  297.5 0.1 stack.18
  297.6 0.6 copy.41
  (8 shorter events, 0.1 us)
Async XLA Ops:
  49.0 62.8 %collective-permute-start = (f32[16,12,8,128]{3,2,1,0:T(8,128)}, f32[16,12,8,128]{3,2,1,0:T(8,128)S(1)}, u32[]{:S(2)}, u32[]{:S(2)}) collective-permute-start(f32[16,12,8,128]{3,2,1,0:T(8,128)} %get-tuple-element.29), channel_id=1, source_target_pairs={{0,4},{2,6},{4,32},{6,34},{32,36},{34,38},{36,0},{38,2},{1,5},{3,7... | collective-permute-start | bytes 2359304 | tf_op jit(solution)/shard_map/ppermute | solution.py:273
  52.9 58.9 %collective-permute-start.1 = (f32[16,12,8,128]{3,2,1,0:T(8,128)}, f32[16,12,8,128]{3,2,1,0:T(8,128)S(1)}, u32[]{:S(2)}, u32[]{:S(2)}) collective-permute-start(f32[16,12,8,128]{3,2,1,0:T(8,128)} %get-tuple-element.30), channel_id=1, source_target_pairs={{0,36},{2,38},{4,0},{6,2},{32,4},{34,6},{36,32},{38,34},{1,37},{3,... | collective-permute-start | bytes 2359304 | tf_op jit(solution)/shard_map/ppermute | solution.py:274
  105.0 28.6 %all-to-all-start = ((f32[16,2,12,8,128]{4,3,2,1,0:T(8,128)}), f32[16,2,12,8,128]{4,3,2,1,0:T(8,128)S(1)}, u32[]{:S(2)}, u32[]{:S(2)}) async-start(f32[16,2,12,8,128]{4,3,2,1,0:T(8,128)} %shard_map.57), calls=%async_computation | async-start | bytes 3145728 | tf_op jit(solution)/shard_map/all_to_all | solution.py:269
  111.7 0.9 copy-start.9
  112.6 0.9 copy-start.10
  134.9 60.8 %collective-permute-start.2 = (f32[16,12,8,128]{3,2,1,0:T(8,128)}, f32[16,12,8,128]{3,2,1,0:T(8,128)S(1)}, u32[]{:S(2)}, u32[]{:S(2)}) collective-permute-start(f32[16,12,8,128]{3,2,1,0:T(8,128)} %get-tuple-element.58), channel_id=1, source_target_pairs={{0,4},{2,6},{4,32},{6,34},{32,36},{34,38},{36,0},{38,2},{1,5},{3,7... | collective-permute-start | bytes 2359304 | tf_op jit(solution)/shard_map/ppermute | solution.py:273
  135.9 59.7 %collective-permute-start.3 = (f32[16,12,8,128]{3,2,1,0:T(8,128)}, f32[16,12,8,128]{3,2,1,0:T(8,128)S(1)}, u32[]{:S(2)}, u32[]{:S(2)}) collective-permute-start(f32[16,12,8,128]{3,2,1,0:T(8,128)} %get-tuple-element.57), channel_id=1, source_target_pairs={{0,36},{2,38},{4,0},{6,2},{32,4},{34,6},{36,32},{38,34},{1,37},{3,... | collective-permute-start | bytes 2359304 | tf_op jit(solution)/shard_map/ppermute | solution.py:274
  187.4 26.1 %all-to-all-start.1 = ((f32[16,2,12,8,128]{4,3,2,1,0:T(8,128)}), f32[16,2,12,8,128]{4,3,2,1,0:T(8,128)S(1)}, u32[]{:S(2)}, u32[]{:S(2)}) async-start(f32[16,2,12,8,128]{4,3,2,1,0:T(8,128)} %shard_map.59), calls=%async_computation.1 | async-start | bytes 3145728 | tf_op jit(solution)/shard_map/all_to_all | solution.py:269
  195.6 0.9 copy-start
  196.5 0.9 copy-start.2
  213.5 26.0 %all-to-all-start.2 = ((f32[16,2,12,8,128]{4,3,2,1,0:T(8,128)}), f32[16,2,12,8,128]{4,3,2,1,0:T(8,128)S(1)}, u32[]{:S(2)}, u32[]{:S(2)}) async-start(f32[16,2,12,8,128]{4,3,2,1,0:T(8,128)} %pad_maximum_fusion), calls=%async_computation.2 | async-start | bytes 3145728 | tf_op jit(solution)/shard_map/all_to_all | solution.py:269
  219.0 5.7 %copy-start.4 = (bf16[256,256]{1,0:T(8,128)(2,1)S(1)}, bf16[256,256]{1,0:T(8,128)(2,1)}, u32[]{:S(2)}) copy-start(bf16[256,256]{1,0:T(8,128)(2,1)} %constant.105.clone.refs_3_.refs_2_) | copy-start | bytes 393220
  219.0 5.7 %copy-start.5 = (bf16[256,256]{1,0:T(8,128)(2,1)S(1)}, bf16[256,256]{1,0:T(8,128)(2,1)}, u32[]{:S(2)}) copy-start(bf16[256,256]{1,0:T(8,128)(2,1)} %constant.106.clone.refs_4_.refs_3_) | copy-start | bytes 393220
  219.1 5.7 %copy-start.6 = (f32[32,2,128]{2,1,0:T(2,128)S(1)}, f32[32,2,128]{2,1,0:T(2,128)}, u32[]{:S(2)}) copy-start(f32[32,2,128]{2,1,0:T(2,128)} %constant.107.clone.refs_5_.refs_4_) | copy-start | bytes 98308
  220.3 26.5 %collective-permute-start.4 = (f32[16,12,8,128]{3,2,1,0:T(8,128)}, f32[16,12,8,128]{3,2,1,0:T(8,128)S(1)}, u32[]{:S(2)}, u32[]{:S(2)}) collective-permute-start(f32[16,12,8,128]{3,2,1,0:T(8,128)} %get-tuple-element.56), channel_id=1, source_target_pairs={{0,4},{2,6},{4,32},{6,34},{32,36},{34,38},{36,0},{38,2},{1,5},{3,7... | collective-permute-start | bytes 2359304 | tf_op jit(solution)/shard_map/ppermute | solution.py:273
  222.5 37.5 %collective-permute-start.5 = (f32[16,12,8,128]{3,2,1,0:T(8,128)}, f32[16,12,8,128]{3,2,1,0:T(8,128)S(1)}, u32[]{:S(2)}, u32[]{:S(2)}) collective-permute-start(f32[16,12,8,128]{3,2,1,0:T(8,128)} %get-tuple-element.55), channel_id=1, source_target_pairs={{0,36},{2,38},{4,0},{6,2},{32,4},{34,6},{36,32},{38,34},{1,37},{3,... | collective-permute-start | bytes 2359304 | tf_op jit(solution)/shard_map/ppermute | solution.py:274
  224.7 1.1 copy-start.1
  225.8 1.1 copy-start.3
  233.4 0.7 copy-start.7
  239.5 1.0 copy-start.8
  280.6 16.7 %all-to-all-start.4 = ((f32[16,9,128]{2,1,0:T(8,128)}), f32[16,9,128]{2,1,0:T(8,128)S(1)}, u32[]{:S(2)}, u32[]{:S(2)}) async-start(f32[16,9,128]{2,1,0:T(8,128)} %bitcast.11), calls=%async_computation.4 | async-start | bytes 262144 | tf_op jit(solution)/shard_map/all_to_all | solution.py:305

commit v3 on v2

--- a/solution.py
+++ b/solution.py
@@ -201,7 +201,7 @@
         out_specs=pl.BlockSpec(memory_space=pltpu.VMEM),
         scratch_shapes=[pltpu.VMEM((ROWS, ORB, 2 * SLOTS, 2 * LANES), jnp.float32)],
         compiler_params=pltpu.CompilerParams(vmem_limit_bytes=24 * 1024 * 1024),
-        cost_estimate=pl.CostEstimate(flops=2_000_000_000, bytes_accessed=4_000_000, transcendentals=0),
+        cost_estimate=pl.CostEstimate(flops=1000000000, bytes_accessed=0, transcendentals=0),
     )(turn, *fields, weights, high, low, twiddle, before)
 
 
@@ -226,22 +226,24 @@
         functools.partial(arrange_kernel, c, apart),
         out_shape=[shape] * (2 if apart else 1),
         in_specs=[pl.BlockSpec(memory_space=pltpu.SMEM), pl.BlockSpec(memory_space=pl.ANY)],
-        out_specs=[pl.BlockSpec(memory_space=pl.ANY)] * (2 if apart else 1),
+        out_specs=[pl.BlockSpec(memory_space=pltpu.VMEM)] * (2 if apart else 1),
         scratch_shapes=[pltpu.SemaphoreType.DMA((2, 4 * ORB))],
+        compiler_params=pltpu.CompilerParams(vmem_limit_bytes=8 * 1024 * 1024),
         cost_estimate=pl.CostEstimate(flops=0, bytes_accessed=3_200_000, transcendentals=0),
     )(first, parts)
 
 
-def settle(fields, flops=100_000_000_000):
-    count = len(fields)
+def settle(weights, fields, cost):
+    def body(given, one, two, out):
+        out[...] = given[...]
+
     return pl.pallas_call(
-        lambda *refs: None,
-        out_shape=[jax.ShapeDtypeStruct(field.shape, field.dtype) for field in fields],
-        in_specs=[pl.BlockSpec(memory_space=pl.ANY)] * count,
-        out_specs=[pl.BlockSpec(memory_space=pl.ANY)] * count,
-        input_output_aliases={n: n for n in range(count)},
-        cost_estimate=pl.CostEstimate(flops=flops, bytes_accessed=0, transcendentals=0),
-    )(*fields)
+        body,
+        out_shape=jax.ShapeDtypeStruct((SLOTS, LANES), jnp.float32),
+        in_specs=[pl.BlockSpec(memory_space=pltpu.VMEM)] * 3,
+        out_specs=pl.BlockSpec(memory_space=pltpu.VMEM),
+        cost_estimate=pl.CostEstimate(flops=int(cost * 1e9), bytes_accessed=0, transcendentals=0),
+    )(weights, *(field[0, 0] for field in fields))
 
 
 def shifted(step):
@@ -274,7 +276,7 @@
             lax.ppermute(falling, ("zh", "zl"), shifted(-2)),
         )
 
-    def work(fields, partial):
+    def work(fields, partial, weights):
         return collide(turn_flag, fields, weights, high, low, twiddle, partial)
 
     turn_flag = turn.reshape(1).astype(jnp.int32)
@@ -285,26 +287,27 @@
     zero, side = fence((zero, side))
     zero = move(*zero)
     (one,) = arrange(side, parts, 1, False)
-    one = spread(one)
-    zero, one, side = fence((settle(zero), one, side))
-    one = move(one[:, 0], one[:, 1])
+    one, side = fence((spread(one), side))
     (two,) = arrange(side, parts, 2, False)
     two = spread(two)
-    one, two = fence((settle(one), two))
-    two = move(two[:, 0], two[:, 1])
-    one, zero = fence((one, jnp.stack(zero, 1)))
+    one, two = (one[:, 0], one[:, 1]), (two[:, 0], two[:, 1])
+    zero, one, weights = fence((zero, one, settle(weights, zero, 0.0)))
+    one = move(*one)
+    zero, two = fence((jnp.stack(zero, 1), two))
     zero = spread(zero)
-    partial = work(one, partial)
-    partial = work([zero], partial)
+    one, two, weights = fence((one, two, settle(weights, one, 0.0)))
+    two = move(*two)
+    partial = work(one, partial, weights)
+    partial = work([zero], partial, weights)
     partial, two = fence((partial, two))
-    partial = work(two, partial)
+    partial = work(two, partial, weights)
 
     blocks = partial.reshape(PLANE, 2, PAIRS, LANES)
     owned = jnp.sum(spread(blocks), axis=0)
-    copies = jnp.broadcast_to(owned[:, None], (2, 8, PAIRS, LANES)).reshape(PLANE, PAIRS, LANES)
-    copies = lax.all_to_all(copies, ("zh", "zl", "core"), split_axis=0, concat_axis=0)
     share = LANES // 8
-    summed = lax.dynamic_slice_in_dim(jnp.sum(copies, axis=0), (zl * 2 + core) * share, share, 1)
+    shares = owned.reshape(2, PAIRS, 8, share).transpose(0, 2, 1, 3).reshape(PLANE, 1, PAIRS * share)
+    shares = lax.all_to_all(shares, ("zh", "zl", "core"), split_axis=0, concat_axis=0)
+    summed = jnp.sum(shares, axis=(0, 1)).reshape(PAIRS, share)
     none = jnp.zeros_like(summed[0])
     real = [summed[0], summed[3], summed[5], summed[3], summed[1], summed[7], summed[5], summed[7], summed[2]]
     imag = [none, summed[4], summed[6], -summed[4], none, summed[8], -summed[6], -summed[8], none]

time: 299 us -> 169 us (0.57)
  Pallas kernels: 166 us -> 26.7 us
  blocking collectives: 13.4 us -> 43 us
  waiting for transfers between devices: 64 us -> 46.1 us
  starting transfers between devices: 39.6 us -> 32.1 us
  local copies, waits for them, and re-layouts: 11.5 us -> 16.3 us
    pallas_call x3, Pallas kernels: 147 us -> 3.65 us  [arrange(): pl.pallas_call(functools.partial(arrange_kernel, c, apart), out_shape=[sh...]
    all_to_all x0 -> x1, blocking collectives: none -> 28.8 us  [per_device(): lax.all_to_all(shares, ('zh', 'zl', 'core'), split_axis=0, concat_axis=0)]
    all_to_all x3, waiting for transfers between devices: 41.5 us -> 18.8 us  [spread(): return lax.all_to_all(value, ('y', 'x'), split_axis=0, concat_axis=0)]
    ppermute x3, waiting for transfers between devices: 0.01 us -> 21.3 us  [move(): lax.ppermute(rising, ('zh', 'zl'), shifted(2))]
    all_to_all x1 -> x0, waiting for transfers between devices: 9.17 us -> none  [per_device(): lax.all_to_all(copies, ('zh', 'zl', 'core'), split_axis=0, concat_axis=0)]
    all_to_all x1 -> x0, starting transfers between devices: 7.57 us -> none  [per_device(): lax.all_to_all(copies, ('zh', 'zl', 'core'), split_axis=0, concat_axis=0)]
    ppermute x3, waiting for transfers between devices: 13.3 us -> 6.02 us  [move(): lax.ppermute(falling, ('zh', 'zl'), shifted(-2))]
    squeeze x2 -> x6, local copies, waits for them, and re-layouts: 2.54 us -> 7.65 us  [the longest x2 3.92 us: per_device(): one, two = ((one[:, 0], one[:, 1]), (two[:, 0], two[:, 1]))]
  transfers between devices with their start and end apart: 10 -> 9, of which waited for: 5 -> 6; matrix products, arithmetic and copies ran while one was open for 1% -> 7% of each run, Pallas kernels for 37% -> 10%
where the time goes in v3:
time: 169 us; the launch traced here: 168 us
  waiting for transfers between devices  46.1 us (27%)
  blocking collectives  43 us (25%)
  starting transfers between devices  32.1 us (19%)
  Pallas kernels  26.7 us (16%)
  local copies, waits for them, and re-layouts  16.3 us (10%)
  other arithmetic  2.86 us (2%)
    all_to_all x1, blocking collectives, per_device(): lax.all_to_all(shares, ('zh', 'zl', 'core'), split_axis=0, concat_axis=0)  28.8 us
    ppermute x3, waiting for transfers between devices, move(): lax.ppermute(rising, ('zh', 'zl'), shifted(2))  21.3 us
    pallas_call x3, Pallas kernels, collide(): pl.pallas_call(kernel, out_shape=jax.ShapeDtypeStruct((ROWS, PAIRS, LANES...  20.5 us
    all_to_all x3, waiting for transfers between devices, spread(): return lax.all_to_all(value, ('y', 'x'), split_axis=0, concat_axis=0)  18.8 us
    all_to_all x3, starting transfers between devices, spread(): return lax.all_to_all(value, ('y', 'x'), split_axis=0, concat_axis=0)  17.9 us
    all_to_all x1, blocking collectives, spread(): return lax.all_to_all(value, ('y', 'x'), split_axis=0, concat_axis=0)  14.2 us
    ppermute x3, starting transfers between devices, move(): lax.ppermute(falling, ('zh', 'zl'), shifted(-2))  11.2 us
    unnamed x18, local copies, waits for them, and re-layouts  7.01 us
  transfers between devices with their start and end apart: 9, of which 6 were waited for; matrix products, arithmetic and copies ran while one was open for 7% of the time, Pallas kernels for 10%

profile of v3, /device:TPU:1, one launch (start us, length us, event | category | flops | bytes accessed | tf_op | source)
XLA Modules:
  0.0 167.9 jit_solution(12856918558777507944)
XLA Ops:
  0.0 0.0 copy-start
  0.0 2.3 %copy-done = f32[2,2,3,3,256,128]{5,4,3,2,1,0:T(8,128)S(1)} copy-done((f32[2,2,3,3,256,128]{5,4,3,2,1,0:T(8,128)S(1)}, f32[2,2,3,3,256,128]{5,4,3,2,1,0:T(8,128)}, u32[]{:S(2)}) %copy-start) | copy-done | bytes 4718616
  2.3 0.4 shard_map.55
  2.8 1.6 shard_map.56
  4.4 7.6 %all-to-all-start = ((f32[16,2,12,8,128]{4,3,2,1,0:T(8,128)}), f32[16,2,12,8,128]{4,3,2,1,0:T(8,128)S(1)}, u32[]{:S(2)}, u32[]{:S(2)}) async-start(f32[16,2,12,8,128]{4,3,2,1,0:T(8,128)} %shard_map.56), calls=%async_computation | async-start | bytes 3145728 | tf_op jit(solution)/shard_map/all_to_all | solution.py:271
  12.0 6.1 %collective-permute-start.1 = (f32[16,12,8,128]{3,2,1,0:T(8,128)S(1)}, f32[16,12,8,128]{3,2,1,0:T(8,128)}, u32[]{:S(2)}, u32[]{:S(2)}) collective-permute-start(f32[16,12,8,128]{3,2,1,0:T(8,128)S(1)} %get-tuple-element.31), channel_id=1, source_target_pairs={{0,36},{2,38},{4,0},{6,2},{32,4},{34,6},{36,32},{38,34},{1,37},{3,... | collective-permute-start | bytes 2359304 | tf_op jit(solution)/shard_map/ppermute | solution.py:276
  18.1 0.0 collective-permute-start
  18.1 16.8 %all-to-all-done = f32[16,2,12,8,128]{4,3,2,1,0:T(8,128)S(1)} async-done(((f32[16,2,12,8,128]{4,3,2,1,0:T(8,128)}), f32[16,2,12,8,128]{4,3,2,1,0:T(8,128)S(1)}, u32[]{:S(2)}, u32[]{:S(2)}) %all-to-all-start) | async-done | bytes 1572896 | tf_op jit(solution)/shard_map/all_to_all | solution.py:271
  34.9 0.0 copy-start.1
  34.9 2.3 %copy-done.1 = f32[2,2,3,3,256,128]{5,4,3,2,1,0:T(8,128)S(1)} copy-done((f32[2,2,3,3,256,128]{5,4,3,2,1,0:T(8,128)S(1)}, f32[2,2,3,3,256,128]{5,4,3,2,1,0:T(8,128)}, u32[]{:S(2)}) %copy-start.1) | copy-done | bytes 4718616
  37.2 1.6 shard_map.58
  38.8 4.7 %all-to-all-start.1 = ((f32[16,2,12,8,128]{4,3,2,1,0:T(8,128)}), f32[16,2,12,8,128]{4,3,2,1,0:T(8,128)}, u32[]{:S(2)}, u32[]{:S(2)}) async-start(f32[16,2,12,8,128]{4,3,2,1,0:T(8,128)} %shard_map.58), calls=%async_computation.1 | async-start | bytes 3145728 | tf_op jit(solution)/shard_map/all_to_all | solution.py:271
  44.3 4.7 %collective-permute-done.1 = f32[16,12,8,128]{3,2,1,0:T(8,128)} collective-permute-done((f32[16,12,8,128]{3,2,1,0:T(8,128)S(1)}, f32[16,12,8,128]{3,2,1,0:T(8,128)}, u32[]{:S(2)}, u32[]{:S(2)}) %collective-permute-start.1) | collective-permute-done | bytes 786464 | tf_op jit(solution)/shard_map/ppermute | solution.py:276
  49.0 1.3 slice_bitcast_fusion.6.two
  50.3 0.0 collective-permute-done
  50.3 1.3 slice_bitcast_fusion.7.one
  51.5 0.7 broadcast_in_dim.19.given
  52.2 1.3 shard_map.57.given
  53.5 1.3 slice_bitcast_fusion.2
  54.8 4.4 %collective-permute-start.3 = (f32[16,12,8,128]{3,2,1,0:T(8,128)}, f32[16,12,8,128]{3,2,1,0:T(8,128)S(1)}, u32[]{:S(2)}, u32[]{:S(2)}) collective-permute-start(f32[16,12,8,128]{3,2,1,0:T(8,128)} %get-tuple-element.39), channel_id=1, source_target_pairs={{0,36},{2,38},{4,0},{6,2},{32,4},{34,6},{36,32},{38,34},{1,37},{3,... | collective-permute-start | bytes 2359304 | tf_op jit(solution)/shard_map/ppermute | solution.py:276
  59.2 0.1 collective-permute-start.2
  59.3 2.7 %pad_maximum_fusion = f32[16,2,12,8,128]{4,3,2,1,0:T(8,128)} fusion(f32[16,1,12,8,128]{4,3,2,1,0:T(8,128)} %bitcast.9, f32[16,1,12,8,128]{4,3,2,1,0:T(8,128)} %bitcast.8), kind=kLoop, calls=%fused_computation | loop fusion | flops 393216 | bytes 3145728 | tf_op jit(solution)/shard_map/stack | solution.py:296
  62.0 2.0 %all-to-all-done.1 = f32[16,2,12,8,128]{4,3,2,1,0:T(8,128)} async-done(((f32[16,2,12,8,128]{4,3,2,1,0:T(8,128)}), f32[16,2,12,8,128]{4,3,2,1,0:T(8,128)}, u32[]{:S(2)}, u32[]{:S(2)}) %all-to-all-start.1) | async-done | bytes 1572896 | tf_op jit(solution)/shard_map/all_to_all | solution.py:271
  64.0 2.6 %slice_bitcast_fusion = (f32[16,12,8,128]{3,2,1,0:T(8,128)}, f32[16,12,8,128]{3,2,1,0:T(8,128)}) fusion(f32[16,2,12,8,128]{4,3,2,1,0:T(8,128)} %all-to-all-done.1), kind=kLoop, calls=%fused_computation.1 | loop fusion | bytes 3145728 | tf_op jit(solution)/shard_map/squeeze | solution.py:293
  66.6 0.0 copy-start.4
  66.6 0.0 copy-start.5
  66.7 0.0 copy-start.6
  66.7 5.6 %all-to-all-start.2 = ((f32[16,2,12,8,128]{4,3,2,1,0:T(8,128)}), f32[16,2,12,8,128]{4,3,2,1,0:T(8,128)S(1)}, u32[]{:S(2)}, u32[]{:S(2)}) async-start(f32[16,2,12,8,128]{4,3,2,1,0:T(8,128)} %pad_maximum_fusion), calls=%async_computation.2 | async-start | bytes 3145728 | tf_op jit(solution)/shard_map/all_to_all | solution.py:271
  72.2 1.3 collective-permute-done.3.refs_1_
  73.5 0.6 slice_bitcast_fusion.4.two
  74.1 4.0 %collective-permute-done.2.refs_0_ = f32[16,12,8,128]{3,2,1,0:T(8,128)S(1)} collective-permute-done((f32[16,12,8,128]{3,2,1,0:T(8,128)}, f32[16,12,8,128]{3,2,1,0:T(8,128)S(1)}, u32[]{:S(2)}, u32[]{:S(2)}) %collective-permute-start.2) | collective-permute-done | bytes 786464 | tf_op jit(solution)/shard_map/ppermute | solution.py:275
  78.1 0.6 slice_bitcast_fusion.5.one
  78.7 1.3 shard_map.59.refs_2_.refs_1_
  80.0 2.8 %collective-permute-start.4 = (f32[16,12,8,128]{3,2,1,0:T(8,128)}, f32[16,12,8,128]{3,2,1,0:T(8,128)}, u32[]{:S(2)}, u32[]{:S(2)}) collective-permute-start(f32[16,12,8,128]{3,2,1,0:T(8,128)} %get-tuple-element.46), channel_id=1, source_target_pairs={{0,4},{2,6},{4,32},{6,34},{32,36},{34,38},{36,0},{38,2},{1,5},{3,7... | collective-permute-start | bytes 2359304 | tf_op jit(solution)/shard_map/ppermute | solution.py:275
  82.9 0.7 collective-permute-start.5
  83.6 0.0 copy-done.4
  83.6 0.0 copy-done.5
  83.6 0.0 copy-done.6
  83.7 0.0 copy-start.2
  83.7 0.7 copy-done.2
  84.3 0.0 copy-start.3
  84.3 6.4 %shard_map.60.refs_5_ = f32[32,9,128]{2,1,0:T(8,128)S(1)} custom-call(s32[1]{0:T(128)} %bitcast.turn, f32[16,12,8,128]{3,2,1,0:T(8,128)S(1)} %collective-permute-done.2.refs_0_, f32[16,12,8,128]{3,2,1,0:T(8,128)S(1)} %collective-permute-done.3.refs_1_, f32[8,128]{1,0:T(8,128)S(1)} %copy-done.2, bf16[256,256]{1,0:T(8,128)(2,1)S(1)} %copy-done.4, ...), custom_call_target="tpu_custom_call" | custom-call | flops 1000000000 | tf_op jit(solution)/shard_map/pallas_call | solution.py:197
  90.7 0.0 copy-start.7
  90.7 0.7 copy-done.7
  91.4 0.0 all-to-all-done.2.refs_0_
  91.4 0.0 copy-done.3
  91.4 0.0 copy-start.8
  91.4 0.9 copy-done.8
  92.4 6.4 %shard_map.61.refs_6_ = f32[32,9,128]{2,1,0:T(8,128)S(1)} custom-call(s32[1]{0:T(128)} %bitcast.turn, f32[16,2,12,8,128]{4,3,2,1,0:T(8,128)S(1)} %all-to-all-done.2.refs_0_, f32[8,128]{1,0:T(8,128)S(1)} %copy-done.3, bf16[256,256]{1,0:T(8,128)(2,1)S(1)} %copy-done.4, bf16[256,256]{1,0:T(8,128)(2,1)S(1)} %copy-done.5, f32[32,2,128]{2,1,0:T(2,128)S(1)} %copy-done.6, ...), custom_call_target="tpu_custom_call" | custom-call | flops 1000000000 | tf_op jit(solution)/shard_map/pallas_call | solution.py:197
  98.7 17.3 %collective-permute-done.4.refs_0_ = f32[16,12,8,128]{3,2,1,0:T(8,128)} collective-permute-done((f32[16,12,8,128]{3,2,1,0:T(8,128)}, f32[16,12,8,128]{3,2,1,0:T(8,128)}, u32[]{:S(2)}, u32[]{:S(2)}) %collective-permute-start.4) | collective-permute-done | bytes 786464 | tf_op jit(solution)/shard_map/ppermute | solution.py:275
  116.0 0.0 collective-permute-done.5.refs_1_
  116.0 7.7 %shard_map.62 = f32[32,9,128]{2,1,0:T(8,128)S(1)} custom-call(s32[1]{0:T(128)} %bitcast.turn, f32[16,12,8,128]{3,2,1,0:T(8,128)} %collective-permute-done.4.refs_0_, f32[16,12,8,128]{3,2,1,0:T(8,128)} %collective-permute-done.5.refs_1_, f32[8,128]{1,0:T(8,128)S(1)} %copy-done.3, bf16[256,256]{1,0:T(8,128)(2,1)S(1)} %copy-done.4, ...), custom_call_target="tpu_custom_call" | custom-call | flops 1000000000 | tf_op jit(solution)/shard_map/pallas_call | solution.py:197
  123.8 0.1 copy.17
  123.9 14.2 %all_to_all.25 = f32[16,2,9,128]{3,1,2,0:T(2,128)S(1)} all-to-all(f32[16,2,9,128]{3,1,2,0:T(2,128)S(1)} %copy.17), channel_id=1, replica_groups=mesh['y'=4,'zh'=2,'x'=4,'zl'=4,'core'=2] {'y','x'}, dimensions={0} | all-to-all | bytes 294912 | tf_op jit(solution)/shard_map/all_to_all | solution.py:271
  138.0 0.1 reduce_sum.18
  138.1 0.1 reshape.72
  138.2 0.1 reshape.75
  138.3 28.8 %all_to_all.26 = f32[16,1,144]{2,1,0:T(1,128)S(1)} all-to-all(f32[16,1,144]{2,1,0:T(1,128)S(1)} %reshape.75), channel_id=1, replica_groups=mesh['y'=4,'zh'=2,'x'=4,'zl'=4,'core'=2] {'zh','zl','core'}, dimensions={0} | all-to-all | bytes 18432 | tf_op jit(solution)/shard_map/all_to_all | solution.py:309
  167.2 0.1 negate_bitcast_fusion
  167.2 0.1 stack.18
  167.3 0.6 copy.22
  (6 shorter events, 0.1 us)
Async XLA Ops:
  0.0 2.3 %copy-start = (f32[2,2,3,3,256,128]{5,4,3,2,1,0:T(8,128)S(1)}, f32[2,2,3,3,256,128]{5,4,3,2,1,0:T(8,128)}, u32[]{:S(2)}) copy-start(f32[2,2,3,3,256,128]{5,4,3,2,1,0:T(8,128)} %param.5) | copy-start | bytes 14155780
  4.4 30.5 %all-to-all-start = ((f32[16,2,12,8,128]{4,3,2,1,0:T(8,128)}), f32[16,2,12,8,128]{4,3,2,1,0:T(8,128)S(1)}, u32[]{:S(2)}, u32[]{:S(2)}) async-start(f32[16,2,12,8,128]{4,3,2,1,0:T(8,128)} %shard_map.56), calls=%async_computation | async-start | bytes 3145728 | tf_op jit(solution)/shard_map/all_to_all | solution.py:271
  12.0 37.0 %collective-permute-start.1 = (f32[16,12,8,128]{3,2,1,0:T(8,128)S(1)}, f32[16,12,8,128]{3,2,1,0:T(8,128)}, u32[]{:S(2)}, u32[]{:S(2)}) collective-permute-start(f32[16,12,8,128]{3,2,1,0:T(8,128)S(1)} %get-tuple-element.31), channel_id=1, source_target_pairs={{0,36},{2,38},{4,0},{6,2},{32,4},{34,6},{36,32},{38,34},{1,37},{3,... | collective-permute-start | bytes 2359304 | tf_op jit(solution)/shard_map/ppermute | solution.py:276
  18.1 32.2 %collective-permute-start = (f32[16,12,8,128]{3,2,1,0:T(8,128)S(1)}, f32[16,12,8,128]{3,2,1,0:T(8,128)}, u32[]{:S(2)}, u32[]{:S(2)}) collective-permute-start(f32[16,12,8,128]{3,2,1,0:T(8,128)S(1)} %get-tuple-element.30), channel_id=1, source_target_pairs={{0,4},{2,6},{4,32},{6,34},{32,36},{34,38},{36,0},{38,2},{1,5},{3,7... | collective-permute-start | bytes 2359304 | tf_op jit(solution)/shard_map/ppermute | solution.py:275
  34.9 2.3 %copy-start.1 = (f32[2,2,3,3,256,128]{5,4,3,2,1,0:T(8,128)S(1)}, f32[2,2,3,3,256,128]{5,4,3,2,1,0:T(8,128)}, u32[]{:S(2)}) copy-start(f32[2,2,3,3,256,128]{5,4,3,2,1,0:T(8,128)} %param.5) | copy-start | bytes 14155780
  38.8 25.2 %all-to-all-start.1 = ((f32[16,2,12,8,128]{4,3,2,1,0:T(8,128)}), f32[16,2,12,8,128]{4,3,2,1,0:T(8,128)}, u32[]{:S(2)}, u32[]{:S(2)}) async-start(f32[16,2,12,8,128]{4,3,2,1,0:T(8,128)} %shard_map.58), calls=%async_computation.1 | async-start | bytes 3145728 | tf_op jit(solution)/shard_map/all_to_all | solution.py:271
  54.8 18.7 %collective-permute-start.3 = (f32[16,12,8,128]{3,2,1,0:T(8,128)}, f32[16,12,8,128]{3,2,1,0:T(8,128)S(1)}, u32[]{:S(2)}, u32[]{:S(2)}) collective-permute-start(f32[16,12,8,128]{3,2,1,0:T(8,128)} %get-tuple-element.39), channel_id=1, source_target_pairs={{0,36},{2,38},{4,0},{6,2},{32,4},{34,6},{36,32},{38,34},{1,37},{3,... | collective-permute-start | bytes 2359304 | tf_op jit(solution)/shard_map/ppermute | solution.py:276
  59.2 18.9 %collective-permute-start.2 = (f32[16,12,8,128]{3,2,1,0:T(8,128)}, f32[16,12,8,128]{3,2,1,0:T(8,128)S(1)}, u32[]{:S(2)}, u32[]{:S(2)}) collective-permute-start(f32[16,12,8,128]{3,2,1,0:T(8,128)} %get-tuple-element.38), channel_id=1, source_target_pairs={{0,4},{2,6},{4,32},{6,34},{32,36},{34,38},{36,0},{38,2},{1,5},{3,7... | collective-permute-start | bytes 2359304 | tf_op jit(solution)/shard_map/ppermute | solution.py:275
  66.6 17.0 %copy-start.4 = (bf16[256,256]{1,0:T(8,128)(2,1)S(1)}, bf16[256,256]{1,0:T(8,128)(2,1)}, u32[]{:S(2)}) copy-start(bf16[256,256]{1,0:T(8,128)(2,1)} %constant.102.clone.refs_3_.refs_2_) | copy-start | bytes 393220
  66.6 17.0 %copy-start.5 = (bf16[256,256]{1,0:T(8,128)(2,1)S(1)}, bf16[256,256]{1,0:T(8,128)(2,1)}, u32[]{:S(2)}) copy-start(bf16[256,256]{1,0:T(8,128)(2,1)} %constant.103.clone.refs_4_.refs_3_) | copy-start | bytes 393220
  66.7 17.0 %copy-start.6 = (f32[32,2,128]{2,1,0:T(2,128)S(1)}, f32[32,2,128]{2,1,0:T(2,128)}, u32[]{:S(2)}) copy-start(f32[32,2,128]{2,1,0:T(2,128)} %constant.104.clone.refs_5_.refs_4_) | copy-start | bytes 98308
  66.7 24.8 %all-to-all-start.2 = ((f32[16,2,12,8,128]{4,3,2,1,0:T(8,128)}), f32[16,2,12,8,128]{4,3,2,1,0:T(8,128)S(1)}, u32[]{:S(2)}, u32[]{:S(2)}) async-start(f32[16,2,12,8,128]{4,3,2,1,0:T(8,128)} %pad_maximum_fusion), calls=%async_computation.2 | async-start | bytes 3145728 | tf_op jit(solution)/shard_map/all_to_all | solution.py:271
  80.0 36.0 %collective-permute-start.4 = (f32[16,12,8,128]{3,2,1,0:T(8,128)}, f32[16,12,8,128]{3,2,1,0:T(8,128)}, u32[]{:S(2)}, u32[]{:S(2)}) collective-permute-start(f32[16,12,8,128]{3,2,1,0:T(8,128)} %get-tuple-element.46), channel_id=1, source_target_pairs={{0,4},{2,6},{4,32},{6,34},{32,36},{34,38},{36,0},{38,2},{1,5},{3,7... | collective-permute-start | bytes 2359304 | tf_op jit(solution)/shard_map/ppermute | solution.py:275
  82.9 33.2 %collective-permute-start.5 = (f32[16,12,8,128]{3,2,1,0:T(8,128)}, f32[16,12,8,128]{3,2,1,0:T(8,128)}, u32[]{:S(2)}, u32[]{:S(2)}) collective-permute-start(f32[16,12,8,128]{3,2,1,0:T(8,128)} %get-tuple-element.47), channel_id=1, source_target_pairs={{0,36},{2,38},{4,0},{6,2},{32,4},{34,6},{36,32},{38,34},{1,37},{3,... | collective-permute-start | bytes 2359304 | tf_op jit(solution)/shard_map/ppermute | solution.py:276
  83.7 0.7 copy-start.2
  84.3 7.1 %copy-start.3 = (f32[8,128]{1,0:T(8,128)S(1)}, f32[8,128]{1,0:T(8,128)}, u32[]{:S(2)}) copy-start(f32[8,128]{1,0:T(8,128)} %shard_map.59.refs_2_.refs_1_) | copy-start | bytes 12292
  90.7 0.7 copy-start.7
  91.4 1.0 copy-start.8

commit v4 on v3

--- a/solution.py
+++ b/solution.py
@@ -225,25 +225,26 @@
     return pl.pallas_call(
         functools.partial(arrange_kernel, c, apart),
         out_shape=[shape] * (2 if apart else 1),
-        in_specs=[pl.BlockSpec(memory_space=pltpu.SMEM), pl.BlockSpec(memory_space=pl.ANY)],
+        in_specs=[pl.BlockSpec(memory_space=pltpu.SMEM), pl.BlockSpec(memory_space=pltpu.HBM)],
         out_specs=[pl.BlockSpec(memory_space=pltpu.VMEM)] * (2 if apart else 1),
         scratch_shapes=[pltpu.SemaphoreType.DMA((2, 4 * ORB))],
-        compiler_params=pltpu.CompilerParams(vmem_limit_bytes=8 * 1024 * 1024),
+        compiler_params=pltpu.CompilerParams(vmem_limit_bytes=60 * 1024 * 1024),
         cost_estimate=pl.CostEstimate(flops=0, bytes_accessed=3_200_000, transcendentals=0),
     )(first, parts)
 
 
 def settle(weights, fields, cost):
-    def body(given, one, two, out):
-        out[...] = given[...]
+    def body(given, *refs):
+        refs[-1][...] = given[...]
 
     return pl.pallas_call(
         body,
         out_shape=jax.ShapeDtypeStruct((SLOTS, LANES), jnp.float32),
-        in_specs=[pl.BlockSpec(memory_space=pltpu.VMEM)] * 3,
+        in_specs=[pl.BlockSpec(memory_space=pltpu.VMEM)] + [pl.BlockSpec(memory_space=pl.ANY)] * len(fields),
         out_specs=pl.BlockSpec(memory_space=pltpu.VMEM),
+        compiler_params=pltpu.CompilerParams(vmem_limit_bytes=1024 * 1024),
         cost_estimate=pl.CostEstimate(flops=int(cost * 1e9), bytes_accessed=0, transcendentals=0),
-    )(weights, *(field[0, 0] for field in fields))
+    )(weights, *fields)
 
 
 def shifted(step):
@@ -285,17 +286,17 @@
     side = zh.reshape(1).astype(jnp.int32)
     zero = arrange(side, parts, 0, True)
     zero, side = fence((zero, side))
-    zero = move(*zero)
+    zero = tuple(move(*zero))
     (one,) = arrange(side, parts, 1, False)
     one, side = fence((spread(one), side))
     (two,) = arrange(side, parts, 2, False)
     two = spread(two)
-    one, two = (one[:, 0], one[:, 1]), (two[:, 0], two[:, 1])
-    zero, one, weights = fence((zero, one, settle(weights, zero, 0.0)))
-    one = move(*one)
+    one, two = tuple(fence((one[:, 0], one[:, 1]))), tuple(fence((two[:, 0], two[:, 1])))
+    zero, one, weights = fence((zero, one, settle(weights, zero + one, 6.0)))
+    one = tuple(move(*one))
     zero, two = fence((jnp.stack(zero, 1), two))
     zero = spread(zero)
-    one, two, weights = fence((one, two, settle(weights, one, 0.0)))
+    one, two, weights = fence((one, two, settle(weights, one + two, 6.0)))
     two = move(*two)
     partial = work(one, partial, weights)
     partial = work([zero], partial, weights)

time: 169 us -> 165 us (0.976)
  waiting for transfers between devices: 46.1 us -> 65 us
  blocking collectives: 43 us -> 26.6 us
  local copies, waits for them, and re-layouts: 16.3 us -> 8.64 us
  Pallas kernels: 26.7 us -> 30.7 us
    all_to_all x1, blocking collectives: 28.8 us -> 13.3 us  [per_device(): lax.all_to_all(shares, ('zh', 'zl', 'core'), split_axis=0, concat_axis=0)]
    ppermute x3, waiting for transfers between devices: 21.3 us -> 35 us  [move(): lax.ppermute(rising, ('zh', 'zl'), shifted(2))]
    ppermute x3, starting transfers between devices: 11.2 us -> 4.8 us  [move(): lax.ppermute(falling, ('zh', 'zl'), shifted(-2))]
    ppermute x3, starting transfers between devices: 2.96 us -> 8.54 us  [move(): lax.ppermute(rising, ('zh', 'zl'), shifted(2))]
    pallas_call x3, Pallas kernels: 3.65 us -> 8.88 us  [arrange(): pl.pallas_call(functools.partial(arrange_kernel, c, apart), out_shape=[sh...]
    unnamed x18 -> x14, local copies, waits for them, and re-layouts: 7.01 us -> 2.79 us
    ppermute x3, waiting for transfers between devices: 6.02 us -> 8.97 us  [move(): lax.ppermute(falling, ('zh', 'zl'), shifted(-2))]
    squeeze x6 -> x2, local copies, waits for them, and re-layouts: 7.65 us -> 4.77 us  [the longest x1 2.4 us: per_device(): one[:, 1]]
  transfers between devices with their start and end apart: 9 -> 9, of which waited for: 6 -> 6; matrix products, arithmetic and copies ran while one was open for 7% -> 4% of each run, Pallas kernels for 10% -> 11%
where the time goes in v4:
time: 165 us; the launch traced here: 164 us
  waiting for transfers between devices  65 us (39%)
  starting transfers between devices  31 us (19%)
  Pallas kernels  30.7 us (19%)
  blocking collectives  26.6 us (16%)
  local copies, waits for them, and re-layouts  8.64 us (5%)
    ppermute x3, waiting for transfers between devices, move(): lax.ppermute(rising, ('zh', 'zl'), shifted(2))  35 us
    pallas_call x3, Pallas kernels, collide(): pl.pallas_call(kernel, out_shape=jax.ShapeDtypeStruct((ROWS, PAIRS, LANES...  21.8 us
    all_to_all x3, waiting for transfers between devices, spread(): return lax.all_to_all(value, ('y', 'x'), split_axis=0, concat_axis=0)  21 us
    all_to_all x3, starting transfers between devices, spread(): return lax.all_to_all(value, ('y', 'x'), split_axis=0, concat_axis=0)  17.7 us
    all_to_all x1, blocking collectives, per_device(): lax.all_to_all(shares, ('zh', 'zl', 'core'), split_axis=0, concat_axis=0)  13.3 us
    all_to_all x1, blocking collectives, spread(): return lax.all_to_all(value, ('y', 'x'), split_axis=0, concat_axis=0)  13.2 us
    ppermute x3, waiting for transfers between devices, move(): lax.ppermute(falling, ('zh', 'zl'), shifted(-2))  8.97 us
    pallas_call x3, Pallas kernels, arrange(): pl.pallas_call(functools.partial(arrange_kernel, c, apart), out_shape=[sh...  8.88 us
  transfers between devices with their start and end apart: 9, of which 6 were waited for; matrix products, arithmetic and copies ran while one was open for 4% of the time, Pallas kernels for 11%

profile of v4, /device:TPU:1, one launch (start us, length us, event | category | flops | bytes accessed | tf_op | source)
XLA Modules:
  0.0 164.3 jit_solution(11625824458634607345)
XLA Ops:
  0.0 2.8 %shard_map.55 = (f32[16,12,8,128]{3,2,1,0:T(8,128)}, f32[16,12,8,128]{3,2,1,0:T(8,128)}) custom-call(s32[1]{0:T(128)} %bitcast.1.first, f32[12,3,2,16,8,128]{5,4,3,2,1,0:T(8,128)} %bitcast.49), custom_call_target="tpu_custom_call" | custom-call | bytes 3200000 | tf_op jit(solution)/shard_map/pallas_call | solution.py:225
  2.8 2.8 %shard_map.56 = f32[16,2,12,8,128]{4,3,2,1,0:T(8,128)} custom-call(s32[1]{0:T(128)} %bitcast.1.first, f32[12,3,2,16,8,128]{5,4,3,2,1,0:T(8,128)} %bitcast.50), custom_call_target="tpu_custom_call" | custom-call | bytes 3200000 | tf_op jit(solution)/shard_map/pallas_call | solution.py:225
  5.6 7.6 %all-to-all-start = ((f32[16,2,12,8,128]{4,3,2,1,0:T(8,128)}), f32[16,2,12,8,128]{4,3,2,1,0:T(8,128)S(1)}, u32[]{:S(2)}, u32[]{:S(2)}) async-start(f32[16,2,12,8,128]{4,3,2,1,0:T(8,128)} %shard_map.56), calls=%async_computation | async-start | bytes 3145728 | tf_op jit(solution)/shard_map/all_to_all | solution.py:272
  13.2 3.1 %collective-permute-start = (f32[16,12,8,128]{3,2,1,0:T(8,128)}, f32[16,12,8,128]{3,2,1,0:T(8,128)S(1)}, u32[]{:S(2)}, u32[]{:S(2)}) collective-permute-start(f32[16,12,8,128]{3,2,1,0:T(8,128)} %get-tuple-element.34), channel_id=1, source_target_pairs={{0,4},{2,6},{4,32},{6,34},{32,36},{34,38},{36,0},{38,2},{1,5},{3,7... | collective-permute-start | bytes 2359304 | tf_op jit(solution)/shard_map/ppermute | solution.py:276
  16.3 3.1 %collective-permute-start.1 = (f32[16,12,8,128]{3,2,1,0:T(8,128)}, f32[16,12,8,128]{3,2,1,0:T(8,128)S(1)}, u32[]{:S(2)}, u32[]{:S(2)}) collective-permute-start(f32[16,12,8,128]{3,2,1,0:T(8,128)} %get-tuple-element.35), channel_id=1, source_target_pairs={{0,36},{2,38},{4,0},{6,2},{32,4},{34,6},{36,32},{38,34},{1,37},{3,... | collective-permute-start | bytes 2359304 | tf_op jit(solution)/shard_map/ppermute | solution.py:277
  19.4 16.7 %all-to-all-done = f32[16,2,12,8,128]{4,3,2,1,0:T(8,128)S(1)} async-done(((f32[16,2,12,8,128]{4,3,2,1,0:T(8,128)}), f32[16,2,12,8,128]{4,3,2,1,0:T(8,128)S(1)}, u32[]{:S(2)}, u32[]{:S(2)}) %all-to-all-start) | async-done | bytes 1572896 | tf_op jit(solution)/shard_map/all_to_all | solution.py:272
  36.1 0.0 copy-start.6
  36.1 3.3 %shard_map.58 = f32[16,2,12,8,128]{4,3,2,1,0:T(8,128)} custom-call(s32[1]{0:T(128)} %bitcast.1.first, f32[12,3,2,16,8,128]{5,4,3,2,1,0:T(8,128)} %bitcast.51), custom_call_target="tpu_custom_call" | custom-call | bytes 3200000 | tf_op jit(solution)/shard_map/pallas_call | solution.py:225
  39.4 0.0 copy-done.6
  39.4 4.6 %all-to-all-start.1 = ((f32[16,2,12,8,128]{4,3,2,1,0:T(8,128)}), f32[16,2,12,8,128]{4,3,2,1,0:T(8,128)}, u32[]{:S(2)}, u32[]{:S(2)}) async-start(f32[16,2,12,8,128]{4,3,2,1,0:T(8,128)} %shard_map.58), calls=%async_computation.1 | async-start | bytes 3145728 | tf_op jit(solution)/shard_map/all_to_all | solution.py:272
  44.7 2.4 %slice_bitcast_fusion.2 = (f32[16,12,8,128]{3,2,1,0:T(8,128)S(1)}, f32[16,12,8,128]{3,2,1,0:T(8,128)}) fusion(f32[16,2,12,8,128]{4,3,2,1,0:T(8,128)} %copy-done.6), kind=kLoop, calls=%fused_computation.3 | loop fusion | bytes 3145728 | tf_op jit(solution)/shard_map/squeeze | solution.py:294
  47.1 0.0 collective-permute-done.refs_0_
  47.1 8.0 %collective-permute-done.1.refs_1_ = f32[16,12,8,128]{3,2,1,0:T(8,128)S(1)} collective-permute-done((f32[16,12,8,128]{3,2,1,0:T(8,128)}, f32[16,12,8,128]{3,2,1,0:T(8,128)S(1)}, u32[]{:S(2)}, u32[]{:S(2)}) %collective-permute-start.1) | collective-permute-done | bytes 786464 | tf_op jit(solution)/shard_map/ppermute | solution.py:277
  55.1 0.1 broadcast_in_dim.19.given
  55.2 3.0 %collective-permute-start.2 = (f32[16,12,8,128]{3,2,1,0:T(8,128)}, f32[16,12,8,128]{3,2,1,0:T(8,128)}, u32[]{:S(2)}, u32[]{:S(2)}) collective-permute-start(f32[16,12,8,128]{3,2,1,0:T(8,128)} %get-tuple-element.46.refs_2_), channel_id=1, source_target_pairs={{0,4},{2,6},{4,32},{6,34},{32,36},{34,38},{36,0},{38,2},{1,5},{3,7... | collective-permute-start | bytes 2359304 | tf_op jit(solution)/shard_map/ppermute | solution.py:276
  58.2 0.6 collective-permute-start.3
  58.8 1.3 pad_maximum_fusion
  60.1 4.3 %all-to-all-done.1 = f32[16,2,12,8,128]{4,3,2,1,0:T(8,128)} async-done(((f32[16,2,12,8,128]{4,3,2,1,0:T(8,128)}), f32[16,2,12,8,128]{4,3,2,1,0:T(8,128)}, u32[]{:S(2)}, u32[]{:S(2)}) %all-to-all-start.1) | async-done | bytes 1572896 | tf_op jit(solution)/shard_map/all_to_all | solution.py:272
  64.3 2.4 %slice_bitcast_fusion = (f32[16,12,8,128]{3,2,1,0:T(8,128)S(1)}, f32[16,12,8,128]{3,2,1,0:T(8,128)}) fusion(f32[16,2,12,8,128]{4,3,2,1,0:T(8,128)} %all-to-all-done.1), kind=kLoop, calls=%fused_computation.1 | loop fusion | bytes 3145728 | tf_op jit(solution)/shard_map/squeeze | solution.py:294
  66.7 0.0 copy-start.1
  66.7 0.0 copy-start.2
  66.7 0.0 copy-start.3
  66.7 5.5 %all-to-all-start.2 = ((f32[16,2,12,8,128]{4,3,2,1,0:T(8,128)}), f32[16,2,12,8,128]{4,3,2,1,0:T(8,128)S(1)}, u32[]{:S(2)}, u32[]{:S(2)}) async-start(f32[16,2,12,8,128]{4,3,2,1,0:T(8,128)} %pad_maximum_fusion), calls=%async_computation.2 | async-start | bytes 3145728 | tf_op jit(solution)/shard_map/all_to_all | solution.py:272
  72.2 20.8 %collective-permute-done.2.refs_0_ = f32[16,12,8,128]{3,2,1,0:T(8,128)} collective-permute-done((f32[16,12,8,128]{3,2,1,0:T(8,128)}, f32[16,12,8,128]{3,2,1,0:T(8,128)}, u32[]{:S(2)}, u32[]{:S(2)}) %collective-permute-start.2) | collective-permute-done | bytes 786464 | tf_op jit(solution)/shard_map/ppermute | solution.py:276
  93.0 0.0 collective-permute-done.3.refs_1_
  93.0 0.0 copy-start
  93.0 1.1 copy-done
  94.2 2.5 %collective-permute-start.4 = (f32[16,12,8,128]{3,2,1,0:T(8,128)S(1)}, f32[16,12,8,128]{3,2,1,0:T(8,128)}, u32[]{:S(2)}, u32[]{:S(2)}) collective-permute-start(f32[16,12,8,128]{3,2,1,0:T(8,128)S(1)} %copy-done), channel_id=1, source_target_pairs={{0,4},{2,6},{4,32},{6,34},{32,36},{34,38},{36,0},{38,2},{1,5},{3,7... | collective-permute-start | bytes 2359304 | tf_op jit(solution)/shard_map/ppermute | solution.py:276
  96.6 1.1 collective-permute-start.5
  97.8 0.0 copy-done.1
  97.8 0.0 copy-done.2
  97.8 0.0 copy-done.3
  97.8 7.7 %shard_map.60.refs_5_ = f32[32,9,128]{2,1,0:T(8,128)S(1)} custom-call(s32[1]{0:T(128)} %bitcast.turn, f32[16,12,8,128]{3,2,1,0:T(8,128)} %collective-permute-done.2.refs_0_, f32[16,12,8,128]{3,2,1,0:T(8,128)} %collective-permute-done.3.refs_1_, f32[8,128]{1,0:T(8,128)S(1)} %shard_map.59.refs_2_.refs_1_, bf16[256,256]{1,0:T(8,128)(2,1)S(1)} %copy-done.1, ...), custom_call_target="tpu_custom_call" | custom-call | flops 1000000000 | tf_op jit(solution)/shard_map/pallas_call | solution.py:197
  105.5 0.0 copy-start.4
  105.5 0.7 copy-done.4
  106.2 0.0 all-to-all-done.2.refs_0_
  106.2 0.0 copy-start.5
  106.2 0.9 copy-done.5
  107.2 6.4 %shard_map.61.refs_6_ = f32[32,9,128]{2,1,0:T(8,128)S(1)} custom-call(s32[1]{0:T(128)} %bitcast.turn, f32[16,2,12,8,128]{4,3,2,1,0:T(8,128)S(1)} %all-to-all-done.2.refs_0_, f32[8,128]{1,0:T(8,128)S(1)} %shard_map.59.refs_2_.refs_1_, bf16[256,256]{1,0:T(8,128)(2,1)S(1)} %copy-done.1, bf16[256,256]{1,0:T(8,128)(2,1)S(1)} %copy-done.2, ...), custom_call_target="tpu_custom_call" | custom-call | flops 1000000000 | tf_op jit(solution)/shard_map/pallas_call | solution.py:197
  113.6 14.2 %collective-permute-done.4.refs_0_ = f32[16,12,8,128]{3,2,1,0:T(8,128)} collective-permute-done((f32[16,12,8,128]{3,2,1,0:T(8,128)S(1)}, f32[16,12,8,128]{3,2,1,0:T(8,128)}, u32[]{:S(2)}, u32[]{:S(2)}) %collective-permute-start.4) | collective-permute-done | bytes 786464 | tf_op jit(solution)/shard_map/ppermute | solution.py:276
  127.8 1.0 collective-permute-done.5.refs_1_
  128.8 7.7 %shard_map.62 = f32[32,9,128]{2,1,0:T(8,128)S(1)} custom-call(s32[1]{0:T(128)} %bitcast.turn, f32[16,12,8,128]{3,2,1,0:T(8,128)} %collective-permute-done.4.refs_0_, f32[16,12,8,128]{3,2,1,0:T(8,128)} %collective-permute-done.5.refs_1_, f32[8,128]{1,0:T(8,128)S(1)} %shard_map.59.refs_2_.refs_1_, bf16[256,256]{1,0:T(8,128)(2,1)S(1)} %copy-done.1, ...), custom_call_target="tpu_custom_call" | custom-call | flops 1000000000 | tf_op jit(solution)/shard_map/pallas_call | solution.py:197
  136.5 0.1 copy.17
  136.6 13.2 %all_to_all.25 = f32[16,2,9,128]{3,1,2,0:T(2,128)S(1)} all-to-all(f32[16,2,9,128]{3,1,2,0:T(2,128)S(1)} %copy.17), channel_id=1, replica_groups=mesh['y'=4,'zh'=2,'x'=4,'zl'=4,'core'=2] {'y','x'}, dimensions={0} | all-to-all | bytes 294912 | tf_op jit(solution)/shard_map/all_to_all | solution.py:272
  149.8 0.1 reduce_sum.18
  149.9 0.1 reshape.72
  150.0 0.1 reshape.75
  150.1 13.3 %all_to_all.26 = f32[16,1,144]{2,1,0:T(1,128)S(1)} all-to-all(f32[16,1,144]{2,1,0:T(1,128)S(1)} %reshape.75), channel_id=1, replica_groups=mesh['y'=4,'zh'=2,'x'=4,'zl'=4,'core'=2] {'zh','zl','core'}, dimensions={0} | all-to-all | bytes 18432 | tf_op jit(solution)/shard_map/all_to_all | solution.py:310
  163.5 0.1 negate_bitcast_fusion
  163.6 0.1 stack.18
  163.7 0.6 copy.22
  (8 shorter events, 0.1 us)
Async XLA Ops:
  5.6 30.5 %all-to-all-start = ((f32[16,2,12,8,128]{4,3,2,1,0:T(8,128)}), f32[16,2,12,8,128]{4,3,2,1,0:T(8,128)S(1)}, u32[]{:S(2)}, u32[]{:S(2)}) async-start(f32[16,2,12,8,128]{4,3,2,1,0:T(8,128)} %shard_map.56), calls=%async_computation | async-start | bytes 3145728 | tf_op jit(solution)/shard_map/all_to_all | solution.py:272
  13.2 33.9 %collective-permute-start = (f32[16,12,8,128]{3,2,1,0:T(8,128)}, f32[16,12,8,128]{3,2,1,0:T(8,128)S(1)}, u32[]{:S(2)}, u32[]{:S(2)}) collective-permute-start(f32[16,12,8,128]{3,2,1,0:T(8,128)} %get-tuple-element.34), channel_id=1, source_target_pairs={{0,4},{2,6},{4,32},{6,34},{32,36},{34,38},{36,0},{38,2},{1,5},{3,7... | collective-permute-start | bytes 2359304 | tf_op jit(solution)/shard_map/ppermute | solution.py:276
  16.3 38.9 %collective-permute-start.1 = (f32[16,12,8,128]{3,2,1,0:T(8,128)}, f32[16,12,8,128]{3,2,1,0:T(8,128)S(1)}, u32[]{:S(2)}, u32[]{:S(2)}) collective-permute-start(f32[16,12,8,128]{3,2,1,0:T(8,128)} %get-tuple-element.35), channel_id=1, source_target_pairs={{0,36},{2,38},{4,0},{6,2},{32,4},{34,6},{36,32},{38,34},{1,37},{3,... | collective-permute-start | bytes 2359304 | tf_op jit(solution)/shard_map/ppermute | solution.py:277
  36.1 3.3 %copy-start.6 = (f32[16,2,12,8,128]{4,3,2,1,0:T(8,128)}, f32[16,2,12,8,128]{4,3,2,1,0:T(8,128)S(1)}, u32[]{:S(2)}) copy-start(f32[16,2,12,8,128]{4,3,2,1,0:T(8,128)S(1)} %all-to-all-done) | copy-start | bytes 4718596
  39.4 24.9 %all-to-all-start.1 = ((f32[16,2,12,8,128]{4,3,2,1,0:T(8,128)}), f32[16,2,12,8,128]{4,3,2,1,0:T(8,128)}, u32[]{:S(2)}, u32[]{:S(2)}) async-start(f32[16,2,12,8,128]{4,3,2,1,0:T(8,128)} %shard_map.58), calls=%async_computation.1 | async-start | bytes 3145728 | tf_op jit(solution)/shard_map/all_to_all | solution.py:272
  55.2 37.8 %collective-permute-start.2 = (f32[16,12,8,128]{3,2,1,0:T(8,128)}, f32[16,12,8,128]{3,2,1,0:T(8,128)}, u32[]{:S(2)}, u32[]{:S(2)}) collective-permute-start(f32[16,12,8,128]{3,2,1,0:T(8,128)} %get-tuple-element.46.refs_2_), channel_id=1, source_target_pairs={{0,4},{2,6},{4,32},{6,34},{32,36},{34,38},{36,0},{38,2},{1,5},{3,7... | collective-permute-start | bytes 2359304 | tf_op jit(solution)/shard_map/ppermute | solution.py:276
  58.2 34.8 %collective-permute-start.3 = (f32[16,12,8,128]{3,2,1,0:T(8,128)S(1)}, f32[16,12,8,128]{3,2,1,0:T(8,128)}, u32[]{:S(2)}, u32[]{:S(2)}) collective-permute-start(f32[16,12,8,128]{3,2,1,0:T(8,128)S(1)} %get-tuple-element.47.refs_3_), channel_id=1, source_target_pairs={{0,36},{2,38},{4,0},{6,2},{32,4},{34,6},{36,32},{38,34},{1,37},{3,... | collective-permute-start | bytes 2359304 | tf_op jit(solution)/shard_map/ppermute | solution.py:277
  66.7 31.1 %copy-start.1 = (bf16[256,256]{1,0:T(8,128)(2,1)S(1)}, bf16[256,256]{1,0:T(8,128)(2,1)}, u32[]{:S(2)}) copy-start(bf16[256,256]{1,0:T(8,128)(2,1)} %constant.102.clone.refs_3_.refs_2_) | copy-start | bytes 393220
  66.7 31.1 %copy-start.2 = (bf16[256,256]{1,0:T(8,128)(2,1)S(1)}, bf16[256,256]{1,0:T(8,128)(2,1)}, u32[]{:S(2)}) copy-start(bf16[256,256]{1,0:T(8,128)(2,1)} %constant.103.clone.refs_4_.refs_3_) | copy-start | bytes 393220
  66.7 31.1 %copy-start.3 = (f32[32,2,128]{2,1,0:T(2,128)S(1)}, f32[32,2,128]{2,1,0:T(2,128)}, u32[]{:S(2)}) copy-start(f32[32,2,128]{2,1,0:T(2,128)} %constant.104.clone.refs_5_.refs_4_) | copy-start | bytes 98308
  66.7 39.5 %all-to-all-start.2 = ((f32[16,2,12,8,128]{4,3,2,1,0:T(8,128)}), f32[16,2,12,8,128]{4,3,2,1,0:T(8,128)S(1)}, u32[]{:S(2)}, u32[]{:S(2)}) async-start(f32[16,2,12,8,128]{4,3,2,1,0:T(8,128)} %pad_maximum_fusion), calls=%async_computation.2 | async-start | bytes 3145728 | tf_op jit(solution)/shard_map/all_to_all | solution.py:272
  93.0 1.1 copy-start
  94.2 33.6 %collective-permute-start.4 = (f32[16,12,8,128]{3,2,1,0:T(8,128)S(1)}, f32[16,12,8,128]{3,2,1,0:T(8,128)}, u32[]{:S(2)}, u32[]{:S(2)}) collective-permute-start(f32[16,12,8,128]{3,2,1,0:T(8,128)S(1)} %copy-done), channel_id=1, source_target_pairs={{0,4},{2,6},{4,32},{6,34},{32,36},{34,38},{36,0},{38,2},{1,5},{3,7... | collective-permute-start | bytes 2359304 | tf_op jit(solution)/shard_map/ppermute | solution.py:276
  96.6 32.2 %collective-permute-start.5 = (f32[16,12,8,128]{3,2,1,0:T(8,128)S(1)}, f32[16,12,8,128]{3,2,1,0:T(8,128)}, u32[]{:S(2)}, u32[]{:S(2)}) collective-permute-start(f32[16,12,8,128]{3,2,1,0:T(8,128)S(1)} %get-tuple-element.55.refs_3_), channel_id=1, source_target_pairs={{0,36},{2,38},{4,0},{6,2},{32,4},{34,6},{36,32},{38,34},{1,37},{3,... | collective-permute-start | bytes 2359304 | tf_op jit(solution)/shard_map/ppermute | solution.py:277
  105.5 0.7 copy-start.4
  106.2 1.0 copy-start.5

commit v5 on v4

--- a/solution.py
+++ b/solution.py
@@ -97,18 +97,26 @@
     return dot(head, high) + (dot(tail, high) + dot(head, low))
 
 
-def kernel(turn, *refs):
-    *given_refs, weight, high_ref, low_ref, twiddle, before, out, field = refs
+def kernel(count, stacked, joined, spilled, turn, *refs):
+    refs = list(refs)
+    if stacked:
+        whole = refs.pop(0)
+        lower, upper = whole.at[:, 0], whole.at[:, 1]
+    else:
+        lower, upper = refs.pop(0), refs.pop(0)
+    if joined:
+        older, older_sigma = refs.pop(0), refs.pop(0)
+    weight, high_ref, low_ref, twiddle, before, out = refs[:6]
+    field = refs[-1]
     straight = turn[0] == 0
-    if len(given_refs) == 2:
-        lower, upper = given_refs
-    else:
-        lower, upper = given_refs[0].at[:, 0], given_refs[0].at[:, 1]
-
-    def green(m, at):
+
+    def choose(one, two, m, at):
         plane, half = m // 8 * 4 + m % 4, m // 4 % 2
-        one, two = lower[plane, at], upper[plane, at]
-        return jnp.where(straight == (half == 0), one, two)
+        return jnp.where(straight == (half == 0), one[plane, at], two[plane, at])
+
+    def pair_of(one, two, pairs, m, comp, pair):
+        at = comp * 2 * pairs + pair
+        return choose(one, two, m, at), choose(one, two, m, at + pairs)
 
     def spot(part):
         return pl.ds(part * LANES, LANES)
@@ -119,26 +127,25 @@
     def times(value, factor):
         return value[0] * factor[0] - value[1] * factor[1], value[0] * factor[1] + value[1] * factor[0]
 
-    @pl.loop(0, 2 * ORB)
+    @pl.loop(0, 2 * count)
     def _(s):
-        comp, pair = s // ORB, s % ORB
-        at = comp * 2 * ORB + pair
+        comp, pair = s // count, s % count
         rows = pl.ds(pl.multiple_of(comp * SLOTS, SLOTS), SLOTS)
-        values = [(green(m, at), green(m, at + ORB)) for m in range(ROWS)]
+        values = [pair_of(lower, upper, count, m, comp, pair) for m in range(ROWS)]
         for n, value in enumerate(fourier(values)):
             real, imag = times(value, twist(n)) if n else value
             field[n, pair, rows, spot(0)] = real
             field[n, pair, rows, spot(1)] = imag
 
     block = 8
-    size = block * ORB * 2 * SLOTS
+    size = block * count * 2 * SLOTS
 
     @pl.loop(0, ROWS // block)
     def _(b):
         take = pl.ds(b * block, block)
         high, low = high_ref[...], low_ref[...]
         space = product(field[take].reshape(size, 2 * LANES), high, low)
-        space = space.reshape(block * ORB, 2, SLOTS, 2 * LANES)
+        space = space.reshape(block * count, 2, SLOTS, 2 * LANES)
         less = space[:, 0, :, :LANES], space[:, 0, :, LANES:]
         great = space[:, 1, :, :LANES], space[:, 1, :, LANES:]
 
@@ -151,11 +158,11 @@
             [jnp.concatenate(bubble(less, great), -1), jnp.concatenate(bubble(great, less), -1)], 1
         )
         back = product(sigma.reshape(size, 2 * LANES), high, low)
-        field[take] = back.reshape(block, ORB, 2 * SLOTS, 2 * LANES)
-
-    @pl.loop(0, 2 * ORB)
+        field[take] = back.reshape(block, count, 2 * SLOTS, 2 * LANES)
+
+    @pl.loop(0, 2 * count)
     def _(s):
-        comp, pair = s // ORB, s % ORB
+        comp, pair = s // count, s % count
         rows = pl.ds(pl.multiple_of(comp * SLOTS, SLOTS), SLOTS)
         values = [(field[n, pair, rows, spot(0)], field[n, pair, rows, spot(1)]) for n in range(ROWS)]
         values = [times(value, twist(n)) if n else value for n, value in enumerate(values)]
@@ -169,11 +176,14 @@
     def _(m):
         def sigma(comp, a):
             rows = pl.ds(comp * SLOTS, SLOTS)
-            return field[m, a, rows, spot(0)], field[m, a, rows, spot(1)]
+            if joined and a == 0:
+                return older_sigma[m, rows, spot(0)], older_sigma[m, rows, spot(1)]
+            return field[m, a - joined, rows, spot(0)], field[m, a - joined, rows, spot(1)]
 
         def given(comp, b):
-            at = comp * 2 * ORB + b
-            return green(m, at), green(m, at + ORB)
+            if joined and b == 0:
+                return pair_of(older.at[:, 0], older.at[:, 1], ORB + 1, m, comp, ORB)
+            return pair_of(lower, upper, count, m, comp, b - joined)
 
         def memory(a, b):
             left, right = sigma(0, a), given(1, b)
@@ -191,43 +201,58 @@
         for i, result in enumerate(results):
             spare, row = (m // 8 * 4 + m % 4) * 2 + m // 4 % 2, pl.ds(i, 1)
             out[spare, row, :] = before[spare, row, :] + jnp.sum(result * scale, axis=0, keepdims=True)
-
-
-def collide(turn, fields, weights, high, low, twiddle, before):
+        if spilled:
+            refs[6][m] = field[m, ORB]
+
+
+def collide(turn, fields, weights, high, low, twiddle, before, older=(), spilled=False):
+    stacked, joined = len(fields) == 1, int(len(older) > 0)
+    count = ORB + 1 if stacked else ORB - joined
+    shapes = [jax.ShapeDtypeStruct((ROWS, PAIRS, LANES), jnp.float32)]
+    if spilled:
+        shapes.append(jax.ShapeDtypeStruct((ROWS, 2 * SLOTS, 2 * LANES), jnp.float32))
+    inputs = (*fields, *older, weights, high, low, twiddle, before)
     return pl.pallas_call(
-        kernel,
-        out_shape=jax.ShapeDtypeStruct((ROWS, PAIRS, LANES), jnp.float32),
-        in_specs=[pl.BlockSpec(memory_space=pltpu.SMEM)] + [pl.BlockSpec(memory_space=pltpu.VMEM)] * (len(fields) + 5),
-        out_specs=pl.BlockSpec(memory_space=pltpu.VMEM),
-        scratch_shapes=[pltpu.VMEM((ROWS, ORB, 2 * SLOTS, 2 * LANES), jnp.float32)],
+        functools.partial(kernel, count, stacked, joined, spilled),
+        out_shape=shapes,
+        in_specs=[pl.BlockSpec(memory_space=pltpu.SMEM)]
+        + [pl.BlockSpec(memory_space=pltpu.VMEM)] * len(inputs),
+        out_specs=[pl.BlockSpec(memory_space=pltpu.VMEM)] * len(shapes),
+        scratch_shapes=[pltpu.VMEM((ROWS, count, 2 * SLOTS, 2 * LANES), jnp.float32)],
         compiler_params=pltpu.CompilerParams(vmem_limit_bytes=24 * 1024 * 1024),
         cost_estimate=pl.CostEstimate(flops=1000000000, bytes_accessed=0, transcendentals=0),
-    )(turn, *fields, weights, high, low, twiddle, before)
-
-
-def arrange_kernel(c, apart, first, parts, *refs):
+    )(turn, *inputs)
+
+
+def arrange_kernel(blocks, apart, first, parts, *refs):
     *outs, sems = refs
-    copies = []
-    for n in range(2):
-        half = first[0] if n == 0 else 1 - first[0]
-        for at in range(4 * ORB):
-            target = outs[n].at[:, at] if apart else outs[0].at[:, n, at]
-            copies.append(pltpu.make_async_copy(parts.at[at, c, half], target, sems.at[n, at]))
+    copies, base = [], 0
+    for pairs in blocks:
+        for kind in range(4):
+            for i, (a, c) in enumerate(pairs):
+                at = base + kind * len(pairs) + i
+                for n in range(2):
+                    half = first[0] if n == 0 else 1 - first[0]
+                    target = outs[n].at[:, at] if apart else outs[0].at[:, n, at]
+                    source = parts.at[kind * ORB + a, c, half]
+                    copies.append(pltpu.make_async_copy(source, target, sems.at[n, at]))
+        base += 4 * len(pairs)
     for copy in copies:
         copy.start()
     for copy in copies:
         copy.wait()
 
 
-def arrange(first, parts, c, apart):
-    whole = (PLANE, 4 * ORB, SLOTS, LANES) if apart else (PLANE, 2, 4 * ORB, SLOTS, LANES)
+def arrange(first, parts, blocks, apart):
+    count = 4 * sum(len(pairs) for pairs in blocks)
+    whole = (PLANE, count, SLOTS, LANES) if apart else (PLANE, 2, count, SLOTS, LANES)
     shape = jax.ShapeDtypeStruct(whole, jnp.float32)
     return pl.pallas_call(
-        functools.partial(arrange_kernel, c, apart),
+        functools.partial(arrange_kernel, blocks, apart),
         out_shape=[shape] * (2 if apart else 1),
-        in_specs=[pl.BlockSpec(memory_space=pltpu.SMEM), pl.BlockSpec(memory_space=pltpu.HBM)],
+        in_specs=[pl.BlockSpec(memory_space=pltpu.SMEM), pl.BlockSpec(memory_space=pl.ANY)],
         out_specs=[pl.BlockSpec(memory_space=pltpu.VMEM)] * (2 if apart else 1),
-        scratch_shapes=[pltpu.SemaphoreType.DMA((2, 4 * ORB))],
+        scratch_shapes=[pltpu.SemaphoreType.DMA((2, count))],
         compiler_params=pltpu.CompilerParams(vmem_limit_bytes=60 * 1024 * 1024),
         cost_estimate=pl.CostEstimate(flops=0, bytes_accessed=3_200_000, transcendentals=0),
     )(first, parts)
@@ -277,32 +302,32 @@
             lax.ppermute(falling, ("zh", "zl"), shifted(-2)),
         )
 
-    def work(fields, partial, weights):
-        return collide(turn_flag, fields, weights, high, low, twiddle, partial)
+    def work(fields, partial, weights, **more):
+        return collide(turn_flag, fields, weights, high, low, twiddle, partial, **more)
 
     turn_flag = turn.reshape(1).astype(jnp.int32)
     partial = jnp.zeros((ROWS, PAIRS, LANES), jnp.float32)
     fence = lax.optimization_barrier
+    early = [[(0, 0), (1, 0), (2, 0), (0, 1)]]
+    late = [[(1, 1), (2, 1)], [(0, 2), (1, 2), (2, 2)]]
+    cut = 4 * len(late[0])
+
     side = zh.reshape(1).astype(jnp.int32)
-    zero = arrange(side, parts, 0, True)
+    zero = arrange(side, parts, early, True)
     zero, side = fence((zero, side))
     zero = tuple(move(*zero))
-    (one,) = arrange(side, parts, 1, False)
-    one, side = fence((spread(one), side))
-    (two,) = arrange(side, parts, 2, False)
-    two = spread(two)
-    one, two = tuple(fence((one[:, 0], one[:, 1]))), tuple(fence((two[:, 0], two[:, 1])))
-    zero, one, weights = fence((zero, one, settle(weights, zero + one, 6.0)))
+    (rest,) = arrange(side, parts, late, False)
+    rest = spread(rest)
+    zero, rest, weights = fence((zero, rest, settle(weights, zero, 50.0)))
+    one, two = (rest[:, 0, :cut], rest[:, 1, :cut]), (rest[:, 0, cut:], rest[:, 1, cut:])
     one = tuple(move(*one))
-    zero, two = fence((jnp.stack(zero, 1), two))
-    zero = spread(zero)
-    one, two, weights = fence((one, two, settle(weights, one + two, 6.0)))
-    two = move(*two)
-    partial = work(one, partial, weights)
-    partial = work([zero], partial, weights)
+    two = tuple(move(*two))
+    zero = spread(jnp.stack(zero, 1))
+    one, zero, weights = fence((one, zero, settle(weights, one, 50.0)))
+    partial, sigma = work([zero], partial, weights, spilled=True)
+    (partial,) = work(one, partial, weights, older=(zero, sigma))
     partial, two = fence((partial, two))
-    partial = work(two, partial, weights)
-
+    (partial,) = work(two, partial, weights)
     blocks = partial.reshape(PLANE, 2, PAIRS, LANES)
     owned = jnp.sum(spread(blocks), axis=0)
     share = LANES // 8

time: 165 us -> 158 us (0.958)
  starting transfers between devices: 31 us -> 26.1 us
  Pallas kernels: 30.7 us -> 27.3 us
  local copies, waits for them, and re-layouts: 8.64 us -> 6.04 us
  waiting for transfers between devices: 65 us -> 67.3 us
    ppermute x3, waiting for transfers between devices: 8.97 us -> 45.4 us  [move(): lax.ppermute(falling, ('zh', 'zl'), shifted(-2))]
    all_to_all x3 -> x2, waiting for transfers between devices: 21 us -> 1.24 us  [spread(): return lax.all_to_all(value, ('y', 'x'), split_axis=0, concat_axis=0)]
    ppermute x3, waiting for transfers between devices: 35 us -> 20.6 us  [move(): lax.ppermute(rising, ('zh', 'zl'), shifted(2))]
    all_to_all x3 -> x2, starting transfers between devices: 17.7 us -> 13 us  [spread(): return lax.all_to_all(value, ('y', 'x'), split_axis=0, concat_axis=0)]
    pallas_call x6 -> x5, Pallas kernels: 30.7 us -> 27.3 us  [the longest x3 20.5 us: collide(): pl.pallas_call(functools.partial(kernel, count, stacked, joined, spilled)...]
    unnamed x14 -> x6, local copies, waits for them, and re-layouts: 2.79 us -> 0.01 us
    ppermute x3, starting transfers between devices: 8.54 us -> 5.78 us  [move(): lax.ppermute(rising, ('zh', 'zl'), shifted(2))]
    ppermute x3, starting transfers between devices: 4.8 us -> 7.27 us  [move(): lax.ppermute(falling, ('zh', 'zl'), shifted(-2))]
  transfers between devices with their start and end apart: 9 -> 8, of which waited for: 6 -> 5; matrix products, arithmetic and copies ran while one was open for 4% -> 3% of each run, Pallas kernels for 11% -> 10%
where the time goes in v5:
time: 158 us; the launch traced here: 157 us
  waiting for transfers between devices  67.3 us (43%)
  blocking collectives  28 us (18%)
  Pallas kernels  27.3 us (17%)
  starting transfers between devices  26.1 us (17%)
  local copies, waits for them, and re-layouts  6.04 us (4%)
  other arithmetic  1.74 us (1%)
    ppermute x3, waiting for transfers between devices, move(): lax.ppermute(falling, ('zh', 'zl'), shifted(-2))  45.4 us
    ppermute x3, waiting for transfers between devices, move(): lax.ppermute(rising, ('zh', 'zl'), shifted(2))  20.6 us
    pallas_call x3, Pallas kernels, collide(): pl.pallas_call(functools.partial(kernel, count, stacked, joined, spilled)...  20.5 us
    all_to_all x1, blocking collectives, per_device(): lax.all_to_all(shares, ('zh', 'zl', 'core'), split_axis=0, concat_axis=0)  15.8 us
    all_to_all x2, starting transfers between devices, spread(): return lax.all_to_all(value, ('y', 'x'), split_axis=0, concat_axis=0)  13 us
    all_to_all x1, blocking collectives, spread(): return lax.all_to_all(value, ('y', 'x'), split_axis=0, concat_axis=0)  12.2 us
    ppermute x3, starting transfers between devices, move(): lax.ppermute(falling, ('zh', 'zl'), shifted(-2))  7.27 us
    pallas_call x2, Pallas kernels, arrange(): pl.pallas_call(functools.partial(arrange_kernel, blocks, apart), out_shap...  6.77 us
  transfers between devices with their start and end apart: 8, of which 5 were waited for; matrix products, arithmetic and copies ran while one was open for 3% of the time, Pallas kernels for 10%

profile of v5, /device:TPU:1, one launch (start us, length us, event | category | flops | bytes accessed | tf_op | source)
XLA Modules:
  0.0 157.2 jit_solution(14167151528481933997)
XLA Ops:
  0.0 3.2 %shard_map.55 = (f32[16,16,8,128]{3,2,1,0:T(8,128)}, f32[16,16,8,128]{3,2,1,0:T(8,128)}) custom-call(s32[1]{0:T(128)} %bitcast.1.first, f32[12,3,2,16,8,128]{5,4,3,2,1,0:T(8,128)} %bitcast.45), custom_call_target="tpu_custom_call" | custom-call | bytes 3200000 | tf_op jit(solution)/shard_map/pallas_call | solution.py:250
  3.2 3.9 %collective-permute-start = (f32[16,16,8,128]{3,2,1,0:T(8,128)}, f32[16,16,8,128]{3,2,1,0:T(8,128)S(1)}, u32[]{:S(2)}, u32[]{:S(2)}) collective-permute-start(f32[16,16,8,128]{3,2,1,0:T(8,128)} %get-tuple-element.25), channel_id=1, source_target_pairs={{0,4},{2,6},{4,32},{6,34},{32,36},{34,38},{36,0},{38,2},{1,5},{3,7... | collective-permute-start | bytes 3145736 | tf_op jit(solution)/shard_map/ppermute | solution.py:301
  7.1 3.1 %collective-permute-start.1 = (f32[16,16,8,128]{3,2,1,0:T(8,128)}, f32[16,16,8,128]{3,2,1,0:T(8,128)S(1)}, u32[]{:S(2)}, u32[]{:S(2)}) collective-permute-start(f32[16,16,8,128]{3,2,1,0:T(8,128)} %get-tuple-element.26), channel_id=1, source_target_pairs={{0,36},{2,38},{4,0},{6,2},{32,4},{34,6},{36,32},{38,34},{1,37},{3,... | collective-permute-start | bytes 3145736 | tf_op jit(solution)/shard_map/ppermute | solution.py:302
  10.2 3.6 %shard_map.56 = f32[16,2,20,8,128]{4,3,2,1,0:T(8,128)} custom-call(s32[1]{0:T(128)} %bitcast.1.first, f32[12,3,2,16,8,128]{5,4,3,2,1,0:T(8,128)} %bitcast.46), custom_call_target="tpu_custom_call" | custom-call | bytes 3200000 | tf_op jit(solution)/shard_map/pallas_call | solution.py:250
  13.8 6.8 %all-to-all-start = ((f32[16,2,20,8,128]{4,3,2,1,0:T(8,128)}), f32[16,2,20,8,128]{4,3,2,1,0:T(8,128)}, u32[]{:S(2)}, u32[]{:S(2)}) async-start(f32[16,2,20,8,128]{4,3,2,1,0:T(8,128)} %shard_map.56), calls=%async_computation | async-start | bytes 5242880 | tf_op jit(solution)/shard_map/all_to_all | solution.py:297
  21.3 20.6 %collective-permute-done.refs_0_ = f32[16,16,8,128]{3,2,1,0:T(8,128)S(1)} collective-permute-done((f32[16,16,8,128]{3,2,1,0:T(8,128)}, f32[16,16,8,128]{3,2,1,0:T(8,128)S(1)}, u32[]{:S(2)}, u32[]{:S(2)}) %collective-permute-start) | collective-permute-done | bytes 1048608 | tf_op jit(solution)/shard_map/ppermute | solution.py:301
  41.9 15.2 %collective-permute-done.1.refs_1_ = f32[16,16,8,128]{3,2,1,0:T(8,128)S(1)} collective-permute-done((f32[16,16,8,128]{3,2,1,0:T(8,128)}, f32[16,16,8,128]{3,2,1,0:T(8,128)S(1)}, u32[]{:S(2)}, u32[]{:S(2)}) %collective-permute-start.1) | collective-permute-done | bytes 1048608 | tf_op jit(solution)/shard_map/ppermute | solution.py:302
  57.1 0.1 broadcast_in_dim.19.given
  57.2 1.2 all-to-all-done
  58.4 2.3 %slice_bitcast_fusion.2 = (f32[16,8,8,128]{3,2,1,0:T(8,128)}, f32[16,8,8,128]{3,2,1,0:T(8,128)}) fusion(f32[16,2,20,8,128]{4,3,2,1,0:T(8,128)} %all-to-all-done), kind=kLoop, calls=%fused_computation.3 | loop fusion | bytes 2097152 | tf_op jit(solution)/shard_map/squeeze | solution.py:322
  60.7 1.3 collective-permute-start.3
  62.0 1.1 collective-permute-start.2
  63.1 1.5 pad_maximum_fusion
  64.7 6.2 %all-to-all-start.1 = ((f32[16,2,16,8,128]{4,3,2,1,0:T(8,128)}), f32[16,2,16,8,128]{4,3,2,1,0:T(8,128)S(1)}, u32[]{:S(2)}, u32[]{:S(2)}) async-start(f32[16,2,16,8,128]{4,3,2,1,0:T(8,128)} %pad_maximum_fusion), calls=%async_computation.1 | async-start | bytes 4194304 | tf_op jit(solution)/shard_map/all_to_all | solution.py:297
  70.9 2.6 %slice_bitcast_fusion = (f32[16,12,8,128]{3,2,1,0:T(8,128)}, f32[16,12,8,128]{3,2,1,0:T(8,128)}) fusion(f32[16,2,20,8,128]{4,3,2,1,0:T(8,128)} %all-to-all-done), kind=kLoop, calls=%fused_computation.1 | loop fusion | bytes 3145728 | tf_op jit(solution)/shard_map/squeeze | solution.py:322
  73.5 2.9 %collective-permute-start.5 = (f32[16,12,8,128]{3,2,1,0:T(8,128)}, f32[16,12,8,128]{3,2,1,0:T(8,128)}, u32[]{:S(2)}, u32[]{:S(2)}) collective-permute-start(f32[16,12,8,128]{3,2,1,0:T(8,128)} %get-tuple-element.41), channel_id=1, source_target_pairs={{0,36},{2,38},{4,0},{6,2},{32,4},{34,6},{36,32},{38,34},{1,37},{3,... | collective-permute-start | bytes 2359304 | tf_op jit(solution)/shard_map/ppermute | solution.py:302
  76.4 0.0 copy-start
  76.4 0.0 copy-start.1
  76.4 0.0 copy-start.2
  76.4 0.8 collective-permute-start.4
  77.2 24.9 %collective-permute-done.3.refs_1_ = f32[16,8,8,128]{3,2,1,0:T(8,128)S(1)} collective-permute-done((f32[16,8,8,128]{3,2,1,0:T(8,128)}, f32[16,8,8,128]{3,2,1,0:T(8,128)S(1)}, u32[]{:S(2)}, u32[]{:S(2)}) %collective-permute-start.3) | collective-permute-done | bytes 524320 | tf_op jit(solution)/shard_map/ppermute | solution.py:302
  102.0 0.0 collective-permute-done.2.refs_0_
  102.0 0.0 all-to-all-done.1.refs_0_.refs_2_
  102.1 0.0 copy-done
  102.1 0.0 copy-done.1
  102.1 0.0 copy-done.2
  102.1 7.5 %shard_map.59 = (f32[32,9,128]{2,1,0:T(8,128)S(1)}, f32[32,16,256]{2,1,0:T(8,128)S(1)}) custom-call(s32[1]{0:T(128)} %bitcast.turn, f32[16,2,16,8,128]{4,3,2,1,0:T(8,128)S(1)} %all-to-all-done.1.refs_0_.refs_2_, f32[8,128]{1,0:T(8,128)S(1)} %shard_map.58.refs_1_.refs_4_.refs_2_, bf16[256,256]{1,0:T(8,128)(2,1)S(1)} %copy-done.1, ...), custom_call_target="tpu_custom_call" | custom-call | flops 1000000000 | tf_op jit(solution)/shard_map/pallas_call | solution.py:215
  109.6 5.2 %shard_map.60.refs_6_ = f32[32,9,128]{2,1,0:T(8,128)S(1)} custom-call(s32[1]{0:T(128)} %bitcast.turn, f32[16,8,8,128]{3,2,1,0:T(8,128)S(1)} %collective-permute-done.2.refs_0_, f32[16,8,8,128]{3,2,1,0:T(8,128)S(1)} %collective-permute-done.3.refs_1_, f32[16,2,16,8,128]{4,3,2,1,0:T(8,128)S(1)} %all-to-all-done.1.refs_0_.refs_2_, ...), custom_call_target="tpu_custom_call" | custom-call | flops 1000000000 | tf_op jit(solution)/shard_map/pallas_call | solution.py:215
  114.8 5.4 %collective-permute-done.5.refs_1_ = f32[16,12,8,128]{3,2,1,0:T(8,128)} collective-permute-done((f32[16,12,8,128]{3,2,1,0:T(8,128)}, f32[16,12,8,128]{3,2,1,0:T(8,128)}, u32[]{:S(2)}, u32[]{:S(2)}) %collective-permute-start.5) | collective-permute-done | bytes 786464 | tf_op jit(solution)/shard_map/ppermute | solution.py:302
  120.2 0.0 collective-permute-done.4.refs_0_
  120.2 7.8 %shard_map.61 = f32[32,9,128]{2,1,0:T(8,128)S(1)} custom-call(s32[1]{0:T(128)} %bitcast.turn, f32[16,12,8,128]{3,2,1,0:T(8,128)} %collective-permute-done.4.refs_0_, f32[16,12,8,128]{3,2,1,0:T(8,128)} %collective-permute-done.5.refs_1_, f32[8,128]{1,0:T(8,128)S(1)} %shard_map.58.refs_1_.refs_4_.refs_2_, bf16[256,256]{1,0:T(8,128)(2,1)S(1)} %copy-done.1, ...), custom_call_target="tpu_custom_call" | custom-call | flops 1000000000 | tf_op jit(solution)/shard_map/pallas_call | solution.py:215
  128.0 0.1 copy.15
  128.1 12.2 %all_to_all.20 = f32[16,2,9,128]{3,1,2,0:T(2,128)S(1)} all-to-all(f32[16,2,9,128]{3,1,2,0:T(2,128)S(1)} %copy.15), channel_id=1, replica_groups=mesh['y'=4,'zh'=2,'x'=4,'zl'=4,'core'=2] {'y','x'}, dimensions={0} | all-to-all | bytes 294912 | tf_op jit(solution)/shard_map/all_to_all | solution.py:297
  140.3 0.1 reduce_sum.18
  140.4 0.1 reshape.72
  140.5 0.1 reshape.75
  140.6 15.8 %all_to_all.21 = f32[16,1,144]{2,1,0:T(1,128)S(1)} all-to-all(f32[16,1,144]{2,1,0:T(1,128)S(1)} %reshape.75), channel_id=1, replica_groups=mesh['y'=4,'zh'=2,'x'=4,'zl'=4,'core'=2] {'zh','zl','core'}, dimensions={0} | all-to-all | bytes 18432 | tf_op jit(solution)/shard_map/all_to_all | solution.py:335
  156.4 0.1 negate_bitcast_fusion
  156.5 0.1 stack.18
  156.6 0.6 copy.20
  (8 shorter events, 0.1 us)
Async XLA Ops:
  3.2 38.7 %collective-permute-start = (f32[16,16,8,128]{3,2,1,0:T(8,128)}, f32[16,16,8,128]{3,2,1,0:T(8,128)S(1)}, u32[]{:S(2)}, u32[]{:S(2)}) collective-permute-start(f32[16,16,8,128]{3,2,1,0:T(8,128)} %get-tuple-element.25), channel_id=1, source_target_pairs={{0,4},{2,6},{4,32},{6,34},{32,36},{34,38},{36,0},{38,2},{1,5},{3,7... | collective-permute-start | bytes 3145736 | tf_op jit(solution)/shard_map/ppermute | solution.py:301
  7.1 50.0 %collective-permute-start.1 = (f32[16,16,8,128]{3,2,1,0:T(8,128)}, f32[16,16,8,128]{3,2,1,0:T(8,128)S(1)}, u32[]{:S(2)}, u32[]{:S(2)}) collective-permute-start(f32[16,16,8,128]{3,2,1,0:T(8,128)} %get-tuple-element.26), channel_id=1, source_target_pairs={{0,36},{2,38},{4,0},{6,2},{32,4},{34,6},{36,32},{38,34},{1,37},{3,... | collective-permute-start | bytes 3145736 | tf_op jit(solution)/shard_map/ppermute | solution.py:302
  13.8 44.6 %all-to-all-start = ((f32[16,2,20,8,128]{4,3,2,1,0:T(8,128)}), f32[16,2,20,8,128]{4,3,2,1,0:T(8,128)}, u32[]{:S(2)}, u32[]{:S(2)}) async-start(f32[16,2,20,8,128]{4,3,2,1,0:T(8,128)} %shard_map.56), calls=%async_computation | async-start | bytes 5242880 | tf_op jit(solution)/shard_map/all_to_all | solution.py:297
  60.7 41.3 %collective-permute-start.3 = (f32[16,8,8,128]{3,2,1,0:T(8,128)}, f32[16,8,8,128]{3,2,1,0:T(8,128)S(1)}, u32[]{:S(2)}, u32[]{:S(2)}) collective-permute-start(f32[16,8,8,128]{3,2,1,0:T(8,128)} %get-tuple-element.43), channel_id=1, source_target_pairs={{0,36},{2,38},{4,0},{6,2},{32,4},{34,6},{36,32},{38,34},{1,37},{3,... | collective-permute-start | bytes 1572872 | tf_op jit(solution)/shard_map/ppermute | solution.py:302
  62.0 40.0 %collective-permute-start.2 = (f32[16,8,8,128]{3,2,1,0:T(8,128)}, f32[16,8,8,128]{3,2,1,0:T(8,128)S(1)}, u32[]{:S(2)}, u32[]{:S(2)}) collective-permute-start(f32[16,8,8,128]{3,2,1,0:T(8,128)} %get-tuple-element.44), channel_id=1, source_target_pairs={{0,4},{2,6},{4,32},{6,34},{32,36},{34,38},{36,0},{38,2},{1,5},{3,7... | collective-permute-start | bytes 1572872 | tf_op jit(solution)/shard_map/ppermute | solution.py:301
  64.7 37.4 %all-to-all-start.1 = ((f32[16,2,16,8,128]{4,3,2,1,0:T(8,128)}), f32[16,2,16,8,128]{4,3,2,1,0:T(8,128)S(1)}, u32[]{:S(2)}, u32[]{:S(2)}) async-start(f32[16,2,16,8,128]{4,3,2,1,0:T(8,128)} %pad_maximum_fusion), calls=%async_computation.1 | async-start | bytes 4194304 | tf_op jit(solution)/shard_map/all_to_all | solution.py:297
  73.5 46.7 %collective-permute-start.5 = (f32[16,12,8,128]{3,2,1,0:T(8,128)}, f32[16,12,8,128]{3,2,1,0:T(8,128)}, u32[]{:S(2)}, u32[]{:S(2)}) collective-permute-start(f32[16,12,8,128]{3,2,1,0:T(8,128)} %get-tuple-element.41), channel_id=1, source_target_pairs={{0,36},{2,38},{4,0},{6,2},{32,4},{34,6},{36,32},{38,34},{1,37},{3,... | collective-permute-start | bytes 2359304 | tf_op jit(solution)/shard_map/ppermute | solution.py:302
  76.4 25.7 %copy-start = (bf16[256,256]{1,0:T(8,128)(2,1)S(1)}, bf16[256,256]{1,0:T(8,128)(2,1)}, u32[]{:S(2)}) copy-start(bf16[256,256]{1,0:T(8,128)(2,1)} %constant.103.clone.refs_3_.refs_6_.refs_4_) | copy-start | bytes 393220
  76.4 25.7 %copy-start.1 = (bf16[256,256]{1,0:T(8,128)(2,1)S(1)}, bf16[256,256]{1,0:T(8,128)(2,1)}, u32[]{:S(2)}) copy-start(bf16[256,256]{1,0:T(8,128)(2,1)} %constant.102.clone.refs_2_.refs_5_.refs_3_) | copy-start | bytes 393220
  76.4 25.7 %copy-start.2 = (f32[32,2,128]{2,1,0:T(2,128)S(1)}, f32[32,2,128]{2,1,0:T(2,128)}, u32[]{:S(2)}) copy-start(f32[32,2,128]{2,1,0:T(2,128)} %constant.104.clone.refs_4_.refs_7_.refs_5_) | copy-start | bytes 98308
  76.4 43.8 %collective-permute-start.4 = (f32[16,12,8,128]{3,2,1,0:T(8,128)}, f32[16,12,8,128]{3,2,1,0:T(8,128)}, u32[]{:S(2)}, u32[]{:S(2)}) collective-permute-start(f32[16,12,8,128]{3,2,1,0:T(8,128)} %get-tuple-element.42), channel_id=1, source_target_pairs={{0,4},{2,6},{4,32},{6,34},{32,36},{34,38},{36,0},{38,2},{1,5},{3,7... | collective-permute-start | bytes 2359304 | tf_op jit(solution)/shard_map/ppermute | solution.py:301

commit v6 on v5

--- a/solution.py
+++ b/solution.py
@@ -97,26 +97,26 @@
     return dot(head, high) + (dot(tail, high) + dot(head, low))
 
 
-def kernel(count, stacked, joined, spilled, turn, *refs):
-    refs = list(refs)
-    if stacked:
-        whole = refs.pop(0)
-        lower, upper = whole.at[:, 0], whole.at[:, 1]
-    else:
-        lower, upper = refs.pop(0), refs.pop(0)
+def kernel(count, joined, spill, turn, *refs):
+    *refs, field, green, sems = refs
+    fields = [refs.pop(0)] if refs[0].ndim == 5 else [refs.pop(0), refs.pop(0)]
     if joined:
-        older, older_sigma = refs.pop(0), refs.pop(0)
-    weight, high_ref, low_ref, twiddle, before, out = refs[:6]
-    field = refs[-1]
-    straight = turn[0] == 0
-
-    def choose(one, two, m, at):
-        plane, half = m // 8 * 4 + m % 4, m // 4 % 2
-        return jnp.where(straight == (half == 0), one[plane, at], two[plane, at])
-
-    def pair_of(one, two, pairs, m, comp, pair):
-        at = comp * 2 * pairs + pair
-        return choose(one, two, m, at), choose(one, two, m, at + pairs)
+        older_green, older_sigma = refs.pop(0), refs.pop(0)
+    weight, high_ref, low_ref, twiddle, before, out, *spilled = refs
+
+    def fetch(n, at):
+        source = fields[n].at[:, at] if len(fields) == 2 else fields[0].at[:, n, at]
+        half = turn[0] if n == 0 else 1 - turn[0]
+        return pltpu.make_async_copy(source, green.at[half, :, at], sems.at[n, at])
+
+    kinds = [(comp, pair, part) for comp in range(2) for pair in range(count) for part in range(2)]
+    for comp, pair, part in kinds:
+        for n in range(2):
+            fetch(n, (2 * comp + part) * count + pair).start()
+
+    def pair_of(source, pairs, m, comp, pair):
+        plane, half, at = m // 8 * 4 + m % 4, m // 4 % 2, comp * 2 * pairs + pair
+        return source[half, plane, at], source[half, plane, at + pairs]
 
     def spot(part):
         return pl.ds(part * LANES, LANES)
@@ -131,7 +131,10 @@
     def _(s):
         comp, pair = s // count, s % count
         rows = pl.ds(pl.multiple_of(comp * SLOTS, SLOTS), SLOTS)
-        values = [pair_of(lower, upper, count, m, comp, pair) for m in range(ROWS)]
+        for part in range(2):
+            for n in range(2):
+                fetch(n, (2 * comp + part) * count + pair).wait()
+        values = [pair_of(green, count, m, comp, pair) for m in range(ROWS)]
         for n, value in enumerate(fourier(values)):
             real, imag = times(value, twist(n)) if n else value
             field[n, pair, rows, spot(0)] = real
@@ -182,8 +185,8 @@
 
         def given(comp, b):
             if joined and b == 0:
-                return pair_of(older.at[:, 0], older.at[:, 1], ORB + 1, m, comp, ORB)
-            return pair_of(lower, upper, count, m, comp, b - joined)
+                return pair_of(older_green, 1, m, comp, 0)
+            return pair_of(green, count, m, comp, b - joined)
 
         def memory(a, b):
             left, right = sigma(0, a), given(1, b)
@@ -202,26 +205,34 @@
             spare, row = (m // 8 * 4 + m % 4) * 2 + m // 4 % 2, pl.ds(i, 1)
             out[spare, row, :] = before[spare, row, :] + jnp.sum(result * scale, axis=0, keepdims=True)
         if spilled:
-            refs[6][m] = field[m, ORB]
-
-
-def collide(turn, fields, weights, high, low, twiddle, before, older=(), spilled=False):
-    stacked, joined = len(fields) == 1, int(len(older) > 0)
-    count = ORB + 1 if stacked else ORB - joined
-    shapes = [jax.ShapeDtypeStruct((ROWS, PAIRS, LANES), jnp.float32)]
+            spilled[1][m] = field[m, spill]
+
     if spilled:
-        shapes.append(jax.ShapeDtypeStruct((ROWS, 2 * SLOTS, 2 * LANES), jnp.float32))
-    inputs = (*fields, *older, weights, high, low, twiddle, before)
+        for kind in range(4):
+            spilled[0][:, :, kind] = green[:, :, kind * count + spill]
+
+
+def collide(turn, fields, weights, high, low, twiddle, before, older=(), spill=None):
+    count = fields[0].shape[-3] // 4
+    shapes = [(ROWS, PAIRS, LANES)]
+    if spill is not None:
+        shapes += [(2, PLANE, 4, SLOTS, LANES), (ROWS, 2 * SLOTS, 2 * LANES)]
+    inputs = (*older, weights, high, low, twiddle, before)
     return pl.pallas_call(
-        functools.partial(kernel, count, stacked, joined, spilled),
-        out_shape=shapes,
+        functools.partial(kernel, count, int(len(older) > 0), spill),
+        out_shape=[jax.ShapeDtypeStruct(shape, jnp.float32) for shape in shapes],
         in_specs=[pl.BlockSpec(memory_space=pltpu.SMEM)]
+        + [pl.BlockSpec(memory_space=pl.ANY)] * len(fields)
         + [pl.BlockSpec(memory_space=pltpu.VMEM)] * len(inputs),
         out_specs=[pl.BlockSpec(memory_space=pltpu.VMEM)] * len(shapes),
-        scratch_shapes=[pltpu.VMEM((ROWS, count, 2 * SLOTS, 2 * LANES), jnp.float32)],
+        scratch_shapes=[
+            pltpu.VMEM((ROWS, count, 2 * SLOTS, 2 * LANES), jnp.float32),
+            pltpu.VMEM((2, PLANE, 4 * count, SLOTS, LANES), jnp.float32),
+            pltpu.SemaphoreType.DMA((2, 4 * count)),
+        ],
         compiler_params=pltpu.CompilerParams(vmem_limit_bytes=24 * 1024 * 1024),
         cost_estimate=pl.CostEstimate(flops=1000000000, bytes_accessed=0, transcendentals=0),
-    )(turn, *inputs)
+    )(turn, *fields, *inputs)
 
 
 def arrange_kernel(blocks, apart, first, parts, *refs):
@@ -253,7 +264,7 @@
         in_specs=[pl.BlockSpec(memory_space=pltpu.SMEM), pl.BlockSpec(memory_space=pl.ANY)],
         out_specs=[pl.BlockSpec(memory_space=pltpu.VMEM)] * (2 if apart else 1),
         scratch_shapes=[pltpu.SemaphoreType.DMA((2, count))],
-        compiler_params=pltpu.CompilerParams(vmem_limit_bytes=60 * 1024 * 1024),
+        compiler_params=pltpu.CompilerParams(vmem_limit_bytes=(57 if apart else 60) * 1024 * 1024),
         cost_estimate=pl.CostEstimate(flops=0, bytes_accessed=3_200_000, transcendentals=0),
     )(first, parts)
 
@@ -309,7 +320,7 @@
     partial = jnp.zeros((ROWS, PAIRS, LANES), jnp.float32)
     fence = lax.optimization_barrier
     early = [[(0, 0), (1, 0), (2, 0), (0, 1)]]
-    late = [[(1, 1), (2, 1)], [(0, 2), (1, 2), (2, 2)]]
+    late = [[(1, 1), (2, 1), (0, 2)], [(1, 2), (2, 2)]]
     cut = 4 * len(late[0])
 
     side = zh.reshape(1).astype(jnp.int32)
@@ -324,10 +335,10 @@
     two = tuple(move(*two))
     zero = spread(jnp.stack(zero, 1))
     one, zero, weights = fence((one, zero, settle(weights, one, 50.0)))
-    partial, sigma = work([zero], partial, weights, spilled=True)
-    (partial,) = work(one, partial, weights, older=(zero, sigma))
+    partial, *older = work([zero], partial, weights, spill=ORB)
+    partial, *older = work(one, partial, weights, older=older, spill=ORB - 1)
     partial, two = fence((partial, two))
-    (partial,) = work(two, partial, weights)
+    (partial,) = work(two, partial, weights, older=older)
     blocks = partial.reshape(PLANE, 2, PAIRS, LANES)
     owned = jnp.sum(spread(blocks), axis=0)
     share = LANES // 8

time: 158 us -> 163 us (1.032)
  waiting for transfers between devices: 67.3 us -> 69.4 us
  local copies, waits for them, and re-layouts: 6.04 us -> 7.76 us
    all_to_all x1, blocking collectives: 12.2 us -> 14.7 us  [spread(): return lax.all_to_all(value, ('y', 'x'), split_axis=0, concat_axis=0)]
    all_to_all x1, blocking collectives: 15.8 us -> 13.3 us  [per_device(): lax.all_to_all(shares, ('zh', 'zl', 'core'), split_axis=0, concat_axis=0)]
    ppermute x3, waiting for transfers between devices: 45.4 us -> 47.5 us  [move(): lax.ppermute(falling, ('zh', 'zl'), shifted(-2))]
    unnamed x6 -> x10, local copies, waits for them, and re-layouts: 0.01 us -> 1.7 us
  transfers between devices with their start and end apart: 8 -> 8, of which waited for: 5 -> 4; matrix products, arithmetic and copies ran while one was open for 3% -> 2% of each run, Pallas kernels for 10% -> 12%
where the time goes in v6:
time: 163 us; the launch traced here: 162 us
  waiting for transfers between devices  69.4 us (43%)
  Pallas kernels  28.2 us (17%)
  blocking collectives  28.1 us (17%)
  starting transfers between devices  26 us (16%)
  local copies, waits for them, and re-layouts  7.76 us (5%)
  other arithmetic  1.68 us (1%)
    ppermute x3, waiting for transfers between devices, move(): lax.ppermute(falling, ('zh', 'zl'), shifted(-2))  47.5 us
    pallas_call x3, Pallas kernels, collide(): pl.pallas_call(functools.partial(kernel, count, int(len(older) > 0), spil...  21.4 us
    ppermute x3, waiting for transfers between devices, move(): lax.ppermute(rising, ('zh', 'zl'), shifted(2))  20.6 us
    all_to_all x1, blocking collectives, spread(): return lax.all_to_all(value, ('y', 'x'), split_axis=0, concat_axis=0)  14.7 us
    all_to_all x1, blocking collectives, per_device(): lax.all_to_all(shares, ('zh', 'zl', 'core'), split_axis=0, concat_axis=0)  13.3 us
    all_to_all x2, starting transfers between devices, spread(): return lax.all_to_all(value, ('y', 'x'), split_axis=0, concat_axis=0)  13 us
    ppermute x3, starting transfers between devices, move(): lax.ppermute(falling, ('zh', 'zl'), shifted(-2))  7.27 us
    pallas_call x2, Pallas kernels, arrange(): pl.pallas_call(functools.partial(arrange_kernel, blocks, apart), out_shap...  6.77 us
  transfers between devices with their start and end apart: 8, of which 4 were waited for; matrix products, arithmetic and copies ran while one was open for 2% of the time, Pallas kernels for 12%

profile of v6, /device:TPU:1, one launch (start us, length us, event | category | flops | bytes accessed | tf_op | source)
XLA Modules:
  0.0 161.8 jit_solution(9794113100803010107)
XLA Ops:
  0.0 3.2 %shard_map.55 = (f32[16,16,8,128]{3,2,1,0:T(8,128)}, f32[16,16,8,128]{3,2,1,0:T(8,128)}) custom-call(s32[1]{0:T(128)} %bitcast.1.first, f32[12,3,2,16,8,128]{5,4,3,2,1,0:T(8,128)} %bitcast.45), custom_call_target="tpu_custom_call" | custom-call | bytes 3200000 | tf_op jit(solution)/shard_map/pallas_call | solution.py:261
  3.2 3.9 %collective-permute-start = (f32[16,16,8,128]{3,2,1,0:T(8,128)}, f32[16,16,8,128]{3,2,1,0:T(8,128)S(1)}, u32[]{:S(2)}, u32[]{:S(2)}) collective-permute-start(f32[16,16,8,128]{3,2,1,0:T(8,128)} %get-tuple-element.29), channel_id=1, source_target_pairs={{0,4},{2,6},{4,32},{6,34},{32,36},{34,38},{36,0},{38,2},{1,5},{3,7... | collective-permute-start | bytes 3145736 | tf_op jit(solution)/shard_map/ppermute | solution.py:312
  7.1 3.1 %collective-permute-start.1 = (f32[16,16,8,128]{3,2,1,0:T(8,128)}, f32[16,16,8,128]{3,2,1,0:T(8,128)S(1)}, u32[]{:S(2)}, u32[]{:S(2)}) collective-permute-start(f32[16,16,8,128]{3,2,1,0:T(8,128)} %get-tuple-element.30), channel_id=1, source_target_pairs={{0,36},{2,38},{4,0},{6,2},{32,4},{34,6},{36,32},{38,34},{1,37},{3,... | collective-permute-start | bytes 3145736 | tf_op jit(solution)/shard_map/ppermute | solution.py:313
  10.2 3.6 %shard_map.56 = f32[16,2,20,8,128]{4,3,2,1,0:T(8,128)} custom-call(s32[1]{0:T(128)} %bitcast.1.first, f32[12,3,2,16,8,128]{5,4,3,2,1,0:T(8,128)} %bitcast.46), custom_call_target="tpu_custom_call" | custom-call | bytes 3200000 | tf_op jit(solution)/shard_map/pallas_call | solution.py:261
  13.8 6.8 %all-to-all-start = ((f32[16,2,20,8,128]{4,3,2,1,0:T(8,128)}), f32[16,2,20,8,128]{4,3,2,1,0:T(8,128)}, u32[]{:S(2)}, u32[]{:S(2)}) async-start(f32[16,2,20,8,128]{4,3,2,1,0:T(8,128)} %shard_map.56), calls=%async_computation | async-start | bytes 5242880 | tf_op jit(solution)/shard_map/all_to_all | solution.py:308
  21.3 20.6 %collective-permute-done.refs_0_ = f32[16,16,8,128]{3,2,1,0:T(8,128)S(1)} collective-permute-done((f32[16,16,8,128]{3,2,1,0:T(8,128)}, f32[16,16,8,128]{3,2,1,0:T(8,128)S(1)}, u32[]{:S(2)}, u32[]{:S(2)}) %collective-permute-start) | collective-permute-done | bytes 1048608 | tf_op jit(solution)/shard_map/ppermute | solution.py:312
  41.9 15.2 %collective-permute-done.1.refs_1_ = f32[16,16,8,128]{3,2,1,0:T(8,128)S(1)} collective-permute-done((f32[16,16,8,128]{3,2,1,0:T(8,128)}, f32[16,16,8,128]{3,2,1,0:T(8,128)S(1)}, u32[]{:S(2)}, u32[]{:S(2)}) %collective-permute-start.1) | collective-permute-done | bytes 1048608 | tf_op jit(solution)/shard_map/ppermute | solution.py:313
  57.1 0.1 broadcast_in_dim.19.given
  57.2 1.2 all-to-all-done
  58.4 2.7 %slice_bitcast_fusion = (f32[16,12,8,128]{3,2,1,0:T(8,128)}, f32[16,12,8,128]{3,2,1,0:T(8,128)}) fusion(f32[16,2,20,8,128]{4,3,2,1,0:T(8,128)} %all-to-all-done), kind=kLoop, calls=%fused_computation.1 | loop fusion | bytes 3145728 | tf_op jit(solution)/shard_map/squeeze | solution.py:333
  61.1 1.3 collective-permute-start.3
  62.4 1.1 collective-permute-start.2
  63.5 1.5 pad_maximum_fusion
  65.0 6.2 %all-to-all-start.1 = ((f32[16,2,16,8,128]{4,3,2,1,0:T(8,128)}), f32[16,2,16,8,128]{4,3,2,1,0:T(8,128)S(1)}, u32[]{:S(2)}, u32[]{:S(2)}) async-start(f32[16,2,16,8,128]{4,3,2,1,0:T(8,128)} %pad_maximum_fusion), calls=%async_computation.1 | async-start | bytes 4194304 | tf_op jit(solution)/shard_map/all_to_all | solution.py:308
  71.2 2.3 %slice_bitcast_fusion.2 = (f32[16,8,8,128]{3,2,1,0:T(8,128)}, f32[16,8,8,128]{3,2,1,0:T(8,128)}) fusion(f32[16,2,20,8,128]{4,3,2,1,0:T(8,128)} %all-to-all-done), kind=kLoop, calls=%fused_computation.3 | loop fusion | bytes 2097152 | tf_op jit(solution)/shard_map/squeeze | solution.py:333
  73.5 2.9 %collective-permute-start.5 = (f32[16,8,8,128]{3,2,1,0:T(8,128)}, f32[16,8,8,128]{3,2,1,0:T(8,128)S(1)}, u32[]{:S(2)}, u32[]{:S(2)}) collective-permute-start(f32[16,8,8,128]{3,2,1,0:T(8,128)} %get-tuple-element.49), channel_id=1, source_target_pairs={{0,36},{2,38},{4,0},{6,2},{32,4},{34,6},{36,32},{38,34},{1,37},{3,... | collective-permute-start | bytes 1572872 | tf_op jit(solution)/shard_map/ppermute | solution.py:313
  76.4 0.0 copy-start
  76.4 0.7 collective-permute-start.4
  77.0 32.3 %collective-permute-done.3.refs_1_ = f32[16,12,8,128]{3,2,1,0:T(8,128)S(1)} collective-permute-done((f32[16,12,8,128]{3,2,1,0:T(8,128)}, f32[16,12,8,128]{3,2,1,0:T(8,128)S(1)}, u32[]{:S(2)}, u32[]{:S(2)}) %collective-permute-start.3) | collective-permute-done | bytes 786464 | tf_op jit(solution)/shard_map/ppermute | solution.py:313
  109.4 0.0 collective-permute-done.2.refs_0_
  109.4 0.0 all-to-all-done.1.refs_0_
  109.4 0.0 copy-start.2
  109.4 0.0 copy-start.4
  109.4 0.0 copy-done
  109.4 0.0 copy-start.1
  109.4 0.9 copy-done.1
  110.4 0.0 copy-start.3
  110.4 0.8 copy-done.3
  111.1 8.1 %shard_map.59 = (f32[32,9,128]{2,1,0:T(8,128)S(1)}, f32[2,16,4,8,128]{4,3,2,1,0:T(8,128)S(1)}, f32[32,16,256]{2,1,0:T(8,128)S(1)}) custom-call(s32[1]{0:T(128)} %bitcast.turn, f32[16,2,16,8,128]{4,3,2,1,0:T(8,128)S(1)} %all-to-all-done.1.refs_0_, f32[8,128]{1,0:T(8,128)S(1)} %shard_map.58.refs_1_.refs_4_, bf16[256,256]{1,0:T(8,128)(2,1)S(1)} %copy-done.1, ...), custom_call_target="tpu_custom_call" | custom-call | flops 1000000000 | tf_op jit(solution)/shard_map/pallas_call | solution.py:221
  119.3 0.0 copy-done.2
  119.3 0.0 copy-done.4
  119.3 7.4 %shard_map.60 = (f32[32,9,128]{2,1,0:T(8,128)S(1)}, f32[2,16,4,8,128]{4,3,2,1,0:T(8,128)S(1)}, f32[32,16,256]{2,1,0:T(8,128)S(1)}) custom-call(s32[1]{0:T(128)} %bitcast.turn, f32[16,12,8,128]{3,2,1,0:T(8,128)} %collective-permute-done.2.refs_0_, f32[16,12,8,128]{3,2,1,0:T(8,128)S(1)} %collective-permute-done.3.refs_1_, ...), custom_call_target="tpu_custom_call" | custom-call | flops 1000000000 | tf_op jit(solution)/shard_map/pallas_call | solution.py:221
  126.7 0.0 collective-permute-done.5.refs_1_
  126.7 0.0 collective-permute-done.4.refs_0_
  126.7 5.9 %shard_map.61 = f32[32,9,128]{2,1,0:T(8,128)S(1)} custom-call(s32[1]{0:T(128)} %bitcast.turn, f32[16,8,8,128]{3,2,1,0:T(8,128)} %collective-permute-done.4.refs_0_, f32[16,8,8,128]{3,2,1,0:T(8,128)S(1)} %collective-permute-done.5.refs_1_, f32[2,16,4,8,128]{4,3,2,1,0:T(8,128)S(1)} %get-tuple-element.46.refs_2_, f32[32,16,256]{2,1,0:T(8,128)S(1)} %get-tuple-element.47.refs_3_, ...), custom_call_target="tpu_custom_call" | custom-call | flops 1000000000 | tf_op jit(solution)/shard_map/pallas_call | solution.py:221
  132.6 0.1 copy.15
  132.7 14.7 %all_to_all.20 = f32[16,2,9,128]{3,1,2,0:T(2,128)S(1)} all-to-all(f32[16,2,9,128]{3,1,2,0:T(2,128)S(1)} %copy.15), channel_id=1, replica_groups=mesh['y'=4,'zh'=2,'x'=4,'zl'=4,'core'=2] {'y','x'}, dimensions={0} | all-to-all | bytes 294912 | tf_op jit(solution)/shard_map/all_to_all | solution.py:308
  147.4 0.1 reduce_sum.18
  147.4 0.1 reshape.72
  147.6 0.1 reshape.75
  147.7 13.3 %all_to_all.21 = f32[16,1,144]{2,1,0:T(1,128)S(1)} all-to-all(f32[16,1,144]{2,1,0:T(1,128)S(1)} %reshape.75), channel_id=1, replica_groups=mesh['y'=4,'zh'=2,'x'=4,'zl'=4,'core'=2] {'zh','zl','core'}, dimensions={0} | all-to-all | bytes 18432 | tf_op jit(solution)/shard_map/all_to_all | solution.py:346
  161.1 0.1 negate_bitcast_fusion
  161.1 0.1 stack.18
  161.2 0.6 copy.20
  (8 shorter events, 0.1 us)
Async XLA Ops:
  3.2 38.7 %collective-permute-start = (f32[16,16,8,128]{3,2,1,0:T(8,128)}, f32[16,16,8,128]{3,2,1,0:T(8,128)S(1)}, u32[]{:S(2)}, u32[]{:S(2)}) collective-permute-start(f32[16,16,8,128]{3,2,1,0:T(8,128)} %get-tuple-element.29), channel_id=1, source_target_pairs={{0,4},{2,6},{4,32},{6,34},{32,36},{34,38},{36,0},{38,2},{1,5},{3,7... | collective-permute-start | bytes 3145736 | tf_op jit(solution)/shard_map/ppermute | solution.py:312
  7.1 50.0 %collective-permute-start.1 = (f32[16,16,8,128]{3,2,1,0:T(8,128)}, f32[16,16,8,128]{3,2,1,0:T(8,128)S(1)}, u32[]{:S(2)}, u32[]{:S(2)}) collective-permute-start(f32[16,16,8,128]{3,2,1,0:T(8,128)} %get-tuple-element.30), channel_id=1, source_target_pairs={{0,36},{2,38},{4,0},{6,2},{32,4},{34,6},{36,32},{38,34},{1,37},{3,... | collective-permute-start | bytes 3145736 | tf_op jit(solution)/shard_map/ppermute | solution.py:313
  13.8 44.6 %all-to-all-start = ((f32[16,2,20,8,128]{4,3,2,1,0:T(8,128)}), f32[16,2,20,8,128]{4,3,2,1,0:T(8,128)}, u32[]{:S(2)}, u32[]{:S(2)}) async-start(f32[16,2,20,8,128]{4,3,2,1,0:T(8,128)} %shard_map.56), calls=%async_computation | async-start | bytes 5242880 | tf_op jit(solution)/shard_map/all_to_all | solution.py:308
  61.1 48.2 %collective-permute-start.3 = (f32[16,12,8,128]{3,2,1,0:T(8,128)}, f32[16,12,8,128]{3,2,1,0:T(8,128)S(1)}, u32[]{:S(2)}, u32[]{:S(2)}) collective-permute-start(f32[16,12,8,128]{3,2,1,0:T(8,128)} %get-tuple-element.51), channel_id=1, source_target_pairs={{0,36},{2,38},{4,0},{6,2},{32,4},{34,6},{36,32},{38,34},{1,37},{3,... | collective-permute-start | bytes 2359304 | tf_op jit(solution)/shard_map/ppermute | solution.py:313
  62.4 47.0 %collective-permute-start.2 = (f32[16,12,8,128]{3,2,1,0:T(8,128)}, f32[16,12,8,128]{3,2,1,0:T(8,128)}, u32[]{:S(2)}, u32[]{:S(2)}) collective-permute-start(f32[16,12,8,128]{3,2,1,0:T(8,128)} %get-tuple-element.52), channel_id=1, source_target_pairs={{0,4},{2,6},{4,32},{6,34},{32,36},{34,38},{36,0},{38,2},{1,5},{3,7... | collective-permute-start | bytes 2359304 | tf_op jit(solution)/shard_map/ppermute | solution.py:312
  65.0 44.4 %all-to-all-start.1 = ((f32[16,2,16,8,128]{4,3,2,1,0:T(8,128)}), f32[16,2,16,8,128]{4,3,2,1,0:T(8,128)S(1)}, u32[]{:S(2)}, u32[]{:S(2)}) async-start(f32[16,2,16,8,128]{4,3,2,1,0:T(8,128)} %pad_maximum_fusion), calls=%async_computation.1 | async-start | bytes 4194304 | tf_op jit(solution)/shard_map/all_to_all | solution.py:308
  73.5 53.2 %collective-permute-start.5 = (f32[16,8,8,128]{3,2,1,0:T(8,128)}, f32[16,8,8,128]{3,2,1,0:T(8,128)S(1)}, u32[]{:S(2)}, u32[]{:S(2)}) collective-permute-start(f32[16,8,8,128]{3,2,1,0:T(8,128)} %get-tuple-element.49), channel_id=1, source_target_pairs={{0,36},{2,38},{4,0},{6,2},{32,4},{34,6},{36,32},{38,34},{1,37},{3,... | collective-permute-start | bytes 1572872 | tf_op jit(solution)/shard_map/ppermute | solution.py:313
  76.4 33.1 %copy-start = (bf16[256,256]{1,0:T(8,128)(2,1)S(1)}, bf16[256,256]{1,0:T(8,128)(2,1)}, u32[]{:S(2)}) copy-start(bf16[256,256]{1,0:T(8,128)(2,1)} %constant.103.clone.refs_3_.refs_6_) | copy-start | bytes 393220
  76.4 50.3 %collective-permute-start.4 = (f32[16,8,8,128]{3,2,1,0:T(8,128)}, f32[16,8,8,128]{3,2,1,0:T(8,128)}, u32[]{:S(2)}, u32[]{:S(2)}) collective-permute-start(f32[16,8,8,128]{3,2,1,0:T(8,128)} %get-tuple-element.50), channel_id=1, source_target_pairs={{0,4},{2,6},{4,32},{6,34},{32,36},{34,38},{36,0},{38,2},{1,5},{3,7... | collective-permute-start | bytes 1572872 | tf_op jit(solution)/shard_map/ppermute | solution.py:312
  109.4 9.9 %copy-start.2 = (bf16[256,256]{1,0:T(8,128)(2,1)S(1)}, bf16[256,256]{1,0:T(8,128)(2,1)}, u32[]{:S(2)}) copy-start(bf16[256,256]{1,0:T(8,128)(2,1)} %constant.102.clone.refs_2_.refs_5_) | copy-start | bytes 393220
  109.4 9.9 %copy-start.4 = (f32[32,2,128]{2,1,0:T(2,128)S(1)}, f32[32,2,128]{2,1,0:T(2,128)}, u32[]{:S(2)}) copy-start(f32[32,2,128]{2,1,0:T(2,128)} %constant.104.clone.refs_4_.refs_7_) | copy-start | bytes 98308
  109.4 0.9 copy-start.1
  110.4 0.8 copy-start.3

commit v7 on v5

--- a/solution.py
+++ b/solution.py
@@ -91,10 +91,8 @@
     head = values.astype(jnp.bfloat16)
     tail = (values - head.astype(jnp.float32)).astype(jnp.bfloat16)
 
-    def dot(left, right):
-        return jnp.dot(left, right, preferred_element_type=jnp.float32)
-
-    return dot(head, high) + (dot(tail, high) + dot(head, low))
+    left, right = jnp.concatenate([head, tail, head], 1), jnp.concatenate([high, high, low], 0)
+    return jnp.dot(left, right, preferred_element_type=jnp.float32)
 
 
 def kernel(count, stacked, joined, spilled, turn, *refs):
@@ -108,15 +106,14 @@
         older, older_sigma = refs.pop(0), refs.pop(0)
     weight, high_ref, low_ref, twiddle, before, out = refs[:6]
     field = refs[-1]
-    straight = turn[0] == 0
-
-    def choose(one, two, m, at):
-        plane, half = m // 8 * 4 + m % 4, m // 4 % 2
-        return jnp.where(straight == (half == 0), one[plane, at], two[plane, at])
-
-    def pair_of(one, two, pairs, m, comp, pair):
+
+    def pair_of(source, plane, pairs, comp, pair):
         at = comp * 2 * pairs + pair
-        return choose(one, two, m, at), choose(one, two, m, at + pairs)
+        return source[plane, at], source[plane, at + pairs]
+
+    def either_way(act, *sides):
+        pl.when(turn[0] == 0)(lambda: act(*sides))
+        pl.when(turn[0] == 1)(lambda: act(*(side[::-1] for side in sides)))
 
     def spot(part):
         return pl.ds(part * LANES, LANES)
@@ -127,17 +124,22 @@
     def times(value, factor):
         return value[0] * factor[0] - value[1] * factor[1], value[0] * factor[1] + value[1] * factor[0]
 
-    @pl.loop(0, 2 * count)
-    def _(s):
-        comp, pair = s // count, s % count
-        rows = pl.ds(pl.multiple_of(comp * SLOTS, SLOTS), SLOTS)
-        values = [pair_of(lower, upper, count, m, comp, pair) for m in range(ROWS)]
-        for n, value in enumerate(fourier(values)):
-            real, imag = times(value, twist(n)) if n else value
-            field[n, pair, rows, spot(0)] = real
-            field[n, pair, rows, spot(1)] = imag
-
-    block = 8
+    def forward(halves):
+        @pl.loop(0, 2 * count)
+        def _(s):
+            comp, pair = s // count, s % count
+            rows = pl.ds(pl.multiple_of(comp * SLOTS, SLOTS), SLOTS)
+            values = [
+                pair_of(halves[m // 4 % 2], m // 8 * 4 + m % 4, count, comp, pair) for m in range(ROWS)
+            ]
+            for n, value in enumerate(fourier(values)):
+                real, imag = times(value, twist(n)) if n else value
+                field[n, pair, rows, spot(0)] = real
+                field[n, pair, rows, spot(1)] = imag
+
+    either_way(forward, (lower, upper))
+
+    block = 32 if count <= ORB else 16
     size = block * count * 2 * SLOTS
 
     @pl.loop(0, ROWS // block)
@@ -172,8 +174,9 @@
 
     scale = weight[...]
 
-    @pl.loop(0, ROWS)
-    def _(m):
+    def contract(plane, half, halves, older_halves):
+        m = plane // 4 * 8 + half * 4 + plane % 4
+
         def sigma(comp, a):
             rows = pl.ds(comp * SLOTS, SLOTS)
             if joined and a == 0:
@@ -182,8 +185,8 @@
 
         def given(comp, b):
             if joined and b == 0:
-                return pair_of(older.at[:, 0], older.at[:, 1], ORB + 1, m, comp, ORB)
-            return pair_of(lower, upper, count, m, comp, b - joined)
+                return pair_of(older_halves[half], plane, ORB + 1, comp, ORB)
+            return pair_of(halves[half], plane, count, comp, b - joined)
 
         def memory(a, b):
             left, right = sigma(0, a), given(1, b)
@@ -199,10 +202,19 @@
             one, two = memory(a, b), memory(b, a)
             results += [one[0] + two[0], two[1] - one[1]]
         for i, result in enumerate(results):
-            spare, row = (m // 8 * 4 + m % 4) * 2 + m // 4 % 2, pl.ds(i, 1)
-            out[spare, row, :] = before[spare, row, :] + jnp.sum(result * scale, axis=0, keepdims=True)
+            spot_out, row = plane * 2 + half, pl.ds(i, 1)
+            out[spot_out, row, :] = before[spot_out, row, :] + jnp.sum(result * scale, axis=0, keepdims=True)
         if spilled:
             refs[6][m] = field[m, ORB]
+
+    def contract_all(halves, older_halves):
+        @pl.loop(0, PLANE, unroll=2)
+        def _(plane):
+            for half in range(2):
+                contract(plane, half, halves, older_halves)
+
+    olders = (older.at[:, 0], older.at[:, 1]) if joined else (None, None)
+    either_way(contract_all, (lower, upper), olders)
 
 
 def collide(turn, fields, weights, high, low, twiddle, before, older=(), spilled=False):

time: 158 us -> 156 us (0.987)
  Pallas kernels: 27.3 us -> 22.6 us
  waiting for transfers between devices: 67.3 us -> 70.3 us
    pallas_call x3, Pallas kernels: 20.5 us -> 15.8 us  [collide(): pl.pallas_call(functools.partial(kernel, count, stacked, joined, spilled)...]
    ppermute x3, waiting for transfers between devices: 45.4 us -> 48.5 us  [move(): lax.ppermute(falling, ('zh', 'zl'), shifted(-2))]
  transfers between devices with their start and end apart: 8 -> 8, of which waited for: 5 -> 5; matrix products, arithmetic and copies ran while one was open for 3% -> 3% of each run, Pallas kernels for 10% -> 9%
where the time goes in v7:
time: 156 us
  waiting for transfers between devices  70.3 us (45%)
  blocking collectives  28 us (18%)
  starting transfers between devices  26.1 us (17%)
  Pallas kernels  22.6 us (14%)
  local copies, waits for them, and re-layouts  6.04 us (4%)
  other arithmetic  1.74 us (1%)
    ppermute x3, waiting for transfers between devices, move(): lax.ppermute(falling, ('zh', 'zl'), shifted(-2))  48.5 us
    ppermute x3, waiting for transfers between devices, move(): lax.ppermute(rising, ('zh', 'zl'), shifted(2))  20.6 us
    all_to_all x1, blocking collectives, per_device(): lax.all_to_all(shares, ('zh', 'zl', 'core'), split_axis=0, concat_axis=0)  15.8 us
    pallas_call x3, Pallas kernels, collide(): pl.pallas_call(functools.partial(kernel, count, stacked, joined, spilled)...  15.8 us
    all_to_all x2, starting transfers between devices, spread(): return lax.all_to_all(value, ('y', 'x'), split_axis=0, concat_axis=0)  13 us
    all_to_all x1, blocking collectives, spread(): return lax.all_to_all(value, ('y', 'x'), split_axis=0, concat_axis=0)  12.2 us
    ppermute x3, starting transfers between devices, move(): lax.ppermute(falling, ('zh', 'zl'), shifted(-2))  7.27 us
    pallas_call x2, Pallas kernels, arrange(): pl.pallas_call(functools.partial(arrange_kernel, blocks, apart), out_shap...  6.77 us
  transfers between devices with their start and end apart: 8, of which 5 were waited for; matrix products, arithmetic and copies ran while one was open for 3% of the time, Pallas kernels for 9%

profile of v7, /device:TPU:1, one launch (start us, length us, event | category | flops | bytes accessed | tf_op | source)
XLA Modules:
  0.0 155.5 jit_solution(559894148830635204)
XLA Ops:
  0.0 3.2 %shard_map.55 = (f32[16,16,8,128]{3,2,1,0:T(8,128)}, f32[16,16,8,128]{3,2,1,0:T(8,128)}) custom-call(s32[1]{0:T(128)} %bitcast.1.first, f32[12,3,2,16,8,128]{5,4,3,2,1,0:T(8,128)} %bitcast.45), custom_call_target="tpu_custom_call" | custom-call | bytes 3200000 | tf_op jit(solution)/shard_map/pallas_call | solution.py:262
  3.2 3.9 %collective-permute-start = (f32[16,16,8,128]{3,2,1,0:T(8,128)}, f32[16,16,8,128]{3,2,1,0:T(8,128)S(1)}, u32[]{:S(2)}, u32[]{:S(2)}) collective-permute-start(f32[16,16,8,128]{3,2,1,0:T(8,128)} %get-tuple-element.25), channel_id=1, source_target_pairs={{0,4},{2,6},{4,32},{6,34},{32,36},{34,38},{36,0},{38,2},{1,5},{3,7... | collective-permute-start | bytes 3145736 | tf_op jit(solution)/shard_map/ppermute | solution.py:313
  7.1 3.1 %collective-permute-start.1 = (f32[16,16,8,128]{3,2,1,0:T(8,128)}, f32[16,16,8,128]{3,2,1,0:T(8,128)S(1)}, u32[]{:S(2)}, u32[]{:S(2)}) collective-permute-start(f32[16,16,8,128]{3,2,1,0:T(8,128)} %get-tuple-element.26), channel_id=1, source_target_pairs={{0,36},{2,38},{4,0},{6,2},{32,4},{34,6},{36,32},{38,34},{1,37},{3,... | collective-permute-start | bytes 3145736 | tf_op jit(solution)/shard_map/ppermute | solution.py:314
  10.2 3.6 %shard_map.56 = f32[16,2,20,8,128]{4,3,2,1,0:T(8,128)} custom-call(s32[1]{0:T(128)} %bitcast.1.first, f32[12,3,2,16,8,128]{5,4,3,2,1,0:T(8,128)} %bitcast.46), custom_call_target="tpu_custom_call" | custom-call | bytes 3200000 | tf_op jit(solution)/shard_map/pallas_call | solution.py:262
  13.8 6.8 %all-to-all-start = ((f32[16,2,20,8,128]{4,3,2,1,0:T(8,128)}), f32[16,2,20,8,128]{4,3,2,1,0:T(8,128)}, u32[]{:S(2)}, u32[]{:S(2)}) async-start(f32[16,2,20,8,128]{4,3,2,1,0:T(8,128)} %shard_map.56), calls=%async_computation | async-start | bytes 5242880 | tf_op jit(solution)/shard_map/all_to_all | solution.py:309
  21.3 20.6 %collective-permute-done.refs_0_ = f32[16,16,8,128]{3,2,1,0:T(8,128)S(1)} collective-permute-done((f32[16,16,8,128]{3,2,1,0:T(8,128)}, f32[16,16,8,128]{3,2,1,0:T(8,128)S(1)}, u32[]{:S(2)}, u32[]{:S(2)}) %collective-permute-start) | collective-permute-done | bytes 1048608 | tf_op jit(solution)/shard_map/ppermute | solution.py:313
  41.9 15.2 %collective-permute-done.1.refs_1_ = f32[16,16,8,128]{3,2,1,0:T(8,128)S(1)} collective-permute-done((f32[16,16,8,128]{3,2,1,0:T(8,128)}, f32[16,16,8,128]{3,2,1,0:T(8,128)S(1)}, u32[]{:S(2)}, u32[]{:S(2)}) %collective-permute-start.1) | collective-permute-done | bytes 1048608 | tf_op jit(solution)/shard_map/ppermute | solution.py:314
  57.1 0.1 broadcast_in_dim.19.given
  57.2 1.2 all-to-all-done
  58.4 2.3 %slice_bitcast_fusion.2 = (f32[16,8,8,128]{3,2,1,0:T(8,128)}, f32[16,8,8,128]{3,2,1,0:T(8,128)}) fusion(f32[16,2,20,8,128]{4,3,2,1,0:T(8,128)} %all-to-all-done), kind=kLoop, calls=%fused_computation.3 | loop fusion | bytes 2097152 | tf_op jit(solution)/shard_map/squeeze | solution.py:334
  60.7 1.3 collective-permute-start.3
  62.0 1.1 collective-permute-start.2
  63.1 1.5 pad_maximum_fusion
  64.7 6.2 %all-to-all-start.1 = ((f32[16,2,16,8,128]{4,3,2,1,0:T(8,128)}), f32[16,2,16,8,128]{4,3,2,1,0:T(8,128)S(1)}, u32[]{:S(2)}, u32[]{:S(2)}) async-start(f32[16,2,16,8,128]{4,3,2,1,0:T(8,128)} %pad_maximum_fusion), calls=%async_computation.1 | async-start | bytes 4194304 | tf_op jit(solution)/shard_map/all_to_all | solution.py:309
  70.9 2.6 %slice_bitcast_fusion = (f32[16,12,8,128]{3,2,1,0:T(8,128)}, f32[16,12,8,128]{3,2,1,0:T(8,128)}) fusion(f32[16,2,20,8,128]{4,3,2,1,0:T(8,128)} %all-to-all-done), kind=kLoop, calls=%fused_computation.1 | loop fusion | bytes 3145728 | tf_op jit(solution)/shard_map/squeeze | solution.py:334
  73.5 2.9 %collective-permute-start.5 = (f32[16,12,8,128]{3,2,1,0:T(8,128)}, f32[16,12,8,128]{3,2,1,0:T(8,128)}, u32[]{:S(2)}, u32[]{:S(2)}) collective-permute-start(f32[16,12,8,128]{3,2,1,0:T(8,128)} %get-tuple-element.41), channel_id=1, source_target_pairs={{0,36},{2,38},{4,0},{6,2},{32,4},{34,6},{36,32},{38,34},{1,37},{3,... | collective-permute-start | bytes 2359304 | tf_op jit(solution)/shard_map/ppermute | solution.py:314
  76.4 0.0 copy-start
  76.4 0.0 copy-start.1
  76.4 0.0 copy-start.2
  76.4 0.8 collective-permute-start.4
  77.2 24.9 %collective-permute-done.3.refs_1_ = f32[16,8,8,128]{3,2,1,0:T(8,128)S(1)} collective-permute-done((f32[16,8,8,128]{3,2,1,0:T(8,128)}, f32[16,8,8,128]{3,2,1,0:T(8,128)S(1)}, u32[]{:S(2)}, u32[]{:S(2)}) %collective-permute-start.3) | collective-permute-done | bytes 524320 | tf_op jit(solution)/shard_map/ppermute | solution.py:314
  102.0 0.0 collective-permute-done.2.refs_0_
  102.0 0.0 all-to-all-done.1.refs_0_.refs_2_
  102.1 0.0 copy-done
  102.1 0.0 copy-done.1
  102.1 0.0 copy-done.2
  102.1 6.1 %shard_map.59 = (f32[32,9,128]{2,1,0:T(8,128)S(1)}, f32[32,16,256]{2,1,0:T(8,128)S(1)}) custom-call(s32[1]{0:T(128)} %bitcast.turn, f32[16,2,16,8,128]{4,3,2,1,0:T(8,128)S(1)} %all-to-all-done.1.refs_0_.refs_2_, f32[8,128]{1,0:T(8,128)S(1)} %shard_map.58.refs_1_.refs_4_.refs_2_, bf16[256,256]{1,0:T(8,128)(2,1)S(1)} %copy-done.1, ...), custom_call_target="tpu_custom_call" | custom-call | flops 1000000000 | tf_op jit(solution)/shard_map/pallas_call | solution.py:227
  108.3 3.5 %shard_map.60.refs_6_ = f32[32,9,128]{2,1,0:T(8,128)S(1)} custom-call(s32[1]{0:T(128)} %bitcast.turn, f32[16,8,8,128]{3,2,1,0:T(8,128)S(1)} %collective-permute-done.2.refs_0_, f32[16,8,8,128]{3,2,1,0:T(8,128)S(1)} %collective-permute-done.3.refs_1_, f32[16,2,16,8,128]{4,3,2,1,0:T(8,128)S(1)} %all-to-all-done.1.refs_0_.refs_2_, ...), custom_call_target="tpu_custom_call" | custom-call | flops 1000000000 | tf_op jit(solution)/shard_map/pallas_call | solution.py:227
  111.8 8.4 %collective-permute-done.5.refs_1_ = f32[16,12,8,128]{3,2,1,0:T(8,128)} collective-permute-done((f32[16,12,8,128]{3,2,1,0:T(8,128)}, f32[16,12,8,128]{3,2,1,0:T(8,128)}, u32[]{:S(2)}, u32[]{:S(2)}) %collective-permute-start.5) | collective-permute-done | bytes 786464 | tf_op jit(solution)/shard_map/ppermute | solution.py:314
  120.2 0.0 collective-permute-done.4.refs_0_
  120.2 6.1 %shard_map.61 = f32[32,9,128]{2,1,0:T(8,128)S(1)} custom-call(s32[1]{0:T(128)} %bitcast.turn, f32[16,12,8,128]{3,2,1,0:T(8,128)} %collective-permute-done.4.refs_0_, f32[16,12,8,128]{3,2,1,0:T(8,128)} %collective-permute-done.5.refs_1_, f32[8,128]{1,0:T(8,128)S(1)} %shard_map.58.refs_1_.refs_4_.refs_2_, bf16[256,256]{1,0:T(8,128)(2,1)S(1)} %copy-done.1, ...), custom_call_target="tpu_custom_call" | custom-call | flops 1000000000 | tf_op jit(solution)/shard_map/pallas_call | solution.py:227
  126.4 0.1 copy.15
  126.4 12.2 %all_to_all.20 = f32[16,2,9,128]{3,1,2,0:T(2,128)S(1)} all-to-all(f32[16,2,9,128]{3,1,2,0:T(2,128)S(1)} %copy.15), channel_id=1, replica_groups=mesh['y'=4,'zh'=2,'x'=4,'zl'=4,'core'=2] {'y','x'}, dimensions={0} | all-to-all | bytes 294912 | tf_op jit(solution)/shard_map/all_to_all | solution.py:309
  138.6 0.1 reduce_sum.18
  138.7 0.1 reshape.72
  138.8 0.1 reshape.75
  138.9 15.8 %all_to_all.21 = f32[16,1,144]{2,1,0:T(1,128)S(1)} all-to-all(f32[16,1,144]{2,1,0:T(1,128)S(1)} %reshape.75), channel_id=1, replica_groups=mesh['y'=4,'zh'=2,'x'=4,'zl'=4,'core'=2] {'zh','zl','core'}, dimensions={0} | all-to-all | bytes 18432 | tf_op jit(solution)/shard_map/all_to_all | solution.py:347
  154.8 0.1 negate_bitcast_fusion
  154.8 0.1 stack.18
  154.9 0.6 copy.20
  (8 shorter events, 0.1 us)
Async XLA Ops:
  3.2 38.7 %collective-permute-start = (f32[16,16,8,128]{3,2,1,0:T(8,128)}, f32[16,16,8,128]{3,2,1,0:T(8,128)S(1)}, u32[]{:S(2)}, u32[]{:S(2)}) collective-permute-start(f32[16,16,8,128]{3,2,1,0:T(8,128)} %get-tuple-element.25), channel_id=1, source_target_pairs={{0,4},{2,6},{4,32},{6,34},{32,36},{34,38},{36,0},{38,2},{1,5},{3,7... | collective-permute-start | bytes 3145736 | tf_op jit(solution)/shard_map/ppermute | solution.py:313
  7.1 50.0 %collective-permute-start.1 = (f32[16,16,8,128]{3,2,1,0:T(8,128)}, f32[16,16,8,128]{3,2,1,0:T(8,128)S(1)}, u32[]{:S(2)}, u32[]{:S(2)}) collective-permute-start(f32[16,16,8,128]{3,2,1,0:T(8,128)} %get-tuple-element.26), channel_id=1, source_target_pairs={{0,36},{2,38},{4,0},{6,2},{32,4},{34,6},{36,32},{38,34},{1,37},{3,... | collective-permute-start | bytes 3145736 | tf_op jit(solution)/shard_map/ppermute | solution.py:314
  13.8 44.6 %all-to-all-start = ((f32[16,2,20,8,128]{4,3,2,1,0:T(8,128)}), f32[16,2,20,8,128]{4,3,2,1,0:T(8,128)}, u32[]{:S(2)}, u32[]{:S(2)}) async-start(f32[16,2,20,8,128]{4,3,2,1,0:T(8,128)} %shard_map.56), calls=%async_computation | async-start | bytes 5242880 | tf_op jit(solution)/shard_map/all_to_all | solution.py:309
  60.7 41.3 %collective-permute-start.3 = (f32[16,8,8,128]{3,2,1,0:T(8,128)}, f32[16,8,8,128]{3,2,1,0:T(8,128)S(1)}, u32[]{:S(2)}, u32[]{:S(2)}) collective-permute-start(f32[16,8,8,128]{3,2,1,0:T(8,128)} %get-tuple-element.43), channel_id=1, source_target_pairs={{0,36},{2,38},{4,0},{6,2},{32,4},{34,6},{36,32},{38,34},{1,37},{3,... | collective-permute-start | bytes 1572872 | tf_op jit(solution)/shard_map/ppermute | solution.py:314
  62.0 40.0 %collective-permute-start.2 = (f32[16,8,8,128]{3,2,1,0:T(8,128)}, f32[16,8,8,128]{3,2,1,0:T(8,128)S(1)}, u32[]{:S(2)}, u32[]{:S(2)}) collective-permute-start(f32[16,8,8,128]{3,2,1,0:T(8,128)} %get-tuple-element.44), channel_id=1, source_target_pairs={{0,4},{2,6},{4,32},{6,34},{32,36},{34,38},{36,0},{38,2},{1,5},{3,7... | collective-permute-start | bytes 1572872 | tf_op jit(solution)/shard_map/ppermute | solution.py:313
  64.7 37.4 %all-to-all-start.1 = ((f32[16,2,16,8,128]{4,3,2,1,0:T(8,128)}), f32[16,2,16,8,128]{4,3,2,1,0:T(8,128)S(1)}, u32[]{:S(2)}, u32[]{:S(2)}) async-start(f32[16,2,16,8,128]{4,3,2,1,0:T(8,128)} %pad_maximum_fusion), calls=%async_computation.1 | async-start | bytes 4194304 | tf_op jit(solution)/shard_map/all_to_all | solution.py:309
  73.5 46.7 %collective-permute-start.5 = (f32[16,12,8,128]{3,2,1,0:T(8,128)}, f32[16,12,8,128]{3,2,1,0:T(8,128)}, u32[]{:S(2)}, u32[]{:S(2)}) collective-permute-start(f32[16,12,8,128]{3,2,1,0:T(8,128)} %get-tuple-element.41), channel_id=1, source_target_pairs={{0,36},{2,38},{4,0},{6,2},{32,4},{34,6},{36,32},{38,34},{1,37},{3,... | collective-permute-start | bytes 2359304 | tf_op jit(solution)/shard_map/ppermute | solution.py:314
  76.4 25.7 %copy-start = (bf16[256,256]{1,0:T(8,128)(2,1)S(1)}, bf16[256,256]{1,0:T(8,128)(2,1)}, u32[]{:S(2)}) copy-start(bf16[256,256]{1,0:T(8,128)(2,1)} %constant.103.clone.refs_3_.refs_6_.refs_4_) | copy-start | bytes 393220
  76.4 25.7 %copy-start.1 = (bf16[256,256]{1,0:T(8,128)(2,1)S(1)}, bf16[256,256]{1,0:T(8,128)(2,1)}, u32[]{:S(2)}) copy-start(bf16[256,256]{1,0:T(8,128)(2,1)} %constant.102.clone.refs_2_.refs_5_.refs_3_) | copy-start | bytes 393220
  76.4 25.7 %copy-start.2 = (f32[32,2,128]{2,1,0:T(2,128)S(1)}, f32[32,2,128]{2,1,0:T(2,128)}, u32[]{:S(2)}) copy-start(f32[32,2,128]{2,1,0:T(2,128)} %constant.104.clone.refs_4_.refs_7_.refs_5_) | copy-start | bytes 98308
  76.4 43.8 %collective-permute-start.4 = (f32[16,12,8,128]{3,2,1,0:T(8,128)}, f32[16,12,8,128]{3,2,1,0:T(8,128)}, u32[]{:S(2)}, u32[]{:S(2)}) collective-permute-start(f32[16,12,8,128]{3,2,1,0:T(8,128)} %get-tuple-element.42), channel_id=1, source_target_pairs={{0,4},{2,6},{4,32},{6,34},{32,36},{34,38},{36,0},{38,2},{1,5},{3,7... | collective-permute-start | bytes 2359304 | tf_op jit(solution)/shard_map/ppermute | solution.py:313

commit v8 on v7

--- a/solution.py
+++ b/solution.py
@@ -95,17 +95,19 @@
     return jnp.dot(left, right, preferred_element_type=jnp.float32)
 
 
-def kernel(count, stacked, joined, spilled, turn, *refs):
+def kernel(count, olds, spills, turn, *refs):
+    *refs, field = refs
     refs = list(refs)
-    if stacked:
-        whole = refs.pop(0)
-        lower, upper = whole.at[:, 0], whole.at[:, 1]
-    else:
-        lower, upper = refs.pop(0), refs.pop(0)
-    if joined:
-        older, older_sigma = refs.pop(0), refs.pop(0)
-    weight, high_ref, low_ref, twiddle, before, out = refs[:6]
-    field = refs[-1]
+
+    def halves_of():
+        if len(refs[0].shape) == 5:
+            whole = refs.pop(0)
+            return whole.at[:, 0], whole.at[:, 1]
+        return refs.pop(0), refs.pop(0)
+
+    sides = halves_of()
+    older_sides, older_sigma = (halves_of(), refs.pop(0)) if olds else ((None, None), None)
+    weight, high_ref, low_ref, twiddle, before, out, *spilled = refs
 
     def pair_of(source, plane, pairs, comp, pair):
         at = comp * 2 * pairs + pair
@@ -137,7 +139,7 @@
                 field[n, pair, rows, spot(0)] = real
                 field[n, pair, rows, spot(1)] = imag
 
-    either_way(forward, (lower, upper))
+    either_way(forward, sides)
 
     block = 32 if count <= ORB else 16
     size = block * count * 2 * SLOTS
@@ -179,14 +181,14 @@
 
         def sigma(comp, a):
             rows = pl.ds(comp * SLOTS, SLOTS)
-            if joined and a == 0:
-                return older_sigma[m, rows, spot(0)], older_sigma[m, rows, spot(1)]
-            return field[m, a - joined, rows, spot(0)], field[m, a - joined, rows, spot(1)]
+            if a < len(olds):
+                return older_sigma[a, m, rows, spot(0)], older_sigma[a, m, rows, spot(1)]
+            return field[m, a - len(olds), rows, spot(0)], field[m, a - len(olds), rows, spot(1)]
 
         def given(comp, b):
-            if joined and b == 0:
-                return pair_of(older_halves[half], plane, ORB + 1, comp, ORB)
-            return pair_of(halves[half], plane, count, comp, b - joined)
+            if b < len(olds):
+                return pair_of(older_halves[half], plane, older_halves[half].shape[1] // 4, comp, olds[b])
+            return pair_of(halves[half], plane, count, comp, b - len(olds))
 
         def memory(a, b):
             left, right = sigma(0, a), given(1, b)
@@ -204,8 +206,8 @@
         for i, result in enumerate(results):
             spot_out, row = plane * 2 + half, pl.ds(i, 1)
             out[spot_out, row, :] = before[spot_out, row, :] + jnp.sum(result * scale, axis=0, keepdims=True)
-        if spilled:
-            refs[6][m] = field[m, ORB]
+        for i, pair in enumerate(spills):
+            spilled[0][i, m] = field[m, pair]
 
     def contract_all(halves, older_halves):
         @pl.loop(0, PLANE, unroll=2)
@@ -213,20 +215,20 @@
             for half in range(2):
                 contract(plane, half, halves, older_halves)
 
-    olders = (older.at[:, 0], older.at[:, 1]) if joined else (None, None)
-    either_way(contract_all, (lower, upper), olders)
-
-
-def collide(turn, fields, weights, high, low, twiddle, before, older=(), spilled=False):
-    stacked, joined = len(fields) == 1, int(len(older) > 0)
-    count = ORB + 1 if stacked else ORB - joined
-    shapes = [jax.ShapeDtypeStruct((ROWS, PAIRS, LANES), jnp.float32)]
-    if spilled:
-        shapes.append(jax.ShapeDtypeStruct((ROWS, 2 * SLOTS, 2 * LANES), jnp.float32))
-    inputs = (*fields, *older, weights, high, low, twiddle, before)
+    either_way(contract_all, sides, older_sides)
+
+
+def collide(turn, fields, weights, high, low, twiddle, before, older=None, spills=()):
+    count = fields[0].shape[-3] // 4
+    shapes = [(ROWS, PAIRS, LANES)]
+    if spills:
+        shapes.append((len(spills), ROWS, 2 * SLOTS, 2 * LANES))
+    older_fields, older_sigma, olds = older or ((), None, ())
+    given = (*older_fields, older_sigma) if older else ()
+    inputs = (*fields, *given, weights, high, low, twiddle, before)
     return pl.pallas_call(
-        functools.partial(kernel, count, stacked, joined, spilled),
-        out_shape=shapes,
+        functools.partial(kernel, count, olds, spills),
+        out_shape=[jax.ShapeDtypeStruct(shape, jnp.float32) for shape in shapes],
         in_specs=[pl.BlockSpec(memory_space=pltpu.SMEM)]
         + [pl.BlockSpec(memory_space=pltpu.VMEM)] * len(inputs),
         out_specs=[pl.BlockSpec(memory_space=pltpu.VMEM)] * len(shapes),
@@ -239,15 +241,15 @@
 def arrange_kernel(blocks, apart, first, parts, *refs):
     *outs, sems = refs
     copies, base = [], 0
-    for pairs in blocks:
+    for block, pairs in enumerate(blocks):
         for kind in range(4):
             for i, (a, c) in enumerate(pairs):
-                at = base + kind * len(pairs) + i
+                at = kind * len(pairs) + i
                 for n in range(2):
                     half = first[0] if n == 0 else 1 - first[0]
-                    target = outs[n].at[:, at] if apart else outs[0].at[:, n, at]
+                    target = outs[2 * block + n].at[:, at] if apart else outs[0].at[:, n, base + at]
                     source = parts.at[kind * ORB + a, c, half]
-                    copies.append(pltpu.make_async_copy(source, target, sems.at[n, at]))
+                    copies.append(pltpu.make_async_copy(source, target, sems.at[n, base + at]))
         base += 4 * len(pairs)
     for copy in copies:
         copy.start()
@@ -256,15 +258,17 @@
 
 
 def arrange(first, parts, blocks, apart):
-    count = 4 * sum(len(pairs) for pairs in blocks)
-    whole = (PLANE, count, SLOTS, LANES) if apart else (PLANE, 2, count, SLOTS, LANES)
-    shape = jax.ShapeDtypeStruct(whole, jnp.float32)
+    counts = [4 * len(pairs) for pairs in blocks]
+    if apart:
+        shapes = [(PLANE, count, SLOTS, LANES) for count in counts for _ in range(2)]
+    else:
+        shapes = [(PLANE, 2, sum(counts), SLOTS, LANES)]
     return pl.pallas_call(
         functools.partial(arrange_kernel, blocks, apart),
-        out_shape=[shape] * (2 if apart else 1),
+        out_shape=[jax.ShapeDtypeStruct(shape, jnp.float32) for shape in shapes],
         in_specs=[pl.BlockSpec(memory_space=pltpu.SMEM), pl.BlockSpec(memory_space=pl.ANY)],
-        out_specs=[pl.BlockSpec(memory_space=pltpu.VMEM)] * (2 if apart else 1),
-        scratch_shapes=[pltpu.SemaphoreType.DMA((2, count))],
+        out_specs=[pl.BlockSpec(memory_space=pltpu.VMEM)] * len(shapes),
+        scratch_shapes=[pltpu.SemaphoreType.DMA((2, sum(counts)))],
         compiler_params=pltpu.CompilerParams(vmem_limit_bytes=60 * 1024 * 1024),
         cost_estimate=pl.CostEstimate(flops=0, bytes_accessed=3_200_000, transcendentals=0),
     )(first, parts)
@@ -320,26 +324,30 @@
     turn_flag = turn.reshape(1).astype(jnp.int32)
     partial = jnp.zeros((ROWS, PAIRS, LANES), jnp.float32)
     fence = lax.optimization_barrier
-    early = [[(0, 0), (1, 0), (2, 0), (0, 1)]]
-    late = [[(1, 1), (2, 1)], [(0, 2), (1, 2), (2, 2)]]
+    early = [[(0, 0), (1, 0)], [(2, 0), (0, 1), (1, 1)]]
+    late = [[(2, 1), (0, 2)], [(1, 2), (2, 2)]]
     cut = 4 * len(late[0])
+
+    def joined(first, second):
+        kinds = [part.reshape(PLANE, 4, -1, SLOTS, LANES) for part in (first, second)]
+        return jnp.concatenate(kinds, 2).reshape(PLANE, -1, SLOTS, LANES)
 
     side = zh.reshape(1).astype(jnp.int32)
     zero = arrange(side, parts, early, True)
     zero, side = fence((zero, side))
-    zero = tuple(move(*zero))
+    ahead, zero = tuple(move(*zero[:2])), tuple(move(*zero[2:]))
     (rest,) = arrange(side, parts, late, False)
     rest = spread(rest)
-    zero, rest, weights = fence((zero, rest, settle(weights, zero, 50.0)))
+    ahead, rest, weights = fence((ahead, rest, settle(weights, ahead, 50.0)))
     one, two = (rest[:, 0, :cut], rest[:, 1, :cut]), (rest[:, 0, cut:], rest[:, 1, cut:])
     one = tuple(move(*one))
     two = tuple(move(*two))
-    zero = spread(jnp.stack(zero, 1))
+    zero = spread(jnp.stack([joined(ahead[n], zero[n]) for n in range(2)], 1))
     one, zero, weights = fence((one, zero, settle(weights, one, 50.0)))
-    partial, sigma = work([zero], partial, weights, spilled=True)
-    (partial,) = work(one, partial, weights, older=(zero, sigma))
+    partial, sigma = work([zero], partial, weights, spills=(3, 4))
+    partial, sigma = work(one, partial, weights, older=([zero], sigma, (3, 4)), spills=(1,))
     partial, two = fence((partial, two))
-    (partial,) = work(two, partial, weights)
+    (partial,) = work(two, partial, weights, older=(one, sigma, (1,)))
     blocks = partial.reshape(PLANE, 2, PAIRS, LANES)
     owned = jnp.sum(spread(blocks), axis=0)
     share = LANES // 8

time: 156 us -> 170 us (1.090)
  starting transfers between devices: 26.1 us -> 39.6 us
  local copies, waits for them, and re-layouts: 6.04 us -> 2.45 us
  blocking collectives: 28 us -> 31.2 us
  waiting for transfers between devices: 70.3 us -> 67.3 us
  other arithmetic: 1.74 us -> 4.36 us
    all_to_all x2, waiting for transfers between devices: 1.24 us -> 27 us  [spread(): return lax.all_to_all(value, ('y', 'x'), split_axis=0, concat_axis=0)]
    ppermute x3 -> x4, waiting for transfers between devices: 20.6 us -> 2.8 us  [move(): lax.ppermute(rising, ('zh', 'zl'), shifted(2))]
    ppermute x3 -> x4, waiting for transfers between devices: 48.5 us -> 37.5 us  [move(): lax.ppermute(falling, ('zh', 'zl'), shifted(-2))]
    all_to_all x2, starting transfers between devices: 13 us -> 22.9 us  [spread(): return lax.all_to_all(value, ('y', 'x'), split_axis=0, concat_axis=0)]
    all_to_all x1, blocking collectives: 12.2 us -> 15.8 us  [spread(): return lax.all_to_all(value, ('y', 'x'), split_axis=0, concat_axis=0)]
    concatenate x0 -> x2, other arithmetic: none -> 2.46 us  [joined(): return jnp.concatenate(kinds, 2).reshape(PLANE, -1, SLOTS, LANES)]
    squeeze x1 -> x0, local copies, waits for them, and re-layouts: 2.3 us -> none  [per_device(): rest[:, 1, :cut]]
    ppermute x3 -> x4, starting transfers between devices: 5.78 us -> 7.7 us  [move(): lax.ppermute(rising, ('zh', 'zl'), shifted(2))]
  transfers between devices with their start and end apart: 8 -> 10, of which waited for: 5 -> 4; matrix products, arithmetic and copies ran while one was open for 3% -> 3% of each run, Pallas kernels for 9% -> 9%
where the time goes in v8:
time: 170 us; the launch traced here: 169 us
  waiting for transfers between devices  67.3 us (40%)
  starting transfers between devices  39.6 us (23%)
  blocking collectives  31.2 us (18%)
  Pallas kernels  23.6 us (14%)
  other arithmetic  4.36 us (3%)
  local copies, waits for them, and re-layouts  2.45 us (1%)
    ppermute x4, waiting for transfers between devices, move(): lax.ppermute(falling, ('zh', 'zl'), shifted(-2))  37.5 us
    all_to_all x2, waiting for transfers between devices, spread(): return lax.all_to_all(value, ('y', 'x'), split_axis=0, concat_axis=0)  27 us
    all_to_all x2, starting transfers between devices, spread(): return lax.all_to_all(value, ('y', 'x'), split_axis=0, concat_axis=0)  22.9 us
    pallas_call x3, Pallas kernels, collide(): pl.pallas_call(functools.partial(kernel, count, olds, spills), out_shape=...  16.8 us
    all_to_all x1, blocking collectives, spread(): return lax.all_to_all(value, ('y', 'x'), split_axis=0, concat_axis=0)  15.8 us
    all_to_all x1, blocking collectives, per_device(): lax.all_to_all(shares, ('zh', 'zl', 'core'), split_axis=0, concat_axis=0)  15.4 us
    ppermute x4, starting transfers between devices, move(): lax.ppermute(falling, ('zh', 'zl'), shifted(-2))  8.98 us
    ppermute x4, starting transfers between devices, move(): lax.ppermute(rising, ('zh', 'zl'), shifted(2))  7.7 us
  transfers between devices with their start and end apart: 10, of which 4 were waited for; matrix products, arithmetic and copies ran while one was open for 3% of the time, Pallas kernels for 9%

profile of v8, /device:TPU:1, one launch (start us, length us, event | category | flops | bytes accessed | tf_op | source)
XLA Modules:
  0.0 169.3 jit_solution(1537228410373988271)
XLA Ops:
  0.0 3.6 %shard_map.55 = (f32[16,8,8,128]{3,2,1,0:T(8,128)}, f32[16,8,8,128]{3,2,1,0:T(8,128)}, f32[16,12,8,128]{3,2,1,0:T(8,128)}, f32[16,12,8,128]{3,2,1,0:T(8,128)}) custom-call(s32[1]{0:T(128)} %bitcast.1.first, f32[12,3,2,16,8,128]{5,4,3,2,1,0:T(8,128)} %bitcast.49), custom_call_target="tpu_custom_call" | custom-call | bytes 3200000 | tf_op jit(solution)/shard_map/pallas_call | solution.py:266
  3.6 3.9 %collective-permute-start = (f32[16,8,8,128]{3,2,1,0:T(8,128)}, f32[16,8,8,128]{3,2,1,0:T(8,128)S(1)}, u32[]{:S(2)}, u32[]{:S(2)}) collective-permute-start(f32[16,8,8,128]{3,2,1,0:T(8,128)} %get-tuple-element.33), channel_id=1, source_target_pairs={{0,4},{2,6},{4,32},{6,34},{32,36},{34,38},{36,0},{38,2},{1,5},{3,7... | collective-permute-start | bytes 1572872 | tf_op jit(solution)/shard_map/ppermute | solution.py:317
  7.5 3.1 %collective-permute-start.1 = (f32[16,8,8,128]{3,2,1,0:T(8,128)}, f32[16,8,8,128]{3,2,1,0:T(8,128)S(1)}, u32[]{:S(2)}, u32[]{:S(2)}) collective-permute-start(f32[16,8,8,128]{3,2,1,0:T(8,128)} %get-tuple-element.34), channel_id=1, source_target_pairs={{0,36},{2,38},{4,0},{6,2},{32,4},{34,6},{36,32},{38,34},{1,37},{3,... | collective-permute-start | bytes 1572872 | tf_op jit(solution)/shard_map/ppermute | solution.py:318
  10.6 3.2 %shard_map.56 = f32[16,2,16,8,128]{4,3,2,1,0:T(8,128)} custom-call(s32[1]{0:T(128)} %bitcast.1.first, f32[12,3,2,16,8,128]{5,4,3,2,1,0:T(8,128)} %bitcast.50), custom_call_target="tpu_custom_call" | custom-call | bytes 3200000 | tf_op jit(solution)/shard_map/pallas_call | solution.py:266
  13.8 6.8 %all-to-all-start = ((f32[16,2,16,8,128]{4,3,2,1,0:T(8,128)}), f32[16,2,16,8,128]{4,3,2,1,0:T(8,128)S(1)}, u32[]{:S(2)}, u32[]{:S(2)}) async-start(f32[16,2,16,8,128]{4,3,2,1,0:T(8,128)} %shard_map.56), calls=%async_computation | async-start | bytes 4194304 | tf_op jit(solution)/shard_map/all_to_all | solution.py:313
  20.6 2.4 %collective-permute-start.5 = (f32[16,12,8,128]{3,2,1,0:T(8,128)}, f32[16,12,8,128]{3,2,1,0:T(8,128)}, u32[]{:S(2)}, u32[]{:S(2)}) collective-permute-start(f32[16,12,8,128]{3,2,1,0:T(8,128)} %get-tuple-element.40), channel_id=1, source_target_pairs={{0,36},{2,38},{4,0},{6,2},{32,4},{34,6},{36,32},{38,34},{1,37},{3,... | collective-permute-start | bytes 2359304 | tf_op jit(solution)/shard_map/ppermute | solution.py:318
  22.9 0.1 collective-permute-start.4
  23.7 2.8 %collective-permute-done.refs_0_ = f32[16,8,8,128]{3,2,1,0:T(8,128)S(1)} collective-permute-done((f32[16,8,8,128]{3,2,1,0:T(8,128)}, f32[16,8,8,128]{3,2,1,0:T(8,128)S(1)}, u32[]{:S(2)}, u32[]{:S(2)}) %collective-permute-start) | collective-permute-done | bytes 524320 | tf_op jit(solution)/shard_map/ppermute | solution.py:317
  26.5 24.8 %collective-permute-done.1.refs_1_ = f32[16,8,8,128]{3,2,1,0:T(8,128)S(1)} collective-permute-done((f32[16,8,8,128]{3,2,1,0:T(8,128)}, f32[16,8,8,128]{3,2,1,0:T(8,128)S(1)}, u32[]{:S(2)}, u32[]{:S(2)}) %collective-permute-start.1) | collective-permute-done | bytes 524320 | tf_op jit(solution)/shard_map/ppermute | solution.py:318
  51.3 0.1 broadcast_in_dim.19.given
  51.4 0.0 all-to-all-done
  51.4 1.4 slice_bitcast_fusion
  52.7 0.5 collective-permute-start.2
  53.2 3.1 %collective-permute-start.3 = (f32[16,8,8,128]{3,2,1,0:T(8,128)}, f32[16,8,8,128]{3,2,1,0:T(8,128)}, u32[]{:S(2)}, u32[]{:S(2)}) collective-permute-start(f32[16,8,8,128]{3,2,1,0:T(8,128)} %get-tuple-element.55), channel_id=1, source_target_pairs={{0,36},{2,38},{4,0},{6,2},{32,4},{34,6},{36,32},{38,34},{1,37},{3,... | collective-permute-start | bytes 1572872 | tf_op jit(solution)/shard_map/ppermute | solution.py:318
  56.3 12.7 %collective-permute-done.5 = f32[16,12,8,128]{3,2,1,0:T(8,128)} collective-permute-done((f32[16,12,8,128]{3,2,1,0:T(8,128)}, f32[16,12,8,128]{3,2,1,0:T(8,128)}, u32[]{:S(2)}, u32[]{:S(2)}) %collective-permute-start.5) | collective-permute-done | bytes 786464 | tf_op jit(solution)/shard_map/ppermute | solution.py:318
  69.0 1.2 pad_maximum_fusion.2
  70.2 0.0 collective-permute-done.4
  70.2 1.2 pad_maximum_fusion.1
  71.5 1.7 %pad_maximum_fusion = f32[16,2,20,8,128]{4,3,2,1,0:T(8,128)} fusion(f32[16,1,20,8,128]{4,3,2,1,0:T(8,128)S(1)} %bitcast.51, f32[16,1,20,8,128]{4,3,2,1,0:T(8,128)S(1)} %bitcast.52), kind=kLoop, calls=%fused_computation | loop fusion | flops 655360 | bytes 5242880 | tf_op jit(solution)/shard_map/stack | solution.py:345
  73.2 16.1 %all-to-all-start.1 = ((f32[16,2,20,8,128]{4,3,2,1,0:T(8,128)}), f32[16,2,20,8,128]{4,3,2,1,0:T(8,128)S(1)}, u32[]{:S(2)}, u32[]{:S(2)}) async-start(f32[16,2,20,8,128]{4,3,2,1,0:T(8,128)} %pad_maximum_fusion), calls=%async_computation.1 | async-start | bytes 5242880 | tf_op jit(solution)/shard_map/all_to_all | solution.py:313
  89.3 3.2 %collective-permute-start.6 = (f32[16,8,8,128]{3,2,1,0:T(8,128)}, f32[16,8,8,128]{3,2,1,0:T(8,128)}, u32[]{:S(2)}, u32[]{:S(2)}) collective-permute-start(f32[16,8,8,128]{3,2,1,0:T(8,128)} %get-tuple-element.54), channel_id=1, source_target_pairs={{0,4},{2,6},{4,32},{6,34},{32,36},{34,38},{36,0},{38,2},{1,5},{3,7... | collective-permute-start | bytes 1572872 | tf_op jit(solution)/shard_map/ppermute | solution.py:317
  92.5 0.0 copy-start
  92.5 0.0 copy-start.1
  92.5 0.0 copy-start.2
  92.5 0.4 collective-permute-start.7
  93.0 0.0 collective-permute-done.2.refs_0_.refs_2_
  93.0 0.0 collective-permute-done.3.refs_1_.refs_3_
  93.0 27.0 %all-to-all-done.1.refs_0_.refs_2_ = f32[16,2,20,8,128]{4,3,2,1,0:T(8,128)S(1)} async-done(((f32[16,2,20,8,128]{4,3,2,1,0:T(8,128)}), f32[16,2,20,8,128]{4,3,2,1,0:T(8,128)S(1)}, u32[]{:S(2)}, u32[]{:S(2)}) %all-to-all-start.1) | async-done | bytes 2621472 | tf_op jit(solution)/shard_map/all_to_all | solution.py:313
  120.0 0.0 copy-done
  120.0 0.0 copy-done.1
  120.0 0.0 copy-done.2
  120.0 7.4 %shard_map.59 = (f32[32,9,128]{2,1,0:T(8,128)S(1)}, f32[2,32,16,256]{3,2,1,0:T(8,128)S(1)}) custom-call(s32[1]{0:T(128)} %bitcast.turn, f32[16,2,20,8,128]{4,3,2,1,0:T(8,128)S(1)} %all-to-all-done.1.refs_0_.refs_2_, f32[8,128]{1,0:T(8,128)S(1)} %shard_map.58.refs_1_.refs_4_.refs_5_, bf16[256,256]{1,0:T(8,128)(2,1)S(1)} %copy-done, ...), custom_call_target="tpu_custom_call" | custom-call | flops 1000000000 | tf_op jit(solution)/shard_map/pallas_call | solution.py:229
  127.4 4.5 %shard_map.60 = (f32[32,9,128]{2,1,0:T(8,128)S(1)}, f32[1,32,16,256]{3,2,1,0:T(8,128)S(1)}) custom-call(s32[1]{0:T(128)} %bitcast.turn, f32[16,8,8,128]{3,2,1,0:T(8,128)S(1)} %collective-permute-done.2.refs_0_.refs_2_, f32[16,8,8,128]{3,2,1,0:T(8,128)} %collective-permute-done.3.refs_1_.refs_3_, f32[16,2,20,8,128]{4,3,2,1,0:T(8,128)S(1)} %all-to-all-done.1.refs_0_.refs_2_, ...), custom_call_target="tpu_custom_call" | custom-call | flops 1000000000 | tf_op jit(solution)/shard_map/pallas_call | solution.py:229
  132.0 0.0 collective-permute-done.6.refs_0_
  132.0 0.0 collective-permute-done.7.refs_1_
  132.0 4.8 %shard_map.61 = f32[32,9,128]{2,1,0:T(8,128)S(1)} custom-call(s32[1]{0:T(128)} %bitcast.turn, f32[16,8,8,128]{3,2,1,0:T(8,128)} %collective-permute-done.6.refs_0_, f32[16,8,8,128]{3,2,1,0:T(8,128)} %collective-permute-done.7.refs_1_, f32[16,8,8,128]{3,2,1,0:T(8,128)S(1)} %collective-permute-done.2.refs_0_.refs_2_, ...), custom_call_target="tpu_custom_call" | custom-call | flops 1000000000 | tf_op jit(solution)/shard_map/pallas_call | solution.py:229
  136.8 0.1 copy.15
  136.9 15.8 %all_to_all.20 = f32[16,2,9,128]{3,1,2,0:T(2,128)S(1)} all-to-all(f32[16,2,9,128]{3,1,2,0:T(2,128)S(1)} %copy.15), channel_id=1, replica_groups=mesh['y'=4,'zh'=2,'x'=4,'zl'=4,'core'=2] {'y','x'}, dimensions={0} | all-to-all | bytes 294912 | tf_op jit(solution)/shard_map/all_to_all | solution.py:313
  152.7 0.1 reduce_sum.18
  152.8 0.1 reshape.88
  152.9 0.1 reshape.91
  153.1 15.4 %all_to_all.21 = f32[16,1,144]{2,1,0:T(1,128)S(1)} all-to-all(f32[16,1,144]{2,1,0:T(1,128)S(1)} %reshape.91), channel_id=1, replica_groups=mesh['y'=4,'zh'=2,'x'=4,'zl'=4,'core'=2] {'zh','zl','core'}, dimensions={0} | all-to-all | bytes 18432 | tf_op jit(solution)/shard_map/all_to_all | solution.py:355
  168.5 0.1 negate_bitcast_fusion
  168.6 0.1 stack.10
  168.7 0.6 copy.20
  (8 shorter events, 0.1 us)
Async XLA Ops:
  3.6 22.9 %collective-permute-start = (f32[16,8,8,128]{3,2,1,0:T(8,128)}, f32[16,8,8,128]{3,2,1,0:T(8,128)S(1)}, u32[]{:S(2)}, u32[]{:S(2)}) collective-permute-start(f32[16,8,8,128]{3,2,1,0:T(8,128)} %get-tuple-element.33), channel_id=1, source_target_pairs={{0,4},{2,6},{4,32},{6,34},{32,36},{34,38},{36,0},{38,2},{1,5},{3,7... | collective-permute-start | bytes 1572872 | tf_op jit(solution)/shard_map/ppermute | solution.py:317
  7.5 43.8 %collective-permute-start.1 = (f32[16,8,8,128]{3,2,1,0:T(8,128)}, f32[16,8,8,128]{3,2,1,0:T(8,128)S(1)}, u32[]{:S(2)}, u32[]{:S(2)}) collective-permute-start(f32[16,8,8,128]{3,2,1,0:T(8,128)} %get-tuple-element.34), channel_id=1, source_target_pairs={{0,36},{2,38},{4,0},{6,2},{32,4},{34,6},{36,32},{38,34},{1,37},{3,... | collective-permute-start | bytes 1572872 | tf_op jit(solution)/shard_map/ppermute | solution.py:318
  13.8 37.5 %all-to-all-start = ((f32[16,2,16,8,128]{4,3,2,1,0:T(8,128)}), f32[16,2,16,8,128]{4,3,2,1,0:T(8,128)S(1)}, u32[]{:S(2)}, u32[]{:S(2)}) async-start(f32[16,2,16,8,128]{4,3,2,1,0:T(8,128)} %shard_map.56), calls=%async_computation | async-start | bytes 4194304 | tf_op jit(solution)/shard_map/all_to_all | solution.py:313
  20.6 48.4 %collective-permute-start.5 = (f32[16,12,8,128]{3,2,1,0:T(8,128)}, f32[16,12,8,128]{3,2,1,0:T(8,128)}, u32[]{:S(2)}, u32[]{:S(2)}) collective-permute-start(f32[16,12,8,128]{3,2,1,0:T(8,128)} %get-tuple-element.40), channel_id=1, source_target_pairs={{0,36},{2,38},{4,0},{6,2},{32,4},{34,6},{36,32},{38,34},{1,37},{3,... | collective-permute-start | bytes 2359304 | tf_op jit(solution)/shard_map/ppermute | solution.py:318
  22.9 47.3 %collective-permute-start.4 = (f32[16,12,8,128]{3,2,1,0:T(8,128)}, f32[16,12,8,128]{3,2,1,0:T(8,128)}, u32[]{:S(2)}, u32[]{:S(2)}) collective-permute-start(f32[16,12,8,128]{3,2,1,0:T(8,128)} %get-tuple-element.38), channel_id=1, source_target_pairs={{0,4},{2,6},{4,32},{6,34},{32,36},{34,38},{36,0},{38,2},{1,5},{3,7... | collective-permute-start | bytes 2359304 | tf_op jit(solution)/shard_map/ppermute | solution.py:317
  52.7 40.2 %collective-permute-start.2 = (f32[16,8,8,128]{3,2,1,0:T(8,128)}, f32[16,8,8,128]{3,2,1,0:T(8,128)S(1)}, u32[]{:S(2)}, u32[]{:S(2)}) collective-permute-start(f32[16,8,8,128]{3,2,1,0:T(8,128)} %get-tuple-element.56), channel_id=1, source_target_pairs={{0,4},{2,6},{4,32},{6,34},{32,36},{34,38},{36,0},{38,2},{1,5},{3,7... | collective-permute-start | bytes 1572872 | tf_op jit(solution)/shard_map/ppermute | solution.py:317
  53.2 39.8 %collective-permute-start.3 = (f32[16,8,8,128]{3,2,1,0:T(8,128)}, f32[16,8,8,128]{3,2,1,0:T(8,128)}, u32[]{:S(2)}, u32[]{:S(2)}) collective-permute-start(f32[16,8,8,128]{3,2,1,0:T(8,128)} %get-tuple-element.55), channel_id=1, source_target_pairs={{0,36},{2,38},{4,0},{6,2},{32,4},{34,6},{36,32},{38,34},{1,37},{3,... | collective-permute-start | bytes 1572872 | tf_op jit(solution)/shard_map/ppermute | solution.py:318
  73.2 46.8 %all-to-all-start.1 = ((f32[16,2,20,8,128]{4,3,2,1,0:T(8,128)}), f32[16,2,20,8,128]{4,3,2,1,0:T(8,128)S(1)}, u32[]{:S(2)}, u32[]{:S(2)}) async-start(f32[16,2,20,8,128]{4,3,2,1,0:T(8,128)} %pad_maximum_fusion), calls=%async_computation.1 | async-start | bytes 5242880 | tf_op jit(solution)/shard_map/all_to_all | solution.py:313
  89.3 42.7 %collective-permute-start.6 = (f32[16,8,8,128]{3,2,1,0:T(8,128)}, f32[16,8,8,128]{3,2,1,0:T(8,128)}, u32[]{:S(2)}, u32[]{:S(2)}) collective-permute-start(f32[16,8,8,128]{3,2,1,0:T(8,128)} %get-tuple-element.54), channel_id=1, source_target_pairs={{0,4},{2,6},{4,32},{6,34},{32,36},{34,38},{36,0},{38,2},{1,5},{3,7... | collective-permute-start | bytes 1572872 | tf_op jit(solution)/shard_map/ppermute | solution.py:317
  92.5 27.4 %copy-start = (bf16[256,256]{1,0:T(8,128)(2,1)S(1)}, bf16[256,256]{1,0:T(8,128)(2,1)}, u32[]{:S(2)}) copy-start(bf16[256,256]{1,0:T(8,128)(2,1)} %constant.102.clone.refs_2_.refs_5_.refs_6_) | copy-start | bytes 393220
  92.5 27.4 %copy-start.1 = (bf16[256,256]{1,0:T(8,128)(2,1)S(1)}, bf16[256,256]{1,0:T(8,128)(2,1)}, u32[]{:S(2)}) copy-start(bf16[256,256]{1,0:T(8,128)(2,1)} %constant.103.clone.refs_3_.refs_6_.refs_7_) | copy-start | bytes 393220
  92.5 27.4 %copy-start.2 = (f32[32,2,128]{2,1,0:T(2,128)S(1)}, f32[32,2,128]{2,1,0:T(2,128)}, u32[]{:S(2)}) copy-start(f32[32,2,128]{2,1,0:T(2,128)} %constant.104.clone.refs_4_.refs_7_.refs_8_) | copy-start | bytes 98308
  92.5 39.4 %collective-permute-start.7 = (f32[16,8,8,128]{3,2,1,0:T(8,128)}, f32[16,8,8,128]{3,2,1,0:T(8,128)}, u32[]{:S(2)}, u32[]{:S(2)}) collective-permute-start(f32[16,8,8,128]{3,2,1,0:T(8,128)} %get-tuple-element.53), channel_id=1, source_target_pairs={{0,36},{2,38},{4,0},{6,2},{32,4},{34,6},{36,32},{38,34},{1,37},{3,... | collective-permute-start | bytes 1572872 | tf_op jit(solution)/shard_map/ppermute | solution.py:318

commit v9 on v7

--- a/solution.py
+++ b/solution.py
@@ -265,9 +265,33 @@
         in_specs=[pl.BlockSpec(memory_space=pltpu.SMEM), pl.BlockSpec(memory_space=pl.ANY)],
         out_specs=[pl.BlockSpec(memory_space=pltpu.VMEM)] * (2 if apart else 1),
         scratch_shapes=[pltpu.SemaphoreType.DMA((2, count))],
-        compiler_params=pltpu.CompilerParams(vmem_limit_bytes=60 * 1024 * 1024),
+        compiler_params=pltpu.CompilerParams(vmem_limit_bytes=8 * 1024 * 1024),
         cost_estimate=pl.CostEstimate(flops=0, bytes_accessed=3_200_000, transcendentals=0),
     )(first, parts)
+
+
+def cut_kernel(base, whole, *refs):
+    *outs, sems = refs
+    copies = []
+    for n, out in enumerate(outs):
+        source = whole.at[:, n, pl.ds(base, out.shape[1])]
+        copies.append(pltpu.make_async_copy(source, out, sems.at[n]))
+    for copy in copies:
+        copy.start()
+    for copy in copies:
+        copy.wait()
+
+
+def cut(whole, base, size):
+    return pl.pallas_call(
+        functools.partial(cut_kernel, base),
+        out_shape=[jax.ShapeDtypeStruct((PLANE, size, SLOTS, LANES), jnp.float32)] * 2,
+        in_specs=[pl.BlockSpec(memory_space=pl.ANY)],
+        out_specs=[pl.BlockSpec(memory_space=pltpu.VMEM)] * 2,
+        scratch_shapes=[pltpu.SemaphoreType.DMA((2,))],
+        compiler_params=pltpu.CompilerParams(vmem_limit_bytes=8 * 1024 * 1024),
+        cost_estimate=pl.CostEstimate(flops=0, bytes_accessed=3_200_000, transcendentals=0),
+    )(whole)
 
 
 def settle(weights, fields, cost):
@@ -322,7 +346,6 @@
     fence = lax.optimization_barrier
     early = [[(0, 0), (1, 0), (2, 0), (0, 1)]]
     late = [[(1, 1), (2, 1)], [(0, 2), (1, 2), (2, 2)]]
-    cut = 4 * len(late[0])
 
     side = zh.reshape(1).astype(jnp.int32)
     zero = arrange(side, parts, early, True)
@@ -331,7 +354,8 @@
     (rest,) = arrange(side, parts, late, False)
     rest = spread(rest)
     zero, rest, weights = fence((zero, rest, settle(weights, zero, 50.0)))
-    one, two = (rest[:, 0, :cut], rest[:, 1, :cut]), (rest[:, 0, cut:], rest[:, 1, cut:])
+    one = cut(rest, 0, 4 * len(late[0]))
+    two = cut(rest, 4 * len(late[0]), 4 * len(late[1]))
     one = tuple(move(*one))
     two = tuple(move(*two))
     zero = spread(jnp.stack(zero, 1))

time: 156 us -> 155 us (level)
  waiting for transfers between devices: 70.3 us -> 66.8 us
  Pallas kernels: 22.6 us -> 20.8 us
  starting transfers between devices: 26.1 us -> 27.8 us
  other arithmetic: 1.74 us -> 3.31 us
    ppermute x3, waiting for transfers between devices: 48.5 us -> 15.3 us  [move(): lax.ppermute(falling, ('zh', 'zl'), shifted(-2))]
    ppermute x3, waiting for transfers between devices: 20.6 us -> 45.2 us  [move(): lax.ppermute(rising, ('zh', 'zl'), shifted(2))]
    unnamed x6 -> x14, local copies, waits for them, and re-layouts: 0.01 us -> 5.64 us
    all_to_all x2, waiting for transfers between devices: 1.24 us -> 6.24 us  [spread(): return lax.all_to_all(value, ('y', 'x'), split_axis=0, concat_axis=0)]
    squeeze x2 -> x0, local copies, waits for them, and re-layouts: 4.95 us -> none  [the longest x1 2.65 us: per_device(): rest[:, 1, cut:]]
    pallas_call x2, Pallas kernels: 6.77 us -> 2.7 us  [arrange(): pl.pallas_call(functools.partial(arrange_kernel, blocks, apart), out_shap...]
    all_to_all x1, blocking collectives: 15.8 us -> 19.2 us  [per_device(): lax.all_to_all(shares, ('zh', 'zl', 'core'), split_axis=0, concat_axis=0)]
    ppermute x3, starting transfers between devices: 5.78 us -> 8.92 us  [move(): lax.ppermute(rising, ('zh', 'zl'), shifted(2))]
  transfers between devices with their start and end apart: 8 -> 8, of which waited for: 5 -> 5; matrix products, arithmetic and copies ran while one was open for 3% -> 2% of each run, Pallas kernels for 9% -> 7%
where the time goes in v9:
time: 155 us
  waiting for transfers between devices  66.8 us (43%)
  blocking collectives  28.8 us (19%)
  starting transfers between devices  27.8 us (18%)
  Pallas kernels  20.8 us (13%)
  local copies, waits for them, and re-layouts  6.72 us (4%)
  other arithmetic  3.31 us (2%)
    ppermute x3, waiting for transfers between devices, move(): lax.ppermute(rising, ('zh', 'zl'), shifted(2))  45.2 us
    all_to_all x1, blocking collectives, per_device(): lax.all_to_all(shares, ('zh', 'zl', 'core'), split_axis=0, concat_axis=0)  19.2 us
    pallas_call x3, Pallas kernels, collide(): pl.pallas_call(functools.partial(kernel, count, stacked, joined, spilled)...  16.9 us
    ppermute x3, waiting for transfers between devices, move(): lax.ppermute(falling, ('zh', 'zl'), shifted(-2))  15.3 us
    all_to_all x2, starting transfers between devices, spread(): return lax.all_to_all(value, ('y', 'x'), split_axis=0, concat_axis=0)  13.5 us
    all_to_all x1, blocking collectives, spread(): return lax.all_to_all(value, ('y', 'x'), split_axis=0, concat_axis=0)  9.52 us
    ppermute x3, starting transfers between devices, move(): lax.ppermute(rising, ('zh', 'zl'), shifted(2))  8.92 us
    all_to_all x2, waiting for transfers between devices, spread(): return lax.all_to_all(value, ('y', 'x'), split_axis=0, concat_axis=0)  6.24 us
  transfers between devices with their start and end apart: 8, of which 5 were waited for; matrix products, arithmetic and copies ran while one was open for 2% of the time, Pallas kernels for 7%

profile of v9, /device:TPU:1, one launch (start us, length us, event | category | flops | bytes accessed | tf_op | source)
XLA Modules:
  0.0 155.1 jit_solution(14231120076566096164)
XLA Ops:
  0.0 0.0 copy-start
  0.0 2.3 %copy-done = f32[2,2,3,3,256,128]{5,4,3,2,1,0:T(8,128)S(1)} copy-done((f32[2,2,3,3,256,128]{5,4,3,2,1,0:T(8,128)S(1)}, f32[2,2,3,3,256,128]{5,4,3,2,1,0:T(8,128)}, u32[]{:S(2)}) %copy-start) | copy-done | bytes 4718616
  2.3 1.9 %shard_map.55 = (f32[16,16,8,128]{3,2,1,0:T(8,128)}, f32[16,16,8,128]{3,2,1,0:T(8,128)}) custom-call(s32[1]{0:T(128)} %bitcast.1.first, f32[12,3,2,16,8,128]{5,4,3,2,1,0:T(8,128)S(1)} %bitcast.34), custom_call_target="tpu_custom_call" | custom-call | bytes 3200000 | tf_op jit(solution)/shard_map/pallas_call | solution.py:262
  4.3 3.9 %collective-permute-start = (f32[16,16,8,128]{3,2,1,0:T(8,128)}, f32[16,16,8,128]{3,2,1,0:T(8,128)}, u32[]{:S(2)}, u32[]{:S(2)}) collective-permute-start(f32[16,16,8,128]{3,2,1,0:T(8,128)} %get-tuple-element.29), channel_id=1, source_target_pairs={{0,4},{2,6},{4,32},{6,34},{32,36},{34,38},{36,0},{38,2},{1,5},{3,7... | collective-permute-start | bytes 3145736 | tf_op jit(solution)/shard_map/ppermute | solution.py:337
  8.2 3.1 %collective-permute-start.1 = (f32[16,16,8,128]{3,2,1,0:T(8,128)}, f32[16,16,8,128]{3,2,1,0:T(8,128)}, u32[]{:S(2)}, u32[]{:S(2)}) collective-permute-start(f32[16,16,8,128]{3,2,1,0:T(8,128)} %get-tuple-element.30), channel_id=1, source_target_pairs={{0,36},{2,38},{4,0},{6,2},{32,4},{34,6},{36,32},{38,34},{1,37},{3,... | collective-permute-start | bytes 3145736 | tf_op jit(solution)/shard_map/ppermute | solution.py:338
  11.3 0.8 shard_map.56
  12.1 0.0 copy-start.1
  12.1 1.5 copy-done.1
  13.6 6.8 %all-to-all-start = ((f32[16,2,20,8,128]{4,3,2,1,0:T(8,128)}), f32[16,2,20,8,128]{4,3,2,1,0:T(8,128)S(1)}, u32[]{:S(2)}, u32[]{:S(2)}) async-start(f32[16,2,20,8,128]{4,3,2,1,0:T(8,128)} %copy-done.1), calls=%async_computation | async-start | bytes 5242880 | tf_op jit(solution)/shard_map/all_to_all | solution.py:333
  21.1 22.0 %collective-permute-done.refs_0_ = f32[16,16,8,128]{3,2,1,0:T(8,128)} collective-permute-done((f32[16,16,8,128]{3,2,1,0:T(8,128)}, f32[16,16,8,128]{3,2,1,0:T(8,128)}, u32[]{:S(2)}, u32[]{:S(2)}) %collective-permute-start) | collective-permute-done | bytes 1048608 | tf_op jit(solution)/shard_map/ppermute | solution.py:337
  43.0 15.3 %collective-permute-done.1.refs_1_ = f32[16,16,8,128]{3,2,1,0:T(8,128)} collective-permute-done((f32[16,16,8,128]{3,2,1,0:T(8,128)}, f32[16,16,8,128]{3,2,1,0:T(8,128)}, u32[]{:S(2)}, u32[]{:S(2)}) %collective-permute-start.1) | collective-permute-done | bytes 1048608 | tf_op jit(solution)/shard_map/ppermute | solution.py:338
  58.3 0.1 broadcast_in_dim.19.given
  58.4 0.0 all-to-all-done.whole
  58.4 1.1 shard_map.58
  59.5 3.1 %collective-permute-start.2 = (f32[16,8,8,128]{3,2,1,0:T(8,128)}, f32[16,8,8,128]{3,2,1,0:T(8,128)S(1)}, u32[]{:S(2)}, u32[]{:S(2)}) collective-permute-start(f32[16,8,8,128]{3,2,1,0:T(8,128)} %get-tuple-element.33), channel_id=1, source_target_pairs={{0,4},{2,6},{4,32},{6,34},{32,36},{34,38},{36,0},{38,2},{1,5},{3,7... | collective-permute-start | bytes 1572872 | tf_op jit(solution)/shard_map/ppermute | solution.py:337
  62.6 0.5 collective-permute-start.3
  63.1 0.1 shard_map.62
  63.3 0.0 copy-start.5
  63.3 0.9 copy-done.5
  64.2 0.0 copy-start.6
  64.2 0.9 copy-done.6
  65.1 3.1 %pad_maximum_fusion = f32[16,2,16,8,128]{4,3,2,1,0:T(8,128)} fusion(f32[16,1,16,8,128]{4,3,2,1,0:T(8,128)} %bitcast.5, f32[16,1,16,8,128]{4,3,2,1,0:T(8,128)} %bitcast.4), kind=kLoop, calls=%fused_computation | loop fusion | flops 524288 | bytes 4194304 | tf_op jit(solution)/shard_map/stack | solution.py:361
  68.2 6.8 %all-to-all-start.1 = ((f32[16,2,16,8,128]{4,3,2,1,0:T(8,128)}), f32[16,2,16,8,128]{4,3,2,1,0:T(8,128)S(1)}, u32[]{:S(2)}, u32[]{:S(2)}) async-start(f32[16,2,16,8,128]{4,3,2,1,0:T(8,128)} %pad_maximum_fusion), calls=%async_computation.1 | async-start | bytes 4194304 | tf_op jit(solution)/shard_map/all_to_all | solution.py:333
  74.9 1.9 %collective-permute-start.4 = (f32[16,12,8,128]{3,2,1,0:T(8,128)}, f32[16,12,8,128]{3,2,1,0:T(8,128)}, u32[]{:S(2)}, u32[]{:S(2)}) collective-permute-start(f32[16,12,8,128]{3,2,1,0:T(8,128)} %copy-done.6), channel_id=1, source_target_pairs={{0,4},{2,6},{4,32},{6,34},{32,36},{34,38},{36,0},{38,2},{1,5},{3,7... | collective-permute-start | bytes 2359304 | tf_op jit(solution)/shard_map/ppermute | solution.py:337
  76.8 0.0 copy-start.2
  76.8 0.0 copy-start.3
  76.8 0.0 copy-start.4
  76.9 1.7 %collective-permute-start.5 = (f32[16,12,8,128]{3,2,1,0:T(8,128)}, f32[16,12,8,128]{3,2,1,0:T(8,128)}, u32[]{:S(2)}, u32[]{:S(2)}) collective-permute-start(f32[16,12,8,128]{3,2,1,0:T(8,128)} %copy-done.5), channel_id=1, source_target_pairs={{0,36},{2,38},{4,0},{6,2},{32,4},{34,6},{36,32},{38,34},{1,37},{3,... | collective-permute-start | bytes 2359304 | tf_op jit(solution)/shard_map/ppermute | solution.py:338
  78.6 17.8 %collective-permute-done.2.refs_0_ = f32[16,8,8,128]{3,2,1,0:T(8,128)S(1)} collective-permute-done((f32[16,8,8,128]{3,2,1,0:T(8,128)}, f32[16,8,8,128]{3,2,1,0:T(8,128)S(1)}, u32[]{:S(2)}, u32[]{:S(2)}) %collective-permute-start.2) | collective-permute-done | bytes 524320 | tf_op jit(solution)/shard_map/ppermute | solution.py:337
  96.4 0.0 collective-permute-done.3.refs_1_
  96.4 6.2 %all-to-all-done.1.refs_0_.refs_2_ = f32[16,2,16,8,128]{4,3,2,1,0:T(8,128)S(1)} async-done(((f32[16,2,16,8,128]{4,3,2,1,0:T(8,128)}), f32[16,2,16,8,128]{4,3,2,1,0:T(8,128)S(1)}, u32[]{:S(2)}, u32[]{:S(2)}) %all-to-all-start.1) | async-done | bytes 2097184 | tf_op jit(solution)/shard_map/all_to_all | solution.py:333
  102.7 0.0 copy-done.2
  102.7 0.0 copy-done.3
  102.7 0.0 copy-done.4
  102.7 6.1 %shard_map.60 = (f32[32,9,128]{2,1,0:T(8,128)S(1)}, f32[32,16,256]{2,1,0:T(8,128)S(1)}) custom-call(s32[1]{0:T(128)} %bitcast.turn, f32[16,2,16,8,128]{4,3,2,1,0:T(8,128)S(1)} %all-to-all-done.1.refs_0_.refs_2_, f32[8,128]{1,0:T(8,128)S(1)} %shard_map.59.refs_1_.refs_4_.refs_2_, bf16[256,256]{1,0:T(8,128)(2,1)S(1)} %copy-done.3, ...), custom_call_target="tpu_custom_call" | custom-call | flops 1000000000 | tf_op jit(solution)/shard_map/pallas_call | solution.py:227
  108.9 4.5 %shard_map.61.refs_6_ = f32[32,9,128]{2,1,0:T(8,128)S(1)} custom-call(s32[1]{0:T(128)} %bitcast.turn, f32[16,8,8,128]{3,2,1,0:T(8,128)S(1)} %collective-permute-done.2.refs_0_, f32[16,8,8,128]{3,2,1,0:T(8,128)} %collective-permute-done.3.refs_1_, f32[16,2,16,8,128]{4,3,2,1,0:T(8,128)S(1)} %all-to-all-done.1.refs_0_.refs_2_, ...), custom_call_target="tpu_custom_call" | custom-call | flops 1000000000 | tf_op jit(solution)/shard_map/pallas_call | solution.py:227
  113.4 5.4 %collective-permute-done.4.refs_0_ = f32[16,12,8,128]{3,2,1,0:T(8,128)} collective-permute-done((f32[16,12,8,128]{3,2,1,0:T(8,128)}, f32[16,12,8,128]{3,2,1,0:T(8,128)}, u32[]{:S(2)}, u32[]{:S(2)}) %collective-permute-start.4) | collective-permute-done | bytes 786464 | tf_op jit(solution)/shard_map/ppermute | solution.py:337
  118.8 0.0 collective-permute-done.5.refs_1_
  118.8 6.3 %shard_map.63 = f32[32,9,128]{2,1,0:T(8,128)S(1)} custom-call(s32[1]{0:T(128)} %bitcast.turn, f32[16,12,8,128]{3,2,1,0:T(8,128)} %collective-permute-done.4.refs_0_, f32[16,12,8,128]{3,2,1,0:T(8,128)} %collective-permute-done.5.refs_1_, f32[8,128]{1,0:T(8,128)S(1)} %shard_map.59.refs_1_.refs_4_.refs_2_, bf16[256,256]{1,0:T(8,128)(2,1)S(1)} %copy-done.3, ...), custom_call_target="tpu_custom_call" | custom-call | flops 1000000000 | tf_op jit(solution)/shard_map/pallas_call | solution.py:227
  125.1 0.1 copy.9
  125.2 9.5 %all_to_all.20 = f32[16,2,9,128]{3,1,2,0:T(2,128)S(1)} all-to-all(f32[16,2,9,128]{3,1,2,0:T(2,128)S(1)} %copy.9), channel_id=1, replica_groups=mesh['y'=4,'zh'=2,'x'=4,'zl'=4,'core'=2] {'y','x'}, dimensions={0} | all-to-all | bytes 294912 | tf_op jit(solution)/shard_map/all_to_all | solution.py:333
  134.7 0.1 reduce_sum.18
  134.8 0.1 reshape.72
  134.9 0.1 reshape.75
  135.0 19.2 %all_to_all.21 = f32[16,1,144]{2,1,0:T(1,128)S(1)} all-to-all(f32[16,1,144]{2,1,0:T(1,128)S(1)} %reshape.75), channel_id=1, replica_groups=mesh['y'=4,'zh'=2,'x'=4,'zl'=4,'core'=2] {'zh','zl','core'}, dimensions={0} | all-to-all | bytes 18432 | tf_op jit(solution)/shard_map/all_to_all | solution.py:371
  154.3 0.1 negate_bitcast_fusion
  154.4 0.1 stack.18
  154.5 0.6 copy.14
  (8 shorter events, 0.1 us)
Async XLA Ops:
  0.0 2.3 %copy-start = (f32[2,2,3,3,256,128]{5,4,3,2,1,0:T(8,128)S(1)}, f32[2,2,3,3,256,128]{5,4,3,2,1,0:T(8,128)}, u32[]{:S(2)}) copy-start(f32[2,2,3,3,256,128]{5,4,3,2,1,0:T(8,128)} %param.5) | copy-start | bytes 14155780
  4.3 38.7 %collective-permute-start = (f32[16,16,8,128]{3,2,1,0:T(8,128)}, f32[16,16,8,128]{3,2,1,0:T(8,128)}, u32[]{:S(2)}, u32[]{:S(2)}) collective-permute-start(f32[16,16,8,128]{3,2,1,0:T(8,128)} %get-tuple-element.29), channel_id=1, source_target_pairs={{0,4},{2,6},{4,32},{6,34},{32,36},{34,38},{36,0},{38,2},{1,5},{3,7... | collective-permute-start | bytes 3145736 | tf_op jit(solution)/shard_map/ppermute | solution.py:337
  8.2 50.1 %collective-permute-start.1 = (f32[16,16,8,128]{3,2,1,0:T(8,128)}, f32[16,16,8,128]{3,2,1,0:T(8,128)}, u32[]{:S(2)}, u32[]{:S(2)}) collective-permute-start(f32[16,16,8,128]{3,2,1,0:T(8,128)} %get-tuple-element.30), channel_id=1, source_target_pairs={{0,36},{2,38},{4,0},{6,2},{32,4},{34,6},{36,32},{38,34},{1,37},{3,... | collective-permute-start | bytes 3145736 | tf_op jit(solution)/shard_map/ppermute | solution.py:338
  12.1 1.5 copy-start.1
  13.6 44.8 %all-to-all-start = ((f32[16,2,20,8,128]{4,3,2,1,0:T(8,128)}), f32[16,2,20,8,128]{4,3,2,1,0:T(8,128)S(1)}, u32[]{:S(2)}, u32[]{:S(2)}) async-start(f32[16,2,20,8,128]{4,3,2,1,0:T(8,128)} %copy-done.1), calls=%async_computation | async-start | bytes 5242880 | tf_op jit(solution)/shard_map/all_to_all | solution.py:333
  59.5 37.0 %collective-permute-start.2 = (f32[16,8,8,128]{3,2,1,0:T(8,128)}, f32[16,8,8,128]{3,2,1,0:T(8,128)S(1)}, u32[]{:S(2)}, u32[]{:S(2)}) collective-permute-start(f32[16,8,8,128]{3,2,1,0:T(8,128)} %get-tuple-element.33), channel_id=1, source_target_pairs={{0,4},{2,6},{4,32},{6,34},{32,36},{34,38},{36,0},{38,2},{1,5},{3,7... | collective-permute-start | bytes 1572872 | tf_op jit(solution)/shard_map/ppermute | solution.py:337
  62.6 33.8 %collective-permute-start.3 = (f32[16,8,8,128]{3,2,1,0:T(8,128)}, f32[16,8,8,128]{3,2,1,0:T(8,128)}, u32[]{:S(2)}, u32[]{:S(2)}) collective-permute-start(f32[16,8,8,128]{3,2,1,0:T(8,128)} %get-tuple-element.34), channel_id=1, source_target_pairs={{0,36},{2,38},{4,0},{6,2},{32,4},{34,6},{36,32},{38,34},{1,37},{3,... | collective-permute-start | bytes 1572872 | tf_op jit(solution)/shard_map/ppermute | solution.py:338
  63.3 0.9 copy-start.5
  64.2 0.9 copy-start.6
  68.2 34.5 %all-to-all-start.1 = ((f32[16,2,16,8,128]{4,3,2,1,0:T(8,128)}), f32[16,2,16,8,128]{4,3,2,1,0:T(8,128)S(1)}, u32[]{:S(2)}, u32[]{:S(2)}) async-start(f32[16,2,16,8,128]{4,3,2,1,0:T(8,128)} %pad_maximum_fusion), calls=%async_computation.1 | async-start | bytes 4194304 | tf_op jit(solution)/shard_map/all_to_all | solution.py:333
  74.9 43.9 %collective-permute-start.4 = (f32[16,12,8,128]{3,2,1,0:T(8,128)}, f32[16,12,8,128]{3,2,1,0:T(8,128)}, u32[]{:S(2)}, u32[]{:S(2)}) collective-permute-start(f32[16,12,8,128]{3,2,1,0:T(8,128)} %copy-done.6), channel_id=1, source_target_pairs={{0,4},{2,6},{4,32},{6,34},{32,36},{34,38},{36,0},{38,2},{1,5},{3,7... | collective-permute-start | bytes 2359304 | tf_op jit(solution)/shard_map/ppermute | solution.py:337
  76.8 25.9 %copy-start.2 = (bf16[256,256]{1,0:T(8,128)(2,1)S(1)}, bf16[256,256]{1,0:T(8,128)(2,1)}, u32[]{:S(2)}) copy-start(bf16[256,256]{1,0:T(8,128)(2,1)} %constant.103.clone.refs_3_.refs_6_.refs_4_) | copy-start | bytes 393220
  76.8 25.9 %copy-start.3 = (bf16[256,256]{1,0:T(8,128)(2,1)S(1)}, bf16[256,256]{1,0:T(8,128)(2,1)}, u32[]{:S(2)}) copy-start(bf16[256,256]{1,0:T(8,128)(2,1)} %constant.102.clone.refs_2_.refs_5_.refs_3_) | copy-start | bytes 393220
  76.8 25.9 %copy-start.4 = (f32[32,2,128]{2,1,0:T(2,128)S(1)}, f32[32,2,128]{2,1,0:T(2,128)}, u32[]{:S(2)}) copy-start(f32[32,2,128]{2,1,0:T(2,128)} %constant.104.clone.refs_4_.refs_7_.refs_5_) | copy-start | bytes 98308
  76.9 42.0 %collective-permute-start.5 = (f32[16,12,8,128]{3,2,1,0:T(8,128)}, f32[16,12,8,128]{3,2,1,0:T(8,128)}, u32[]{:S(2)}, u32[]{:S(2)}) collective-permute-start(f32[16,12,8,128]{3,2,1,0:T(8,128)} %copy-done.5), channel_id=1, source_target_pairs={{0,36},{2,38},{4,0},{6,2},{32,4},{34,6},{36,32},{38,34},{1,37},{3,... | collective-permute-start | bytes 2359304 | tf_op jit(solution)/shard_map/ppermute | solution.py:338

commit v10 on v9

--- a/solution.py
+++ b/solution.py
@@ -308,18 +308,12 @@
     )(weights, *fields)
 
 
-def shifted(step):
-    return [(z, (z + step) % 8) for z in range(8)]
-
-
 def per_device(green_row, time_step):
     slot_count = green_row.shape[4]
     history = slot_count * 8
     zh, zl, core = (lax.axis_index(axis) for axis in ("zh", "zl", "core"))
     plane = lax.axis_index("y") * 4 + lax.axis_index("x")
-    turn = ((zh * 4 + zl + 2) // 4 + 1) % 2
-    origin = (zl + 2) % 4 * 2 + core
-    first = origin * slot_count + turn * (slot_count // 2) + plane * SLOTS
+    first = (zl * 2 + core) * slot_count + zh * (slot_count // 2) + plane * SLOTS
     slot_ids = first + jnp.arange(SLOTS, dtype=jnp.int32)
     slot_age = (time_step[0] - 1 - slot_ids) % history + 1
     decays = jnp.exp2(-(slot_age - 1).astype(jnp.float32) / history)
@@ -332,16 +326,13 @@
     def spread(value):
         return lax.all_to_all(value, ("y", "x"), split_axis=0, concat_axis=0)
 
-    def move(rising, falling):
-        return (
-            lax.ppermute(rising, ("zh", "zl"), shifted(2)),
-            lax.ppermute(falling, ("zh", "zl"), shifted(-2)),
-        )
+    def move(kept, sent):
+        return kept, lax.ppermute(sent, "zh", [(0, 1), (1, 0)])
 
     def work(fields, partial, weights, **more):
         return collide(turn_flag, fields, weights, high, low, twiddle, partial, **more)
 
-    turn_flag = turn.reshape(1).astype(jnp.int32)
+    turn_flag = zh.reshape(1).astype(jnp.int32)
     partial = jnp.zeros((ROWS, PAIRS, LANES), jnp.float32)
     fence = lax.optimization_barrier
     early = [[(0, 0), (1, 0), (2, 0), (0, 1)]]
@@ -353,13 +344,13 @@
     zero = tuple(move(*zero))
     (rest,) = arrange(side, parts, late, False)
     rest = spread(rest)
-    zero, rest, weights = fence((zero, rest, settle(weights, zero, 50.0)))
+    zero, rest, weights = fence((zero, rest, settle(weights, zero[1:], 50.0)))
     one = cut(rest, 0, 4 * len(late[0]))
     two = cut(rest, 4 * len(late[0]), 4 * len(late[1]))
     one = tuple(move(*one))
     two = tuple(move(*two))
     zero = spread(jnp.stack(zero, 1))
-    one, zero, weights = fence((one, zero, settle(weights, one, 50.0)))
+    one, zero, weights = fence((one, zero, settle(weights, one[1:], 50.0)))
     partial, sigma = work([zero], partial, weights, spilled=True)
     (partial,) = work(one, partial, weights, older=(zero, sigma))
     partial, two = fence((partial, two))

time: 155 us -> 156 us (level)
  blocking collectives: 28.8 us -> 44.5 us
  waiting for transfers between devices: 66.8 us -> 55.5 us
  starting transfers between devices: 27.8 us -> 23.8 us
    ppermute x6 -> x3, waiting for transfers between devices: 60.5 us -> 22.7 us  [move(): return (kept, lax.ppermute(sent, 'zh', [(0, 1), (1, 0)]))]
    all_to_all x2, waiting for transfers between devices: 6.24 us -> 32.8 us  [spread(): return lax.all_to_all(value, ('y', 'x'), split_axis=0, concat_axis=0)]
    all_to_all x1, blocking collectives: 9.52 us -> 26.8 us  [spread(): return lax.all_to_all(value, ('y', 'x'), split_axis=0, concat_axis=0)]
    all_to_all x2, starting transfers between devices: 13.5 us -> 10.5 us  [spread(): return lax.all_to_all(value, ('y', 'x'), split_axis=0, concat_axis=0)]
    all_to_all x1, blocking collectives: 19.2 us -> 17.6 us  [per_device(): lax.all_to_all(shares, ('zh', 'zl', 'core'), split_axis=0, concat_axis=0)]
    ppermute x6 -> x3, starting transfers between devices: 14.3 us -> 13.3 us  [move(): return (kept, lax.ppermute(sent, 'zh', [(0, 1), (1, 0)]))]
    unnamed x14 -> x20, local copies, waits for them, and re-layouts: 5.64 us -> 6.64 us
  transfers between devices with their start and end apart: 8 -> 5, of which waited for: 5 -> 4; matrix products, arithmetic and copies ran while one was open for 2% -> 2% of each run, Pallas kernels for 7% -> 7%
where the time goes in v10:
time: 156 us; the launch traced here: 155 us
  waiting for transfers between devices  55.5 us (36%)
  blocking collectives  44.5 us (29%)
  starting transfers between devices  23.8 us (15%)
  Pallas kernels  20 us (13%)
  local copies, waits for them, and re-layouts  7.72 us (5%)
  other arithmetic  2.98 us (2%)
    all_to_all x2, waiting for transfers between devices, spread(): return lax.all_to_all(value, ('y', 'x'), split_axis=0, concat_axis=0)  32.8 us
    all_to_all x1, blocking collectives, spread(): return lax.all_to_all(value, ('y', 'x'), split_axis=0, concat_axis=0)  26.8 us
    ppermute x3, waiting for transfers between devices, move(): return (kept, lax.ppermute(sent, 'zh', [(0, 1), (1, 0)]))  22.7 us
    all_to_all x1, blocking collectives, per_device(): lax.all_to_all(shares, ('zh', 'zl', 'core'), split_axis=0, concat_axis=0)  17.6 us
    pallas_call x3, Pallas kernels, collide(): pl.pallas_call(functools.partial(kernel, count, stacked, joined, spilled)...  16.6 us
    ppermute x3, starting transfers between devices, move(): return (kept, lax.ppermute(sent, 'zh', [(0, 1), (1, 0)]))  13.3 us
    all_to_all x2, starting transfers between devices, spread(): return lax.all_to_all(value, ('y', 'x'), split_axis=0, concat_axis=0)  10.5 us
    unnamed x20, local copies, waits for them, and re-layouts  6.64 us
  transfers between devices with their start and end apart: 5, of which 4 were waited for; matrix products, arithmetic and copies ran while one was open for 2% of the time, Pallas kernels for 7%

profile of v10, /device:TPU:1, one launch (start us, length us, event | category | flops | bytes accessed | tf_op | source)
XLA Modules:
  0.0 155.3 jit_solution(4481973035300254875)
XLA Ops:
  0.0 0.0 copy-start
  0.0 2.3 %copy-done = f32[2,2,3,3,256,128]{5,4,3,2,1,0:T(8,128)S(1)} copy-done((f32[2,2,3,3,256,128]{5,4,3,2,1,0:T(8,128)S(1)}, f32[2,2,3,3,256,128]{5,4,3,2,1,0:T(8,128)}, u32[]{:S(2)}) %copy-start) | copy-done | bytes 4718616
  2.3 1.6 %shard_map.55 = (f32[16,16,8,128]{3,2,1,0:T(8,128)S(1)}, f32[16,16,8,128]{3,2,1,0:T(8,128)}) custom-call(s32[1]{0:T(128)} %bitcast.first.turn, f32[12,3,2,16,8,128]{5,4,3,2,1,0:T(8,128)S(1)} %bitcast.33), custom_call_target="tpu_custom_call" | custom-call | bytes 3200000 | tf_op jit(solution)/shard_map/pallas_call | solution.py:262
  3.9 0.0 copy-start.2
  3.9 1.0 copy-done.2
  4.9 7.7 %collective-permute-start = (f32[16,16,8,128]{3,2,1,0:T(8,128)}, f32[16,16,8,128]{3,2,1,0:T(8,128)}, u32[]{:S(2)}, u32[]{:S(2)}) collective-permute-start(f32[16,16,8,128]{3,2,1,0:T(8,128)} %get-tuple-element.30), channel_id=1, source_target_pairs={{0,32},{32,0},{1,33},{33,1},{2,34},{34,2},{3,35},{35,3},{4,36},{36... | collective-permute-start | bytes 3145736 | tf_op jit(solution)/shard_map/ppermute | solution.py:330
  12.6 0.8 shard_map.56
  13.4 0.0 copy-start.1
  13.4 1.5 copy-done.1
  14.9 6.8 %all-to-all-start = ((f32[16,2,20,8,128]{4,3,2,1,0:T(8,128)}), f32[16,2,20,8,128]{4,3,2,1,0:T(8,128)S(1)}, u32[]{:S(2)}, u32[]{:S(2)}) async-start(f32[16,2,20,8,128]{4,3,2,1,0:T(8,128)} %copy-done.1), calls=%async_computation | async-start | bytes 5242880 | tf_op jit(solution)/shard_map/all_to_all | solution.py:327
  22.4 18.9 %collective-permute-done.refs_0_ = f32[16,16,8,128]{3,2,1,0:T(8,128)} collective-permute-done((f32[16,16,8,128]{3,2,1,0:T(8,128)}, f32[16,16,8,128]{3,2,1,0:T(8,128)}, u32[]{:S(2)}, u32[]{:S(2)}) %collective-permute-start) | collective-permute-done | bytes 1048608 | tf_op jit(solution)/shard_map/ppermute | solution.py:330
  41.3 0.1 broadcast_in_dim.19.given
  41.4 18.1 %all-to-all-done.whole = f32[16,2,20,8,128]{4,3,2,1,0:T(8,128)S(1)} async-done(((f32[16,2,20,8,128]{4,3,2,1,0:T(8,128)}), f32[16,2,20,8,128]{4,3,2,1,0:T(8,128)S(1)}, u32[]{:S(2)}, u32[]{:S(2)}) %all-to-all-start) | async-done | bytes 2621472 | tf_op jit(solution)/shard_map/all_to_all | solution.py:327
  59.5 0.0 copy-start.3
  59.5 0.9 shard_map.58
  60.4 1.2 collective-permute-start.1
  61.6 0.1 shard_map.62
  61.7 0.0 copy-start.7
  61.7 0.9 copy-done.7
  62.6 0.0 copy-start.9
  62.6 0.9 copy-done.9
  63.5 0.0 copy-done.3
  63.5 2.8 %pad_maximum_fusion = f32[16,2,16,8,128]{4,3,2,1,0:T(8,128)} fusion(f32[16,1,16,8,128]{4,3,2,1,0:T(8,128)} %bitcast.4, f32[16,1,16,8,128]{4,3,2,1,0:T(8,128)S(1)} %bitcast.35), kind=kLoop, calls=%fused_computation | loop fusion | flops 524288 | bytes 4194304 | tf_op jit(solution)/shard_map/stack | solution.py:352
  66.3 3.7 %all-to-all-start.1 = ((f32[16,2,16,8,128]{4,3,2,1,0:T(8,128)}), f32[16,2,16,8,128]{4,3,2,1,0:T(8,128)S(1)}, u32[]{:S(2)}, u32[]{:S(2)}) async-start(f32[16,2,16,8,128]{4,3,2,1,0:T(8,128)} %pad_maximum_fusion), calls=%async_computation.1 | async-start | bytes 4194304 | tf_op jit(solution)/shard_map/all_to_all | solution.py:327
  70.0 0.0 copy-start.4
  70.1 0.0 copy-start.5
  70.1 0.0 copy-start.6
  70.1 4.3 %collective-permute-start.2 = (f32[16,12,8,128]{3,2,1,0:T(8,128)}, f32[16,12,8,128]{3,2,1,0:T(8,128)}, u32[]{:S(2)}, u32[]{:S(2)}) collective-permute-start(f32[16,12,8,128]{3,2,1,0:T(8,128)} %copy-done.9), channel_id=1, source_target_pairs={{0,32},{32,0},{1,33},{33,1},{2,34},{34,2},{3,35},{35,3},{4,36},{36... | collective-permute-start | bytes 2359304 | tf_op jit(solution)/shard_map/ppermute | solution.py:330
  74.4 3.8 %collective-permute-done.1.refs_0_.refs_1_ = f32[16,8,8,128]{3,2,1,0:T(8,128)} collective-permute-done((f32[16,8,8,128]{3,2,1,0:T(8,128)}, f32[16,8,8,128]{3,2,1,0:T(8,128)}, u32[]{:S(2)}, u32[]{:S(2)}) %collective-permute-start.1) | collective-permute-done | bytes 524320 | tf_op jit(solution)/shard_map/ppermute | solution.py:330
  78.2 14.7 %all-to-all-done.1.refs_0_.refs_2_ = f32[16,2,16,8,128]{4,3,2,1,0:T(8,128)S(1)} async-done(((f32[16,2,16,8,128]{4,3,2,1,0:T(8,128)}), f32[16,2,16,8,128]{4,3,2,1,0:T(8,128)S(1)}, u32[]{:S(2)}, u32[]{:S(2)}) %all-to-all-start.1) | async-done | bytes 2097184 | tf_op jit(solution)/shard_map/all_to_all | solution.py:327
  92.9 0.0 copy-done.4
  92.9 0.0 copy-done.5
  92.9 0.0 copy-done.6
  92.9 6.1 %shard_map.60 = (f32[32,9,128]{2,1,0:T(8,128)S(1)}, f32[32,16,256]{2,1,0:T(8,128)S(1)}) custom-call(s32[1]{0:T(128)} %bitcast.first.turn, f32[16,2,16,8,128]{4,3,2,1,0:T(8,128)S(1)} %all-to-all-done.1.refs_0_.refs_2_, f32[8,128]{1,0:T(8,128)S(1)} %shard_map.59.refs_1_.refs_4_.refs_2_, bf16[256,256]{1,0:T(8,128)(2,1)S(1)} %copy-done.5, ...), custom_call_target="tpu_custom_call" | custom-call | flops 1000000000 | tf_op jit(solution)/shard_map/pallas_call | solution.py:227
  99.1 0.0 copy-start.8
  99.1 4.6 %shard_map.61.refs_6_ = f32[32,9,128]{2,1,0:T(8,128)S(1)} custom-call(s32[1]{0:T(128)} %bitcast.first.turn, f32[16,8,8,128]{3,2,1,0:T(8,128)S(1)} %get-tuple-element.38.refs_0_, f32[16,8,8,128]{3,2,1,0:T(8,128)} %collective-permute-done.1.refs_0_.refs_1_, f32[16,2,16,8,128]{4,3,2,1,0:T(8,128)S(1)} %all-to-all-done.1.refs_0_.refs_2_, ...), custom_call_target="tpu_custom_call" | custom-call | flops 1000000000 | tf_op jit(solution)/shard_map/pallas_call | solution.py:227
  103.7 0.0 collective-permute-done.2.refs_1_
  103.7 0.0 copy-done.8
  103.7 5.9 %shard_map.63 = f32[32,9,128]{2,1,0:T(8,128)S(1)} custom-call(s32[1]{0:T(128)} %bitcast.first.turn, f32[16,12,8,128]{3,2,1,0:T(8,128)S(1)} %copy-done.8, f32[16,12,8,128]{3,2,1,0:T(8,128)} %collective-permute-done.2.refs_1_, f32[8,128]{1,0:T(8,128)S(1)} %shard_map.59.refs_1_.refs_4_.refs_2_, bf16[256,256]{1,0:T(8,128)(2,1)S(1)} %copy-done.5, ...), custom_call_target="tpu_custom_call" | custom-call | flops 1000000000 | tf_op jit(solution)/shard_map/pallas_call | solution.py:227
  109.6 0.1 copy.9
  109.7 26.8 %all_to_all.20 = f32[16,2,9,128]{3,1,2,0:T(2,128)S(1)} all-to-all(f32[16,2,9,128]{3,1,2,0:T(2,128)S(1)} %copy.9), channel_id=1, replica_groups=mesh['y'=4,'zh'=2,'x'=4,'zl'=4,'core'=2] {'y','x'}, dimensions={0} | all-to-all | bytes 294912 | tf_op jit(solution)/shard_map/all_to_all | solution.py:327
  136.5 0.1 reduce_sum.18
  136.6 0.1 reshape.69
  136.7 0.1 reshape.72
  136.8 17.6 %all_to_all.21 = f32[16,1,144]{2,1,0:T(1,128)S(1)} all-to-all(f32[16,1,144]{2,1,0:T(1,128)S(1)} %reshape.72), channel_id=1, replica_groups=mesh['y'=4,'zh'=2,'x'=4,'zl'=4,'core'=2] {'zh','zl','core'}, dimensions={0} | all-to-all | bytes 18432 | tf_op jit(solution)/shard_map/all_to_all | solution.py:362
  154.5 0.1 negate_bitcast_fusion
  154.6 0.1 stack.18
  154.6 0.6 copy.14
  (8 shorter events, 0.1 us)
Async XLA Ops:
  0.0 2.3 %copy-start = (f32[2,2,3,3,256,128]{5,4,3,2,1,0:T(8,128)S(1)}, f32[2,2,3,3,256,128]{5,4,3,2,1,0:T(8,128)}, u32[]{:S(2)}) copy-start(f32[2,2,3,3,256,128]{5,4,3,2,1,0:T(8,128)} %param.5) | copy-start | bytes 14155780
  3.9 1.0 copy-start.2
  4.9 36.4 %collective-permute-start = (f32[16,16,8,128]{3,2,1,0:T(8,128)}, f32[16,16,8,128]{3,2,1,0:T(8,128)}, u32[]{:S(2)}, u32[]{:S(2)}) collective-permute-start(f32[16,16,8,128]{3,2,1,0:T(8,128)} %get-tuple-element.30), channel_id=1, source_target_pairs={{0,32},{32,0},{1,33},{33,1},{2,34},{34,2},{3,35},{35,3},{4,36},{36... | collective-permute-start | bytes 3145736 | tf_op jit(solution)/shard_map/ppermute | solution.py:330
  13.4 1.5 copy-start.1
  14.9 44.5 %all-to-all-start = ((f32[16,2,20,8,128]{4,3,2,1,0:T(8,128)}), f32[16,2,20,8,128]{4,3,2,1,0:T(8,128)S(1)}, u32[]{:S(2)}, u32[]{:S(2)}) async-start(f32[16,2,20,8,128]{4,3,2,1,0:T(8,128)} %copy-done.1), calls=%async_computation | async-start | bytes 5242880 | tf_op jit(solution)/shard_map/all_to_all | solution.py:327
  59.5 4.1 %copy-start.3 = (f32[16,16,8,128]{3,2,1,0:T(8,128)S(1)}, f32[16,16,8,128]{3,2,1,0:T(8,128)}, u32[]{:S(2)}) copy-start(f32[16,16,8,128]{3,2,1,0:T(8,128)} %copy-done.2) | copy-start | bytes 3145732
  60.4 17.8 %collective-permute-start.1 = (f32[16,8,8,128]{3,2,1,0:T(8,128)}, f32[16,8,8,128]{3,2,1,0:T(8,128)}, u32[]{:S(2)}, u32[]{:S(2)}) collective-permute-start(f32[16,8,8,128]{3,2,1,0:T(8,128)} %get-tuple-element.34), channel_id=1, source_target_pairs={{0,32},{32,0},{1,33},{33,1},{2,34},{34,2},{3,35},{35,3},{4,36},{36... | collective-permute-start | bytes 1572872 | tf_op jit(solution)/shard_map/ppermute | solution.py:330
  61.7 0.9 copy-start.7
  62.6 0.9 copy-start.9
  66.3 26.6 %all-to-all-start.1 = ((f32[16,2,16,8,128]{4,3,2,1,0:T(8,128)}), f32[16,2,16,8,128]{4,3,2,1,0:T(8,128)S(1)}, u32[]{:S(2)}, u32[]{:S(2)}) async-start(f32[16,2,16,8,128]{4,3,2,1,0:T(8,128)} %pad_maximum_fusion), calls=%async_computation.1 | async-start | bytes 4194304 | tf_op jit(solution)/shard_map/all_to_all | solution.py:327
  70.0 22.9 %copy-start.4 = (bf16[256,256]{1,0:T(8,128)(2,1)S(1)}, bf16[256,256]{1,0:T(8,128)(2,1)}, u32[]{:S(2)}) copy-start(bf16[256,256]{1,0:T(8,128)(2,1)} %constant.75.clone.refs_3_.refs_6_.refs_4_) | copy-start | bytes 393220
  70.1 22.9 %copy-start.5 = (bf16[256,256]{1,0:T(8,128)(2,1)S(1)}, bf16[256,256]{1,0:T(8,128)(2,1)}, u32[]{:S(2)}) copy-start(bf16[256,256]{1,0:T(8,128)(2,1)} %constant.74.clone.refs_2_.refs_5_.refs_3_) | copy-start | bytes 393220
  70.1 22.9 %copy-start.6 = (f32[32,2,128]{2,1,0:T(2,128)S(1)}, f32[32,2,128]{2,1,0:T(2,128)}, u32[]{:S(2)}) copy-start(f32[32,2,128]{2,1,0:T(2,128)} %constant.76.clone.refs_4_.refs_7_.refs_5_) | copy-start | bytes 98308
  70.1 33.6 %collective-permute-start.2 = (f32[16,12,8,128]{3,2,1,0:T(8,128)}, f32[16,12,8,128]{3,2,1,0:T(8,128)}, u32[]{:S(2)}, u32[]{:S(2)}) collective-permute-start(f32[16,12,8,128]{3,2,1,0:T(8,128)} %copy-done.9), channel_id=1, source_target_pairs={{0,32},{32,0},{1,33},{33,1},{2,34},{34,2},{3,35},{35,3},{4,36},{36... | collective-permute-start | bytes 2359304 | tf_op jit(solution)/shard_map/ppermute | solution.py:330
  99.1 4.6 %copy-start.8 = (f32[16,12,8,128]{3,2,1,0:T(8,128)S(1)}, f32[16,12,8,128]{3,2,1,0:T(8,128)}, u32[]{:S(2)}) copy-start(f32[16,12,8,128]{3,2,1,0:T(8,128)} %copy-done.7) | copy-start | bytes 2359300

commit v11 on v10

--- a/solution.py
+++ b/solution.py
@@ -236,16 +236,15 @@
     )(turn, *inputs)
 
 
-def arrange_kernel(blocks, apart, first, parts, *refs):
-    *outs, sems = refs
+def arrange_kernel(blocks, ways, first, parts, out, sems):
     copies, base = [], 0
     for pairs in blocks:
         for kind in range(4):
             for i, (a, c) in enumerate(pairs):
                 at = base + kind * len(pairs) + i
-                for n in range(2):
-                    half = first[0] if n == 0 else 1 - first[0]
-                    target = outs[n].at[:, at] if apart else outs[0].at[:, n, at]
+                for n, way in enumerate(ways):
+                    half = first[0] if way == 0 else 1 - first[0]
+                    target = out.at[:, n, at] if len(ways) > 1 else out.at[:, at]
                     source = parts.at[kind * ORB + a, c, half]
                     copies.append(pltpu.make_async_copy(source, target, sems.at[n, at]))
         base += 4 * len(pairs)
@@ -255,17 +254,16 @@
         copy.wait()
 
 
-def arrange(first, parts, blocks, apart):
+def arrange(first, parts, blocks, ways):
     count = 4 * sum(len(pairs) for pairs in blocks)
-    whole = (PLANE, count, SLOTS, LANES) if apart else (PLANE, 2, count, SLOTS, LANES)
-    shape = jax.ShapeDtypeStruct(whole, jnp.float32)
+    shape = (PLANE, *((len(ways),) if len(ways) > 1 else ()), count, SLOTS, LANES)
     return pl.pallas_call(
-        functools.partial(arrange_kernel, blocks, apart),
-        out_shape=[shape] * (2 if apart else 1),
+        functools.partial(arrange_kernel, blocks, ways),
+        out_shape=jax.ShapeDtypeStruct(shape, jnp.float32),
         in_specs=[pl.BlockSpec(memory_space=pltpu.SMEM), pl.BlockSpec(memory_space=pl.ANY)],
-        out_specs=[pl.BlockSpec(memory_space=pltpu.VMEM)] * (2 if apart else 1),
-        scratch_shapes=[pltpu.SemaphoreType.DMA((2, count))],
-        compiler_params=pltpu.CompilerParams(vmem_limit_bytes=8 * 1024 * 1024),
+        out_specs=pl.BlockSpec(memory_space=pltpu.VMEM),
+        scratch_shapes=[pltpu.SemaphoreType.DMA((len(ways), count))],
+        compiler_params=pltpu.CompilerParams(vmem_limit_bytes=60 * 1024 * 1024),
         cost_estimate=pl.CostEstimate(flops=0, bytes_accessed=3_200_000, transcendentals=0),
     )(first, parts)
 
@@ -326,8 +324,8 @@
     def spread(value):
         return lax.all_to_all(value, ("y", "x"), split_axis=0, concat_axis=0)
 
-    def move(kept, sent):
-        return kept, lax.ppermute(sent, "zh", [(0, 1), (1, 0)])
+    def move(value):
+        return lax.ppermute(value, "zh", [(0, 1), (1, 0)])
 
     def work(fields, partial, weights, **more):
         return collide(turn_flag, fields, weights, high, low, twiddle, partial, **more)
@@ -339,17 +337,18 @@
     late = [[(1, 1), (2, 1)], [(0, 2), (1, 2), (2, 2)]]
 
     side = zh.reshape(1).astype(jnp.int32)
-    zero = arrange(side, parts, early, True)
-    zero, side = fence((zero, side))
-    zero = tuple(move(*zero))
-    (rest,) = arrange(side, parts, late, False)
+    sent = arrange(side, parts, early, (1,))
+    sent, side = fence((sent, side))
+    landed = move(sent)
+    rest = arrange(side, parts, late, (0, 1))
     rest = spread(rest)
-    zero, rest, weights = fence((zero, rest, settle(weights, zero[1:], 50.0)))
+    kept = arrange(side, parts, early, (0,))
+    kept, weights = fence((kept, weights))
+    landed, rest, weights = fence((landed, rest, settle(weights, [landed], 50.0)))
     one = cut(rest, 0, 4 * len(late[0]))
     two = cut(rest, 4 * len(late[0]), 4 * len(late[1]))
-    one = tuple(move(*one))
-    two = tuple(move(*two))
-    zero = spread(jnp.stack(zero, 1))
+    one, two = (one[0], move(one[1])), (two[0], move(two[1]))
+    zero = spread(jnp.stack([kept, landed], 1))
     one, zero, weights = fence((one, zero, settle(weights, one[1:], 50.0)))
     partial, sigma = work([zero], partial, weights, spilled=True)
     (partial,) = work(one, partial, weights, older=(zero, sigma))

time: 156 us -> 156 us (level)
  Pallas kernels: 20 us -> 25.9 us
  local copies, waits for them, and re-layouts: 7.72 us -> 2.92 us
    pallas_call x2 -> x3, Pallas kernels: 2.34 us -> 8.27 us  [arrange(): pl.pallas_call(functools.partial(arrange_kernel, blocks, ways), out_shape...]
    unnamed x20 -> x14, local copies, waits for them, and re-layouts: 6.64 us -> 1.83 us
    ppermute x3, waiting for transfers between devices: 22.7 us -> 19.1 us  [move(): return lax.ppermute(value, 'zh', [(0, 1), (1, 0)])]
    all_to_all x2, waiting for transfers between devices: 32.8 us -> 35 us  [spread(): return lax.all_to_all(value, ('y', 'x'), split_axis=0, concat_axis=0)]
    all_to_all x1, blocking collectives: 17.6 us -> 15.6 us  [per_device(): lax.all_to_all(shares, ('zh', 'zl', 'core'), split_axis=0, concat_axis=0)]
    all_to_all x1, blocking collectives: 26.8 us -> 28.8 us  [spread(): return lax.all_to_all(value, ('y', 'x'), split_axis=0, concat_axis=0)]
  transfers between devices with their start and end apart: 5 -> 5, of which waited for: 4 -> 4; matrix products, arithmetic and copies ran while one was open for 2% -> 2% of each run, Pallas kernels for 7% -> 11%
where the time goes in v11:
time: 156 us; the launch traced here: 155 us
  waiting for transfers between devices  54.1 us (35%)
  blocking collectives  44.4 us (28%)
  Pallas kernels  25.9 us (17%)
  starting transfers between devices  23.9 us (15%)
  other arithmetic  3 us (2%)
  local copies, waits for them, and re-layouts  2.92 us (2%)
    all_to_all x2, waiting for transfers between devices, spread(): return lax.all_to_all(value, ('y', 'x'), split_axis=0, concat_axis=0)  35 us
    all_to_all x1, blocking collectives, spread(): return lax.all_to_all(value, ('y', 'x'), split_axis=0, concat_axis=0)  28.8 us
    ppermute x3, waiting for transfers between devices, move(): return lax.ppermute(value, 'zh', [(0, 1), (1, 0)])  19.1 us
    pallas_call x3, Pallas kernels, collide(): pl.pallas_call(functools.partial(kernel, count, stacked, joined, spilled)...  16.6 us
    all_to_all x1, blocking collectives, per_device(): lax.all_to_all(shares, ('zh', 'zl', 'core'), split_axis=0, concat_axis=0)  15.6 us
    ppermute x3, starting transfers between devices, move(): return lax.ppermute(value, 'zh', [(0, 1), (1, 0)])  13.4 us
    all_to_all x2, starting transfers between devices, spread(): return lax.all_to_all(value, ('y', 'x'), split_axis=0, concat_axis=0)  10.5 us
    pallas_call x3, Pallas kernels, arrange(): pl.pallas_call(functools.partial(arrange_kernel, blocks, ways), out_shape...  8.27 us
  transfers between devices with their start and end apart: 5, of which 4 were waited for; matrix products, arithmetic and copies ran while one was open for 2% of the time, Pallas kernels for 11%

profile of v11, /device:TPU:1, one launch (start us, length us, event | category | flops | bytes accessed | tf_op | source)
XLA Modules:
  0.0 155.1 jit_solution(10232132844298781537)
XLA Ops:
  0.0 2.3 %shard_map.55 = f32[16,16,8,128]{3,2,1,0:T(8,128)} custom-call(s32[1]{0:T(128)} %bitcast.first.turn, f32[12,3,2,16,8,128]{5,4,3,2,1,0:T(8,128)} %bitcast.34), custom_call_target="tpu_custom_call" | custom-call | bytes 3200000 | tf_op jit(solution)/shard_map/pallas_call | solution.py:260
  2.4 7.8 %collective-permute-start = (f32[16,16,8,128]{3,2,1,0:T(8,128)}, f32[16,16,8,128]{3,2,1,0:T(8,128)}, u32[]{:S(2)}, u32[]{:S(2)}) collective-permute-start(f32[16,16,8,128]{3,2,1,0:T(8,128)} %shard_map.55), channel_id=1, source_target_pairs={{0,32},{32,0},{1,33},{33,1},{2,34},{34,2},{3,35},{35,3},{4,36},{36... | collective-permute-start | bytes 3145736 | tf_op jit(solution)/shard_map/ppermute | solution.py:328
  10.2 3.6 %shard_map.56 = f32[16,2,20,8,128]{4,3,2,1,0:T(8,128)} custom-call(s32[1]{0:T(128)} %bitcast.first.turn, f32[12,3,2,16,8,128]{5,4,3,2,1,0:T(8,128)} %bitcast.35), custom_call_target="tpu_custom_call" | custom-call | bytes 3200000 | tf_op jit(solution)/shard_map/pallas_call | solution.py:260
  13.8 6.8 %all-to-all-start = ((f32[16,2,20,8,128]{4,3,2,1,0:T(8,128)}), f32[16,2,20,8,128]{4,3,2,1,0:T(8,128)S(1)}, u32[]{:S(2)}, u32[]{:S(2)}) async-start(f32[16,2,20,8,128]{4,3,2,1,0:T(8,128)} %shard_map.56), calls=%async_computation | async-start | bytes 5242880 | tf_op jit(solution)/shard_map/all_to_all | solution.py:325
  20.5 2.4 %shard_map.57 = f32[16,16,8,128]{3,2,1,0:T(8,128)} custom-call(s32[1]{0:T(128)} %bitcast.first.turn, f32[12,3,2,16,8,128]{5,4,3,2,1,0:T(8,128)} %bitcast.36), custom_call_target="tpu_custom_call" | custom-call | bytes 3200000 | tf_op jit(solution)/shard_map/pallas_call | solution.py:260
  23.6 0.1 broadcast_in_dim.19.given
  23.6 15.2 %collective-permute-done.refs_0_ = f32[16,16,8,128]{3,2,1,0:T(8,128)} collective-permute-done((f32[16,16,8,128]{3,2,1,0:T(8,128)}, f32[16,16,8,128]{3,2,1,0:T(8,128)}, u32[]{:S(2)}, u32[]{:S(2)}) %collective-permute-start) | collective-permute-done | bytes 1048608 | tf_op jit(solution)/shard_map/ppermute | solution.py:328
  38.8 19.5 %all-to-all-done.whole = f32[16,2,20,8,128]{4,3,2,1,0:T(8,128)S(1)} async-done(((f32[16,2,20,8,128]{4,3,2,1,0:T(8,128)}), f32[16,2,20,8,128]{4,3,2,1,0:T(8,128)S(1)}, u32[]{:S(2)}, u32[]{:S(2)}) %all-to-all-start) | async-done | bytes 2621472 | tf_op jit(solution)/shard_map/all_to_all | solution.py:325
  58.3 0.0 copy-start.6
  58.3 0.9 shard_map.59
  59.2 1.3 collective-permute-start.1
  60.4 0.1 shard_map.63
  60.6 0.0 copy-start.3
  60.6 0.9 copy-done.3
  61.5 0.0 copy-start.5
  61.5 0.9 copy-done.5
  62.4 0.0 copy-done.6
  62.4 2.8 %pad_maximum_fusion = f32[16,2,16,8,128]{4,3,2,1,0:T(8,128)} fusion(f32[16,1,16,8,128]{4,3,2,1,0:T(8,128)} %bitcast.4, f32[16,1,16,8,128]{4,3,2,1,0:T(8,128)S(1)} %bitcast.37), kind=kLoop, calls=%fused_computation | loop fusion | flops 524288 | bytes 4194304 | tf_op jit(solution)/shard_map/stack | solution.py:351
  65.2 3.7 %all-to-all-start.1 = ((f32[16,2,16,8,128]{4,3,2,1,0:T(8,128)}), f32[16,2,16,8,128]{4,3,2,1,0:T(8,128)S(1)}, u32[]{:S(2)}, u32[]{:S(2)}) async-start(f32[16,2,16,8,128]{4,3,2,1,0:T(8,128)} %pad_maximum_fusion), calls=%async_computation.1 | async-start | bytes 4194304 | tf_op jit(solution)/shard_map/all_to_all | solution.py:325
  68.9 0.0 copy-start
  68.9 0.0 copy-start.1
  68.9 0.0 copy-start.2
  69.0 4.3 %collective-permute-start.2 = (f32[16,12,8,128]{3,2,1,0:T(8,128)}, f32[16,12,8,128]{3,2,1,0:T(8,128)}, u32[]{:S(2)}, u32[]{:S(2)}) collective-permute-start(f32[16,12,8,128]{3,2,1,0:T(8,128)} %copy-done.5), channel_id=1, source_target_pairs={{0,32},{32,0},{1,33},{33,1},{2,34},{34,2},{3,35},{35,3},{4,36},{36... | collective-permute-start | bytes 2359304 | tf_op jit(solution)/shard_map/ppermute | solution.py:328
  73.2 3.9 %collective-permute-done.1.refs_0_.refs_1_ = f32[16,8,8,128]{3,2,1,0:T(8,128)} collective-permute-done((f32[16,8,8,128]{3,2,1,0:T(8,128)}, f32[16,8,8,128]{3,2,1,0:T(8,128)}, u32[]{:S(2)}, u32[]{:S(2)}) %collective-permute-start.1) | collective-permute-done | bytes 524320 | tf_op jit(solution)/shard_map/ppermute | solution.py:328
  77.2 15.6 %all-to-all-done.1.refs_0_.refs_2_ = f32[16,2,16,8,128]{4,3,2,1,0:T(8,128)S(1)} async-done(((f32[16,2,16,8,128]{4,3,2,1,0:T(8,128)}), f32[16,2,16,8,128]{4,3,2,1,0:T(8,128)S(1)}, u32[]{:S(2)}, u32[]{:S(2)}) %all-to-all-start.1) | async-done | bytes 2097184 | tf_op jit(solution)/shard_map/all_to_all | solution.py:325
  92.8 0.0 copy-done
  92.8 0.0 copy-done.1
  92.8 0.0 copy-done.2
  92.8 6.1 %shard_map.61 = (f32[32,9,128]{2,1,0:T(8,128)S(1)}, f32[32,16,256]{2,1,0:T(8,128)S(1)}) custom-call(s32[1]{0:T(128)} %bitcast.first.turn, f32[16,2,16,8,128]{4,3,2,1,0:T(8,128)S(1)} %all-to-all-done.1.refs_0_.refs_2_, f32[8,128]{1,0:T(8,128)S(1)} %shard_map.60.refs_1_.refs_4_.refs_2_, bf16[256,256]{1,0:T(8,128)(2,1)S(1)} %copy-done.1, ...), custom_call_target="tpu_custom_call" | custom-call | flops 1000000000 | tf_op jit(solution)/shard_map/pallas_call | solution.py:227
  98.9 0.0 copy-start.4
  98.9 4.6 %shard_map.62.refs_6_ = f32[32,9,128]{2,1,0:T(8,128)S(1)} custom-call(s32[1]{0:T(128)} %bitcast.first.turn, f32[16,8,8,128]{3,2,1,0:T(8,128)S(1)} %get-tuple-element.34.refs_0_, f32[16,8,8,128]{3,2,1,0:T(8,128)} %collective-permute-done.1.refs_0_.refs_1_, f32[16,2,16,8,128]{4,3,2,1,0:T(8,128)S(1)} %all-to-all-done.1.refs_0_.refs_2_, ...), custom_call_target="tpu_custom_call" | custom-call | flops 1000000000 | tf_op jit(solution)/shard_map/pallas_call | solution.py:227
  103.5 0.0 collective-permute-done.2.refs_1_
  103.6 0.0 copy-done.4
  103.6 5.9 %shard_map.64 = f32[32,9,128]{2,1,0:T(8,128)S(1)} custom-call(s32[1]{0:T(128)} %bitcast.first.turn, f32[16,12,8,128]{3,2,1,0:T(8,128)S(1)} %copy-done.4, f32[16,12,8,128]{3,2,1,0:T(8,128)} %collective-permute-done.2.refs_1_, f32[8,128]{1,0:T(8,128)S(1)} %shard_map.60.refs_1_.refs_4_.refs_2_, bf16[256,256]{1,0:T(8,128)(2,1)S(1)} %copy-done.1, ...), custom_call_target="tpu_custom_call" | custom-call | flops 1000000000 | tf_op jit(solution)/shard_map/pallas_call | solution.py:227
  109.5 0.1 copy.9
  109.5 28.8 %all_to_all.20 = f32[16,2,9,128]{3,1,2,0:T(2,128)S(1)} all-to-all(f32[16,2,9,128]{3,1,2,0:T(2,128)S(1)} %copy.9), channel_id=1, replica_groups=mesh['y'=4,'zh'=2,'x'=4,'zl'=4,'core'=2] {'y','x'}, dimensions={0} | all-to-all | bytes 294912 | tf_op jit(solution)/shard_map/all_to_all | solution.py:325
  138.3 0.1 reduce_sum.18
  138.4 0.1 reshape.69
  138.5 0.1 reshape.72
  138.6 15.6 %all_to_all.21 = f32[16,1,144]{2,1,0:T(1,128)S(1)} all-to-all(f32[16,1,144]{2,1,0:T(1,128)S(1)} %reshape.72), channel_id=1, replica_groups=mesh['y'=4,'zh'=2,'x'=4,'zl'=4,'core'=2] {'zh','zl','core'}, dimensions={0} | all-to-all | bytes 18432 | tf_op jit(solution)/shard_map/all_to_all | solution.py:361
  154.3 0.1 negate_bitcast_fusion
  154.4 0.1 stack.18
  154.5 0.6 copy.14
  (8 shorter events, 0.1 us)
Async XLA Ops:
  2.4 36.5 %collective-permute-start = (f32[16,16,8,128]{3,2,1,0:T(8,128)}, f32[16,16,8,128]{3,2,1,0:T(8,128)}, u32[]{:S(2)}, u32[]{:S(2)}) collective-permute-start(f32[16,16,8,128]{3,2,1,0:T(8,128)} %shard_map.55), channel_id=1, source_target_pairs={{0,32},{32,0},{1,33},{33,1},{2,34},{34,2},{3,35},{35,3},{4,36},{36... | collective-permute-start | bytes 3145736 | tf_op jit(solution)/shard_map/ppermute | solution.py:328
  13.8 44.5 %all-to-all-start = ((f32[16,2,20,8,128]{4,3,2,1,0:T(8,128)}), f32[16,2,20,8,128]{4,3,2,1,0:T(8,128)S(1)}, u32[]{:S(2)}, u32[]{:S(2)}) async-start(f32[16,2,20,8,128]{4,3,2,1,0:T(8,128)} %shard_map.56), calls=%async_computation | async-start | bytes 5242880 | tf_op jit(solution)/shard_map/all_to_all | solution.py:325
  58.3 4.1 %copy-start.6 = (f32[16,16,8,128]{3,2,1,0:T(8,128)S(1)}, f32[16,16,8,128]{3,2,1,0:T(8,128)}, u32[]{:S(2)}) copy-start(f32[16,16,8,128]{3,2,1,0:T(8,128)} %shard_map.57) | copy-start | bytes 3145732
  59.2 18.0 %collective-permute-start.1 = (f32[16,8,8,128]{3,2,1,0:T(8,128)}, f32[16,8,8,128]{3,2,1,0:T(8,128)}, u32[]{:S(2)}, u32[]{:S(2)}) collective-permute-start(f32[16,8,8,128]{3,2,1,0:T(8,128)} %get-tuple-element.30), channel_id=1, source_target_pairs={{0,32},{32,0},{1,33},{33,1},{2,34},{34,2},{3,35},{35,3},{4,36},{36... | collective-permute-start | bytes 1572872 | tf_op jit(solution)/shard_map/ppermute | solution.py:328
  60.6 0.9 copy-start.3
  61.5 0.9 copy-start.5
  65.2 27.6 %all-to-all-start.1 = ((f32[16,2,16,8,128]{4,3,2,1,0:T(8,128)}), f32[16,2,16,8,128]{4,3,2,1,0:T(8,128)S(1)}, u32[]{:S(2)}, u32[]{:S(2)}) async-start(f32[16,2,16,8,128]{4,3,2,1,0:T(8,128)} %pad_maximum_fusion), calls=%async_computation.1 | async-start | bytes 4194304 | tf_op jit(solution)/shard_map/all_to_all | solution.py:325
  68.9 23.9 %copy-start = (bf16[256,256]{1,0:T(8,128)(2,1)S(1)}, bf16[256,256]{1,0:T(8,128)(2,1)}, u32[]{:S(2)}) copy-start(bf16[256,256]{1,0:T(8,128)(2,1)} %constant.75.clone.refs_3_.refs_6_.refs_4_) | copy-start | bytes 393220
  68.9 23.9 %copy-start.1 = (bf16[256,256]{1,0:T(8,128)(2,1)S(1)}, bf16[256,256]{1,0:T(8,128)(2,1)}, u32[]{:S(2)}) copy-start(bf16[256,256]{1,0:T(8,128)(2,1)} %constant.74.clone.refs_2_.refs_5_.refs_3_) | copy-start | bytes 393220
  68.9 23.8 %copy-start.2 = (f32[32,2,128]{2,1,0:T(2,128)S(1)}, f32[32,2,128]{2,1,0:T(2,128)}, u32[]{:S(2)}) copy-start(f32[32,2,128]{2,1,0:T(2,128)} %constant.76.clone.refs_4_.refs_7_.refs_5_) | copy-start | bytes 98308
  69.0 34.6 %collective-permute-start.2 = (f32[16,12,8,128]{3,2,1,0:T(8,128)}, f32[16,12,8,128]{3,2,1,0:T(8,128)}, u32[]{:S(2)}, u32[]{:S(2)}) collective-permute-start(f32[16,12,8,128]{3,2,1,0:T(8,128)} %copy-done.5), channel_id=1, source_target_pairs={{0,32},{32,0},{1,33},{33,1},{2,34},{34,2},{3,35},{35,3},{4,36},{36... | collective-permute-start | bytes 2359304 | tf_op jit(solution)/shard_map/ppermute | solution.py:328
  98.9 4.6 %copy-start.4 = (f32[16,12,8,128]{3,2,1,0:T(8,128)S(1)}, f32[16,12,8,128]{3,2,1,0:T(8,128)}, u32[]{:S(2)}) copy-start(f32[16,12,8,128]{3,2,1,0:T(8,128)} %copy-done.3) | copy-start | bytes 2359300

commit v12 on v11

--- a/solution.py
+++ b/solution.py
@@ -108,8 +108,9 @@
     field = refs[-1]
 
     def pair_of(source, plane, pairs, comp, pair):
-        at = comp * 2 * pairs + pair
-        return source[plane, at], source[plane, at + pairs]
+        size = 2 if pairs == ORB + 1 else pairs
+        at = pair // size * 4 * size + 2 * comp * size + pair % size
+        return source[plane, at], source[plane, at + size]
 
     def either_way(act, *sides):
         pl.when(turn[0] == 0)(lambda: act(*sides))
@@ -268,6 +269,31 @@
     )(first, parts)
 
 
+def join_kernel(kept, ahead, landed, out, sems):
+    first = ahead.shape[1]
+    copies = [
+        pltpu.make_async_copy(kept, out.at[:, 0], sems.at[0]),
+        pltpu.make_async_copy(ahead, out.at[:, 1, pl.ds(0, first)], sems.at[1]),
+        pltpu.make_async_copy(landed, out.at[:, 1, pl.ds(first, landed.shape[1])], sems.at[2]),
+    ]
+    for copy in copies:
+        copy.start()
+    for copy in copies:
+        copy.wait()
+
+
+def join(kept, ahead, landed):
+    return pl.pallas_call(
+        join_kernel,
+        out_shape=jax.ShapeDtypeStruct((PLANE, 2, *kept.shape[1:]), jnp.float32),
+        in_specs=[pl.BlockSpec(memory_space=pl.ANY)] * 3,
+        out_specs=pl.BlockSpec(memory_space=pltpu.VMEM),
+        scratch_shapes=[pltpu.SemaphoreType.DMA((3,))],
+        compiler_params=pltpu.CompilerParams(vmem_limit_bytes=8 * 1024 * 1024),
+        cost_estimate=pl.CostEstimate(flops=0, bytes_accessed=3_200_000, transcendentals=0),
+    )(kept, ahead, landed)
+
+
 def cut_kernel(base, whole, *refs):
     *outs, sems = refs
     copies = []
@@ -333,22 +359,24 @@
     turn_flag = zh.reshape(1).astype(jnp.int32)
     partial = jnp.zeros((ROWS, PAIRS, LANES), jnp.float32)
     fence = lax.optimization_barrier
-    early = [[(0, 0), (1, 0), (2, 0), (0, 1)]]
+    early = [[(0, 0), (1, 0)], [(2, 0), (0, 1)]]
     late = [[(1, 1), (2, 1)], [(0, 2), (1, 2), (2, 2)]]
 
     side = zh.reshape(1).astype(jnp.int32)
-    sent = arrange(side, parts, early, (1,))
+    ahead = arrange(side, parts, early[:1], (1,))
+    ahead, side = fence((ahead, side))
+    sent = arrange(side, parts, early[1:], (1,))
     sent, side = fence((sent, side))
-    landed = move(sent)
+    ahead, landed = move(ahead), move(sent)
     rest = arrange(side, parts, late, (0, 1))
     rest = spread(rest)
     kept = arrange(side, parts, early, (0,))
     kept, weights = fence((kept, weights))
-    landed, rest, weights = fence((landed, rest, settle(weights, [landed], 50.0)))
+    ahead, rest, weights = fence((ahead, rest, settle(weights, [ahead], 50.0)))
     one = cut(rest, 0, 4 * len(late[0]))
     two = cut(rest, 4 * len(late[0]), 4 * len(late[1]))
     one, two = (one[0], move(one[1])), (two[0], move(two[1]))
-    zero = spread(jnp.stack([kept, landed], 1))
+    zero = spread(join(kept, ahead, landed))
     one, zero, weights = fence((one, zero, settle(weights, one[1:], 50.0)))
     partial, sigma = work([zero], partial, weights, spilled=True)
     (partial,) = work(one, partial, weights, older=(zero, sigma))

time: 156 us -> 158 us (1.013)
  waiting for transfers between devices: 54.1 us -> 61.5 us
  blocking collectives: 44.4 us -> 37.6 us
  Pallas kernels: 25.9 us -> 29.6 us
  other arithmetic: 3 us -> 0.19 us
    all_to_all x2, waiting for transfers between devices: 35 us -> 55.8 us  [spread(): return lax.all_to_all(value, ('y', 'x'), split_axis=0, concat_axis=0)]
    ppermute x3 -> x4, waiting for transfers between devices: 19.1 us -> 5.72 us  [move(): return lax.ppermute(value, 'zh', [(0, 1), (1, 0)])]
    all_to_all x1, blocking collectives: 28.8 us -> 21.5 us  [spread(): return lax.all_to_all(value, ('y', 'x'), split_axis=0, concat_axis=0)]
    another operation x1 -> x0, other arithmetic: 2.8 us -> none  [per_device(): zero = spread(jnp.stack([kept, landed], 1))]
    pallas_call x3 -> x4, Pallas kernels: 8.27 us -> 9.81 us  [arrange(): pl.pallas_call(functools.partial(arrange_kernel, blocks, ways), out_shape...]
    ppermute x3 -> x4, starting transfers between devices: 13.4 us -> 12.5 us  [move(): return lax.ppermute(value, 'zh', [(0, 1), (1, 0)])]
  transfers between devices with their start and end apart: 5 -> 6, of which waited for: 4 -> 3; matrix products, arithmetic and copies ran while one was open for 2% -> 0% of each run, Pallas kernels for 11% -> 14%
where the time goes in v12:
time: 158 us
  waiting for transfers between devices  61.5 us (39%)
  blocking collectives  37.6 us (24%)
  Pallas kernels  29.6 us (19%)
  starting transfers between devices  23.9 us (15%)
  local copies, waits for them, and re-layouts  4.12 us (3%)
    all_to_all x2, waiting for transfers between devices, spread(): return lax.all_to_all(value, ('y', 'x'), split_axis=0, concat_axis=0)  55.8 us
    all_to_all x1, blocking collectives, spread(): return lax.all_to_all(value, ('y', 'x'), split_axis=0, concat_axis=0)  21.5 us
    pallas_call x3, Pallas kernels, collide(): pl.pallas_call(functools.partial(kernel, count, stacked, joined, spilled)...  16.7 us
    all_to_all x1, blocking collectives, per_device(): lax.all_to_all(shares, ('zh', 'zl', 'core'), split_axis=0, concat_axis=0)  16.1 us
    ppermute x4, starting transfers between devices, move(): return lax.ppermute(value, 'zh', [(0, 1), (1, 0)])  12.5 us
    all_to_all x2, starting transfers between devices, spread(): return lax.all_to_all(value, ('y', 'x'), split_axis=0, concat_axis=0)  11.3 us
    pallas_call x4, Pallas kernels, arrange(): pl.pallas_call(functools.partial(arrange_kernel, blocks, ways), out_shape...  9.81 us
    ppermute x4, waiting for transfers between devices, move(): return lax.ppermute(value, 'zh', [(0, 1), (1, 0)])  5.72 us
  transfers between devices with their start and end apart: 6, of which 3 were waited for; matrix products, arithmetic and copies ran while one was open for 0% of the time, Pallas kernels for 14%

profile of v12, /device:TPU:1, one launch (start us, length us, event | category | flops | bytes accessed | tf_op | source)
XLA Modules:
  0.0 157.8 jit_solution(819397084077176505)
XLA Ops:
  0.0 1.9 %shard_map.55 = f32[16,8,8,128]{3,2,1,0:T(8,128)} custom-call(s32[1]{0:T(128)} %bitcast.first.turn, f32[12,3,2,16,8,128]{5,4,3,2,1,0:T(8,128)} %bitcast.32), custom_call_target="tpu_custom_call" | custom-call | bytes 3200000 | tf_op jit(solution)/shard_map/pallas_call | solution.py:261
  1.9 7.8 %collective-permute-start = (f32[16,8,8,128]{3,2,1,0:T(8,128)}, f32[16,8,8,128]{3,2,1,0:T(8,128)S(1)}, u32[]{:S(2)}, u32[]{:S(2)}) collective-permute-start(f32[16,8,8,128]{3,2,1,0:T(8,128)} %shard_map.55), channel_id=1, source_target_pairs={{0,32},{32,0},{1,33},{33,1},{2,34},{34,2},{3,35},{35,3},{4,36},{36... | collective-permute-start | bytes 1572872 | tf_op jit(solution)/shard_map/ppermute | solution.py:354
  9.8 1.9 %shard_map.56 = f32[16,8,8,128]{3,2,1,0:T(8,128)} custom-call(s32[1]{0:T(128)} %bitcast.first.turn, f32[12,3,2,16,8,128]{5,4,3,2,1,0:T(8,128)} %bitcast.33), custom_call_target="tpu_custom_call" | custom-call | bytes 3200000 | tf_op jit(solution)/shard_map/pallas_call | solution.py:261
  11.7 0.1 collective-permute-start.2
  11.8 3.6 %shard_map.57 = f32[16,2,20,8,128]{4,3,2,1,0:T(8,128)} custom-call(s32[1]{0:T(128)} %bitcast.first.turn, f32[12,3,2,16,8,128]{5,4,3,2,1,0:T(8,128)} %bitcast.34), custom_call_target="tpu_custom_call" | custom-call | bytes 3200000 | tf_op jit(solution)/shard_map/pallas_call | solution.py:261
  15.4 6.8 %all-to-all-start = ((f32[16,2,20,8,128]{4,3,2,1,0:T(8,128)}), f32[16,2,20,8,128]{4,3,2,1,0:T(8,128)S(1)}, u32[]{:S(2)}, u32[]{:S(2)}) async-start(f32[16,2,20,8,128]{4,3,2,1,0:T(8,128)} %shard_map.57), calls=%async_computation | async-start | bytes 5242880 | tf_op jit(solution)/shard_map/all_to_all | solution.py:351
  22.2 2.4 %shard_map.58.kept = f32[16,16,8,128]{3,2,1,0:T(8,128)} custom-call(s32[1]{0:T(128)} %bitcast.first.turn, f32[12,3,2,16,8,128]{5,4,3,2,1,0:T(8,128)} %bitcast.35), custom_call_target="tpu_custom_call" | custom-call | bytes 3200000 | tf_op jit(solution)/shard_map/pallas_call | solution.py:261
  25.2 0.1 broadcast_in_dim.19.given
  25.3 0.0 collective-permute-done.refs_0_.ahead
  25.3 34.6 %all-to-all-done.whole = f32[16,2,20,8,128]{4,3,2,1,0:T(8,128)S(1)} async-done(((f32[16,2,20,8,128]{4,3,2,1,0:T(8,128)}), f32[16,2,20,8,128]{4,3,2,1,0:T(8,128)S(1)}, u32[]{:S(2)}, u32[]{:S(2)}) %all-to-all-start) | async-done | bytes 2621472 | tf_op jit(solution)/shard_map/all_to_all | solution.py:351
  59.9 0.0 copy-start.1
  59.9 0.9 shard_map.60
  60.8 0.0 copy-start.2
  60.8 0.8 copy-done.2
  61.6 4.3 %collective-permute-start.1 = (f32[16,8,8,128]{3,2,1,0:T(8,128)}, f32[16,8,8,128]{3,2,1,0:T(8,128)}, u32[]{:S(2)}, u32[]{:S(2)}) collective-permute-start(f32[16,8,8,128]{3,2,1,0:T(8,128)} %get-tuple-element.33), channel_id=1, source_target_pairs={{0,32},{32,0},{1,33},{33,1},{2,34},{34,2},{3,35},{35,3},{4,36},{36... | collective-permute-start | bytes 1572872 | tf_op jit(solution)/shard_map/ppermute | solution.py:354
  66.0 1.0 shard_map.65
  67.0 0.0 copy-start.7
  67.0 0.9 copy-done.7
  67.9 0.0 collective-permute-done.2.landed
  67.9 0.0 copy-done.1
  67.9 1.2 shard_map.61
  69.1 0.0 copy-start
  69.1 1.3 copy-done
  70.4 4.6 %all-to-all-start.1 = ((f32[16,2,16,8,128]{4,3,2,1,0:T(8,128)}), f32[16,2,16,8,128]{4,3,2,1,0:T(8,128)S(1)}, u32[]{:S(2)}, u32[]{:S(2)}) async-start(f32[16,2,16,8,128]{4,3,2,1,0:T(8,128)} %copy-done), calls=%async_computation.1 | async-start | bytes 4194304 | tf_op jit(solution)/shard_map/all_to_all | solution.py:351
  75.0 0.0 copy-start.4
  75.0 0.0 copy-start.5
  75.0 0.0 copy-start.6
  75.0 0.3 collective-permute-start.3
  75.3 5.7 %collective-permute-done.1.refs_0_.refs_1_ = f32[16,8,8,128]{3,2,1,0:T(8,128)} collective-permute-done((f32[16,8,8,128]{3,2,1,0:T(8,128)}, f32[16,8,8,128]{3,2,1,0:T(8,128)}, u32[]{:S(2)}, u32[]{:S(2)}) %collective-permute-start.1) | collective-permute-done | bytes 524320 | tf_op jit(solution)/shard_map/ppermute | solution.py:354
  81.0 0.0 copy-start.3
  81.0 21.2 %all-to-all-done.1.refs_0_.refs_2_ = f32[16,2,16,8,128]{4,3,2,1,0:T(8,128)S(1)} async-done(((f32[16,2,16,8,128]{4,3,2,1,0:T(8,128)}), f32[16,2,16,8,128]{4,3,2,1,0:T(8,128)S(1)}, u32[]{:S(2)}, u32[]{:S(2)}) %all-to-all-start.1) | async-done | bytes 2097184 | tf_op jit(solution)/shard_map/all_to_all | solution.py:351
  102.2 0.0 copy-done.4
  102.2 0.0 copy-done.5
  102.2 0.0 copy-done.6
  102.2 6.1 %shard_map.63 = (f32[32,9,128]{2,1,0:T(8,128)S(1)}, f32[32,16,256]{2,1,0:T(8,128)S(1)}) custom-call(s32[1]{0:T(128)} %bitcast.first.turn, f32[16,2,16,8,128]{4,3,2,1,0:T(8,128)S(1)} %all-to-all-done.1.refs_0_.refs_2_, f32[8,128]{1,0:T(8,128)S(1)} %shard_map.62.refs_1_.refs_4_.refs_2_, bf16[256,256]{1,0:T(8,128)(2,1)S(1)} %copy-done.5, ...), custom_call_target="tpu_custom_call" | custom-call | flops 1000000000 | tf_op jit(solution)/shard_map/pallas_call | solution.py:228
  108.4 0.0 copy-start.8
  108.4 0.0 copy-done.3
  108.4 4.6 %shard_map.64.refs_6_ = f32[32,9,128]{2,1,0:T(8,128)S(1)} custom-call(s32[1]{0:T(128)} %bitcast.first.turn, f32[16,8,8,128]{3,2,1,0:T(8,128)S(1)} %copy-done.3, f32[16,8,8,128]{3,2,1,0:T(8,128)} %collective-permute-done.1.refs_0_.refs_1_, f32[16,2,16,8,128]{4,3,2,1,0:T(8,128)S(1)} %all-to-all-done.1.refs_0_.refs_2_, ...), custom_call_target="tpu_custom_call" | custom-call | flops 1000000000 | tf_op jit(solution)/shard_map/pallas_call | solution.py:228
  113.0 0.0 collective-permute-done.3.refs_1_
  113.0 0.0 copy-done.8
  113.0 5.9 %shard_map.66 = f32[32,9,128]{2,1,0:T(8,128)S(1)} custom-call(s32[1]{0:T(128)} %bitcast.first.turn, f32[16,12,8,128]{3,2,1,0:T(8,128)S(1)} %copy-done.8, f32[16,12,8,128]{3,2,1,0:T(8,128)} %collective-permute-done.3.refs_1_, f32[8,128]{1,0:T(8,128)S(1)} %shard_map.62.refs_1_.refs_4_.refs_2_, bf16[256,256]{1,0:T(8,128)(2,1)S(1)} %copy-done.5, ...), custom_call_target="tpu_custom_call" | custom-call | flops 1000000000 | tf_op jit(solution)/shard_map/pallas_call | solution.py:228
  119.0 0.1 copy.9
  119.1 21.5 %all_to_all.20 = f32[16,2,9,128]{3,1,2,0:T(2,128)S(1)} all-to-all(f32[16,2,9,128]{3,1,2,0:T(2,128)S(1)} %copy.9), channel_id=1, replica_groups=mesh['y'=4,'zh'=2,'x'=4,'zl'=4,'core'=2] {'y','x'}, dimensions={0} | all-to-all | bytes 294912 | tf_op jit(solution)/shard_map/all_to_all | solution.py:351
  140.6 0.1 reduce_sum.18
  140.7 0.1 reshape.69
  140.8 0.1 reshape.72
  140.9 16.1 %all_to_all.21 = f32[16,1,144]{2,1,0:T(1,128)S(1)} all-to-all(f32[16,1,144]{2,1,0:T(1,128)S(1)} %reshape.72), channel_id=1, replica_groups=mesh['y'=4,'zh'=2,'x'=4,'zl'=4,'core'=2] {'zh','zl','core'}, dimensions={0} | all-to-all | bytes 18432 | tf_op jit(solution)/shard_map/all_to_all | solution.py:389
  157.0 0.1 negate_bitcast_fusion
  157.1 0.1 stack.2
  157.2 0.6 copy.14
  (8 shorter events, 0.1 us)
Async XLA Ops:
  1.9 23.4 %collective-permute-start = (f32[16,8,8,128]{3,2,1,0:T(8,128)}, f32[16,8,8,128]{3,2,1,0:T(8,128)S(1)}, u32[]{:S(2)}, u32[]{:S(2)}) collective-permute-start(f32[16,8,8,128]{3,2,1,0:T(8,128)} %shard_map.55), channel_id=1, source_target_pairs={{0,32},{32,0},{1,33},{33,1},{2,34},{34,2},{3,35},{35,3},{4,36},{36... | collective-permute-start | bytes 1572872 | tf_op jit(solution)/shard_map/ppermute | solution.py:354
  11.7 56.2 %collective-permute-start.2 = (f32[16,8,8,128]{3,2,1,0:T(8,128)}, f32[16,8,8,128]{3,2,1,0:T(8,128)}, u32[]{:S(2)}, u32[]{:S(2)}) collective-permute-start(f32[16,8,8,128]{3,2,1,0:T(8,128)} %shard_map.56), channel_id=1, source_target_pairs={{0,32},{32,0},{1,33},{33,1},{2,34},{34,2},{3,35},{35,3},{4,36},{36... | collective-permute-start | bytes 1572872 | tf_op jit(solution)/shard_map/ppermute | solution.py:354
  15.4 44.5 %all-to-all-start = ((f32[16,2,20,8,128]{4,3,2,1,0:T(8,128)}), f32[16,2,20,8,128]{4,3,2,1,0:T(8,128)S(1)}, u32[]{:S(2)}, u32[]{:S(2)}) async-start(f32[16,2,20,8,128]{4,3,2,1,0:T(8,128)} %shard_map.57), calls=%async_computation | async-start | bytes 5242880 | tf_op jit(solution)/shard_map/all_to_all | solution.py:351
  59.9 7.9 %copy-start.1 = (f32[16,16,8,128]{3,2,1,0:T(8,128)S(1)}, f32[16,16,8,128]{3,2,1,0:T(8,128)}, u32[]{:S(2)}) copy-start(f32[16,16,8,128]{3,2,1,0:T(8,128)} %shard_map.58.kept) | copy-start | bytes 3145732
  60.8 0.8 copy-start.2
  61.6 19.4 %collective-permute-start.1 = (f32[16,8,8,128]{3,2,1,0:T(8,128)}, f32[16,8,8,128]{3,2,1,0:T(8,128)}, u32[]{:S(2)}, u32[]{:S(2)}) collective-permute-start(f32[16,8,8,128]{3,2,1,0:T(8,128)} %get-tuple-element.33), channel_id=1, source_target_pairs={{0,32},{32,0},{1,33},{33,1},{2,34},{34,2},{3,35},{35,3},{4,36},{36... | collective-permute-start | bytes 1572872 | tf_op jit(solution)/shard_map/ppermute | solution.py:354
  67.0 0.9 copy-start.7
  69.1 1.4 copy-start
  70.4 31.8 %all-to-all-start.1 = ((f32[16,2,16,8,128]{4,3,2,1,0:T(8,128)}), f32[16,2,16,8,128]{4,3,2,1,0:T(8,128)S(1)}, u32[]{:S(2)}, u32[]{:S(2)}) async-start(f32[16,2,16,8,128]{4,3,2,1,0:T(8,128)} %copy-done), calls=%async_computation.1 | async-start | bytes 4194304 | tf_op jit(solution)/shard_map/all_to_all | solution.py:351
  75.0 27.2 %copy-start.4 = (bf16[256,256]{1,0:T(8,128)(2,1)S(1)}, bf16[256,256]{1,0:T(8,128)(2,1)}, u32[]{:S(2)}) copy-start(bf16[256,256]{1,0:T(8,128)(2,1)} %constant.75.clone.refs_3_.refs_6_.refs_4_) | copy-start | bytes 393220
  75.0 27.2 %copy-start.5 = (bf16[256,256]{1,0:T(8,128)(2,1)S(1)}, bf16[256,256]{1,0:T(8,128)(2,1)}, u32[]{:S(2)}) copy-start(bf16[256,256]{1,0:T(8,128)(2,1)} %constant.74.clone.refs_2_.refs_5_.refs_3_) | copy-start | bytes 393220
  75.0 27.2 %copy-start.6 = (f32[32,2,128]{2,1,0:T(2,128)S(1)}, f32[32,2,128]{2,1,0:T(2,128)}, u32[]{:S(2)}) copy-start(f32[32,2,128]{2,1,0:T(2,128)} %constant.76.clone.refs_4_.refs_7_.refs_5_) | copy-start | bytes 98308
  75.0 38.0 %collective-permute-start.3 = (f32[16,12,8,128]{3,2,1,0:T(8,128)}, f32[16,12,8,128]{3,2,1,0:T(8,128)}, u32[]{:S(2)}, u32[]{:S(2)}) collective-permute-start(f32[16,12,8,128]{3,2,1,0:T(8,128)} %get-tuple-element.45), channel_id=1, source_target_pairs={{0,32},{32,0},{1,33},{33,1},{2,34},{34,2},{3,35},{35,3},{4,36},{36... | collective-permute-start | bytes 2359304 | tf_op jit(solution)/shard_map/ppermute | solution.py:354
  81.0 27.4 %copy-start.3 = (f32[16,8,8,128]{3,2,1,0:T(8,128)S(1)}, f32[16,8,8,128]{3,2,1,0:T(8,128)}, u32[]{:S(2)}) copy-start(f32[16,8,8,128]{3,2,1,0:T(8,128)} %copy-done.2) | copy-start | bytes 1572868
  108.4 4.7 %copy-start.8 = (f32[16,12,8,128]{3,2,1,0:T(8,128)S(1)}, f32[16,12,8,128]{3,2,1,0:T(8,128)}, u32[]{:S(2)}) copy-start(f32[16,12,8,128]{3,2,1,0:T(8,128)} %copy-done.7) | copy-start | bytes 2359300

commit v13 on v12

--- a/solution.py
+++ b/solution.py
@@ -365,11 +365,12 @@
     side = zh.reshape(1).astype(jnp.int32)
     ahead = arrange(side, parts, early[:1], (1,))
     ahead, side = fence((ahead, side))
+    ahead = move(ahead)
+    rest = arrange(side, parts, late, (0, 1))
+    rest, side = fence((rest, side))
     sent = arrange(side, parts, early[1:], (1,))
-    sent, side = fence((sent, side))
-    ahead, landed = move(ahead), move(sent)
-    rest = arrange(side, parts, late, (0, 1))
-    rest = spread(rest)
+    rest, sent = spread(rest), fence(sent)
+    landed = move(sent)
     kept = arrange(side, parts, early, (0,))
     kept, weights = fence((kept, weights))
     ahead, rest, weights = fence((ahead, rest, settle(weights, [ahead], 50.0)))

time: 158 us -> 153 us (0.968)
  blocking collectives: 37.6 us -> 33.6 us
    all_to_all x2, waiting for transfers between devices: 55.8 us -> 45.4 us  [spread(): return lax.all_to_all(value, ('y', 'x'), split_axis=0, concat_axis=0)]
    ppermute x4, waiting for transfers between devices: 5.72 us -> 14.7 us  [move(): return lax.ppermute(value, 'zh', [(0, 1), (1, 0)])]
    all_to_all x1, blocking collectives: 16.1 us -> 13.5 us  [per_device(): lax.all_to_all(shares, ('zh', 'zl', 'core'), split_axis=0, concat_axis=0)]
  transfers between devices with their start and end apart: 6 -> 6, of which waited for: 3 -> 4; matrix products, arithmetic and copies ran while one was open for 0% -> 0% of each run, Pallas kernels for 14% -> 14%
where the time goes in v13:
time: 153 us; the launch traced here: 152 us
  waiting for transfers between devices  60 us (39%)
  blocking collectives  33.6 us (22%)
  Pallas kernels  29.5 us (19%)
  starting transfers between devices  23.9 us (16%)
  local copies, waits for them, and re-layouts  4.12 us (3%)
    all_to_all x2, waiting for transfers between devices, spread(): return lax.all_to_all(value, ('y', 'x'), split_axis=0, concat_axis=0)  45.4 us
    all_to_all x1, blocking collectives, spread(): return lax.all_to_all(value, ('y', 'x'), split_axis=0, concat_axis=0)  20.1 us
    pallas_call x3, Pallas kernels, collide(): pl.pallas_call(functools.partial(kernel, count, stacked, joined, spilled)...  16.7 us
    ppermute x4, waiting for transfers between devices, move(): return lax.ppermute(value, 'zh', [(0, 1), (1, 0)])  14.7 us
    all_to_all x1, blocking collectives, per_device(): lax.all_to_all(shares, ('zh', 'zl', 'core'), split_axis=0, concat_axis=0)  13.5 us
    ppermute x4, starting transfers between devices, move(): return lax.ppermute(value, 'zh', [(0, 1), (1, 0)])  13.4 us
    all_to_all x2, starting transfers between devices, spread(): return lax.all_to_all(value, ('y', 'x'), split_axis=0, concat_axis=0)  10.5 us
    pallas_call x4, Pallas kernels, arrange(): pl.pallas_call(functools.partial(arrange_kernel, blocks, ways), out_shape...  9.78 us
  transfers between devices with their start and end apart: 6, of which 4 were waited for; matrix products, arithmetic and copies ran while one was open for 0% of the time, Pallas kernels for 14%

profile of v13, /device:TPU:1, one launch (start us, length us, event | category | flops | bytes accessed | tf_op | source)
XLA Modules:
  0.0 152.3 jit_solution(10281368820616810671)
XLA Ops:
  0.0 1.9 %shard_map.55 = f32[16,8,8,128]{3,2,1,0:T(8,128)} custom-call(s32[1]{0:T(128)} %bitcast.first.turn, f32[12,3,2,16,8,128]{5,4,3,2,1,0:T(8,128)} %bitcast.32), custom_call_target="tpu_custom_call" | custom-call | bytes 3200000 | tf_op jit(solution)/shard_map/pallas_call | solution.py:261
  1.9 7.8 %collective-permute-start = (f32[16,8,8,128]{3,2,1,0:T(8,128)}, f32[16,8,8,128]{3,2,1,0:T(8,128)S(1)}, u32[]{:S(2)}, u32[]{:S(2)}) collective-permute-start(f32[16,8,8,128]{3,2,1,0:T(8,128)} %shard_map.55), channel_id=1, source_target_pairs={{0,32},{32,0},{1,33},{33,1},{2,34},{34,2},{3,35},{35,3},{4,36},{36... | collective-permute-start | bytes 1572872 | tf_op jit(solution)/shard_map/ppermute | solution.py:354
  9.8 3.6 %shard_map.56 = f32[16,2,20,8,128]{4,3,2,1,0:T(8,128)} custom-call(s32[1]{0:T(128)} %bitcast.first.turn, f32[12,3,2,16,8,128]{5,4,3,2,1,0:T(8,128)} %bitcast.33), custom_call_target="tpu_custom_call" | custom-call | bytes 3200000 | tf_op jit(solution)/shard_map/pallas_call | solution.py:261
  13.3 6.8 %all-to-all-start = ((f32[16,2,20,8,128]{4,3,2,1,0:T(8,128)}), f32[16,2,20,8,128]{4,3,2,1,0:T(8,128)S(1)}, u32[]{:S(2)}, u32[]{:S(2)}) async-start(f32[16,2,20,8,128]{4,3,2,1,0:T(8,128)} %shard_map.56), calls=%async_computation | async-start | bytes 5242880 | tf_op jit(solution)/shard_map/all_to_all | solution.py:351
  20.1 1.9 %shard_map.60 = f32[16,8,8,128]{3,2,1,0:T(8,128)} custom-call(s32[1]{0:T(128)} %bitcast.first.turn, f32[12,3,2,16,8,128]{5,4,3,2,1,0:T(8,128)} %bitcast.34), custom_call_target="tpu_custom_call" | custom-call | bytes 3200000 | tf_op jit(solution)/shard_map/pallas_call | solution.py:261
  22.0 0.1 collective-permute-start.2
  22.2 2.4 %shard_map.57.kept = f32[16,16,8,128]{3,2,1,0:T(8,128)} custom-call(s32[1]{0:T(128)} %bitcast.first.turn, f32[12,3,2,16,8,128]{5,4,3,2,1,0:T(8,128)} %bitcast.35), custom_call_target="tpu_custom_call" | custom-call | bytes 3200000 | tf_op jit(solution)/shard_map/pallas_call | solution.py:261
  25.2 0.1 broadcast_in_dim.19.given
  25.3 0.0 collective-permute-done.refs_0_.ahead
  25.3 32.6 %all-to-all-done.whole = f32[16,2,20,8,128]{4,3,2,1,0:T(8,128)S(1)} async-done(((f32[16,2,20,8,128]{4,3,2,1,0:T(8,128)}), f32[16,2,20,8,128]{4,3,2,1,0:T(8,128)S(1)}, u32[]{:S(2)}, u32[]{:S(2)}) %all-to-all-start) | async-done | bytes 2621472 | tf_op jit(solution)/shard_map/all_to_all | solution.py:351
  57.9 0.0 copy-start.1
  57.9 0.9 shard_map.59
  58.8 0.0 copy-start.2
  58.8 0.8 copy-done.2
  59.6 1.2 collective-permute-start.1
  60.7 1.0 shard_map.65
  61.8 0.0 copy-start.7
  61.8 0.9 copy-done.7
  62.6 0.0 collective-permute-done.2.landed
  62.6 0.0 copy-done.1
  62.6 1.2 shard_map.61
  63.8 0.0 copy-start
  63.8 1.3 copy-done
  65.2 3.7 %all-to-all-start.1 = ((f32[16,2,16,8,128]{4,3,2,1,0:T(8,128)}), f32[16,2,16,8,128]{4,3,2,1,0:T(8,128)S(1)}, u32[]{:S(2)}, u32[]{:S(2)}) async-start(f32[16,2,16,8,128]{4,3,2,1,0:T(8,128)} %copy-done), calls=%async_computation.1 | async-start | bytes 4194304 | tf_op jit(solution)/shard_map/all_to_all | solution.py:351
  68.9 0.0 copy-start.4
  68.9 0.0 copy-start.5
  68.9 0.0 copy-start.6
  68.9 4.3 %collective-permute-start.3 = (f32[16,12,8,128]{3,2,1,0:T(8,128)}, f32[16,12,8,128]{3,2,1,0:T(8,128)}, u32[]{:S(2)}, u32[]{:S(2)}) collective-permute-start(f32[16,12,8,128]{3,2,1,0:T(8,128)} %get-tuple-element.45), channel_id=1, source_target_pairs={{0,32},{32,0},{1,33},{33,1},{2,34},{34,2},{3,35},{35,3},{4,36},{36... | collective-permute-start | bytes 2359304 | tf_op jit(solution)/shard_map/ppermute | solution.py:354
  73.2 9.9 %collective-permute-done.1.refs_0_.refs_1_ = f32[16,8,8,128]{3,2,1,0:T(8,128)} collective-permute-done((f32[16,8,8,128]{3,2,1,0:T(8,128)}, f32[16,8,8,128]{3,2,1,0:T(8,128)}, u32[]{:S(2)}, u32[]{:S(2)}) %collective-permute-start.1) | collective-permute-done | bytes 524320 | tf_op jit(solution)/shard_map/ppermute | solution.py:354
  83.1 0.0 copy-start.3
  83.1 12.8 %all-to-all-done.1.refs_0_.refs_2_ = f32[16,2,16,8,128]{4,3,2,1,0:T(8,128)S(1)} async-done(((f32[16,2,16,8,128]{4,3,2,1,0:T(8,128)}), f32[16,2,16,8,128]{4,3,2,1,0:T(8,128)S(1)}, u32[]{:S(2)}, u32[]{:S(2)}) %all-to-all-start.1) | async-done | bytes 2097184 | tf_op jit(solution)/shard_map/all_to_all | solution.py:351
  96.0 0.0 copy-done.4
  96.0 0.0 copy-done.5
  96.0 0.0 copy-done.6
  96.0 6.1 %shard_map.63 = (f32[32,9,128]{2,1,0:T(8,128)S(1)}, f32[32,16,256]{2,1,0:T(8,128)S(1)}) custom-call(s32[1]{0:T(128)} %bitcast.first.turn, f32[16,2,16,8,128]{4,3,2,1,0:T(8,128)S(1)} %all-to-all-done.1.refs_0_.refs_2_, f32[8,128]{1,0:T(8,128)S(1)} %shard_map.62.refs_1_.refs_4_.refs_2_, bf16[256,256]{1,0:T(8,128)(2,1)S(1)} %copy-done.5, ...), custom_call_target="tpu_custom_call" | custom-call | flops 1000000000 | tf_op jit(solution)/shard_map/pallas_call | solution.py:228
  102.1 0.0 copy-start.8
  102.1 0.0 copy-done.3
  102.1 4.6 %shard_map.64.refs_6_ = f32[32,9,128]{2,1,0:T(8,128)S(1)} custom-call(s32[1]{0:T(128)} %bitcast.first.turn, f32[16,8,8,128]{3,2,1,0:T(8,128)S(1)} %copy-done.3, f32[16,8,8,128]{3,2,1,0:T(8,128)} %collective-permute-done.1.refs_0_.refs_1_, f32[16,2,16,8,128]{4,3,2,1,0:T(8,128)S(1)} %all-to-all-done.1.refs_0_.refs_2_, ...), custom_call_target="tpu_custom_call" | custom-call | flops 1000000000 | tf_op jit(solution)/shard_map/pallas_call | solution.py:228
  106.8 4.7 %collective-permute-done.3.refs_1_ = f32[16,12,8,128]{3,2,1,0:T(8,128)} collective-permute-done((f32[16,12,8,128]{3,2,1,0:T(8,128)}, f32[16,12,8,128]{3,2,1,0:T(8,128)}, u32[]{:S(2)}, u32[]{:S(2)}) %collective-permute-start.3) | collective-permute-done | bytes 786464 | tf_op jit(solution)/shard_map/ppermute | solution.py:354
  111.5 0.0 copy-done.8
  111.5 5.9 %shard_map.66 = f32[32,9,128]{2,1,0:T(8,128)S(1)} custom-call(s32[1]{0:T(128)} %bitcast.first.turn, f32[16,12,8,128]{3,2,1,0:T(8,128)S(1)} %copy-done.8, f32[16,12,8,128]{3,2,1,0:T(8,128)} %collective-permute-done.3.refs_1_, f32[8,128]{1,0:T(8,128)S(1)} %shard_map.62.refs_1_.refs_4_.refs_2_, bf16[256,256]{1,0:T(8,128)(2,1)S(1)} %copy-done.5, ...), custom_call_target="tpu_custom_call" | custom-call | flops 1000000000 | tf_op jit(solution)/shard_map/pallas_call | solution.py:228
  117.4 0.1 copy.9
  117.5 20.1 %all_to_all.20 = f32[16,2,9,128]{3,1,2,0:T(2,128)S(1)} all-to-all(f32[16,2,9,128]{3,1,2,0:T(2,128)S(1)} %copy.9), channel_id=1, replica_groups=mesh['y'=4,'zh'=2,'x'=4,'zl'=4,'core'=2] {'y','x'}, dimensions={0} | all-to-all | bytes 294912 | tf_op jit(solution)/shard_map/all_to_all | solution.py:351
  137.6 0.1 reduce_sum.18
  137.7 0.1 reshape.69
  137.8 0.1 reshape.72
  137.9 13.5 %all_to_all.21 = f32[16,1,144]{2,1,0:T(1,128)S(1)} all-to-all(f32[16,1,144]{2,1,0:T(1,128)S(1)} %reshape.72), channel_id=1, replica_groups=mesh['y'=4,'zh'=2,'x'=4,'zl'=4,'core'=2] {'zh','zl','core'}, dimensions={0} | all-to-all | bytes 18432 | tf_op jit(solution)/shard_map/all_to_all | solution.py:390
  151.5 0.1 negate_bitcast_fusion
  151.6 0.1 stack.2
  151.7 0.6 copy.14
  (8 shorter events, 0.1 us)
Async XLA Ops:
  1.9 23.3 %collective-permute-start = (f32[16,8,8,128]{3,2,1,0:T(8,128)}, f32[16,8,8,128]{3,2,1,0:T(8,128)S(1)}, u32[]{:S(2)}, u32[]{:S(2)}) collective-permute-start(f32[16,8,8,128]{3,2,1,0:T(8,128)} %shard_map.55), channel_id=1, source_target_pairs={{0,32},{32,0},{1,33},{33,1},{2,34},{34,2},{3,35},{35,3},{4,36},{36... | collective-permute-start | bytes 1572872 | tf_op jit(solution)/shard_map/ppermute | solution.py:354
  13.3 44.5 %all-to-all-start = ((f32[16,2,20,8,128]{4,3,2,1,0:T(8,128)}), f32[16,2,20,8,128]{4,3,2,1,0:T(8,128)S(1)}, u32[]{:S(2)}, u32[]{:S(2)}) async-start(f32[16,2,20,8,128]{4,3,2,1,0:T(8,128)} %shard_map.56), calls=%async_computation | async-start | bytes 5242880 | tf_op jit(solution)/shard_map/all_to_all | solution.py:351
  22.0 40.6 %collective-permute-start.2 = (f32[16,8,8,128]{3,2,1,0:T(8,128)}, f32[16,8,8,128]{3,2,1,0:T(8,128)}, u32[]{:S(2)}, u32[]{:S(2)}) collective-permute-start(f32[16,8,8,128]{3,2,1,0:T(8,128)} %shard_map.60), channel_id=1, source_target_pairs={{0,32},{32,0},{1,33},{33,1},{2,34},{34,2},{3,35},{35,3},{4,36},{36... | collective-permute-start | bytes 1572872 | tf_op jit(solution)/shard_map/ppermute | solution.py:354
  57.9 4.8 %copy-start.1 = (f32[16,16,8,128]{3,2,1,0:T(8,128)S(1)}, f32[16,16,8,128]{3,2,1,0:T(8,128)}, u32[]{:S(2)}) copy-start(f32[16,16,8,128]{3,2,1,0:T(8,128)} %shard_map.57.kept) | copy-start | bytes 3145732
  58.8 0.8 copy-start.2
  59.6 23.6 %collective-permute-start.1 = (f32[16,8,8,128]{3,2,1,0:T(8,128)}, f32[16,8,8,128]{3,2,1,0:T(8,128)}, u32[]{:S(2)}, u32[]{:S(2)}) collective-permute-start(f32[16,8,8,128]{3,2,1,0:T(8,128)} %get-tuple-element.34), channel_id=1, source_target_pairs={{0,32},{32,0},{1,33},{33,1},{2,34},{34,2},{3,35},{35,3},{4,36},{36... | collective-permute-start | bytes 1572872 | tf_op jit(solution)/shard_map/ppermute | solution.py:354
  61.8 0.9 copy-start.7
  63.8 1.4 copy-start
  65.2 30.7 %all-to-all-start.1 = ((f32[16,2,16,8,128]{4,3,2,1,0:T(8,128)}), f32[16,2,16,8,128]{4,3,2,1,0:T(8,128)S(1)}, u32[]{:S(2)}, u32[]{:S(2)}) async-start(f32[16,2,16,8,128]{4,3,2,1,0:T(8,128)} %copy-done), calls=%async_computation.1 | async-start | bytes 4194304 | tf_op jit(solution)/shard_map/all_to_all | solution.py:351
  68.9 27.0 %copy-start.4 = (bf16[256,256]{1,0:T(8,128)(2,1)S(1)}, bf16[256,256]{1,0:T(8,128)(2,1)}, u32[]{:S(2)}) copy-start(bf16[256,256]{1,0:T(8,128)(2,1)} %constant.75.clone.refs_3_.refs_6_.refs_4_) | copy-start | bytes 393220
  68.9 27.0 %copy-start.5 = (bf16[256,256]{1,0:T(8,128)(2,1)S(1)}, bf16[256,256]{1,0:T(8,128)(2,1)}, u32[]{:S(2)}) copy-start(bf16[256,256]{1,0:T(8,128)(2,1)} %constant.74.clone.refs_2_.refs_5_.refs_3_) | copy-start | bytes 393220
  68.9 27.0 %copy-start.6 = (f32[32,2,128]{2,1,0:T(2,128)S(1)}, f32[32,2,128]{2,1,0:T(2,128)}, u32[]{:S(2)}) copy-start(f32[32,2,128]{2,1,0:T(2,128)} %constant.76.clone.refs_4_.refs_7_.refs_5_) | copy-start | bytes 98308
  68.9 42.6 %collective-permute-start.3 = (f32[16,12,8,128]{3,2,1,0:T(8,128)}, f32[16,12,8,128]{3,2,1,0:T(8,128)}, u32[]{:S(2)}, u32[]{:S(2)}) collective-permute-start(f32[16,12,8,128]{3,2,1,0:T(8,128)} %get-tuple-element.45), channel_id=1, source_target_pairs={{0,32},{32,0},{1,33},{33,1},{2,34},{34,2},{3,35},{35,3},{4,36},{36... | collective-permute-start | bytes 2359304 | tf_op jit(solution)/shard_map/ppermute | solution.py:354
  83.1 19.0 %copy-start.3 = (f32[16,8,8,128]{3,2,1,0:T(8,128)S(1)}, f32[16,8,8,128]{3,2,1,0:T(8,128)}, u32[]{:S(2)}) copy-start(f32[16,8,8,128]{3,2,1,0:T(8,128)} %copy-done.2) | copy-start | bytes 1572868
  102.1 9.4 %copy-start.8 = (f32[16,12,8,128]{3,2,1,0:T(8,128)S(1)}, f32[16,12,8,128]{3,2,1,0:T(8,128)}, u32[]{:S(2)}) copy-start(f32[16,12,8,128]{3,2,1,0:T(8,128)} %copy-done.7) | copy-start | bytes 2359300

commit v14 on v13

--- a/solution.py
+++ b/solution.py
@@ -294,27 +294,21 @@
     )(kept, ahead, landed)
 
 
-def cut_kernel(base, whole, *refs):
-    *outs, sems = refs
-    copies = []
-    for n, out in enumerate(outs):
-        source = whole.at[:, n, pl.ds(base, out.shape[1])]
-        copies.append(pltpu.make_async_copy(source, out, sems.at[n]))
-    for copy in copies:
-        copy.start()
-    for copy in copies:
-        copy.wait()
-
-
-def cut(whole, base, size):
+def cut_kernel(base, way, whole, out, sem):
+    copy = pltpu.make_async_copy(whole.at[:, way, pl.ds(base, out.shape[1])], out, sem)
+    copy.start()
+    copy.wait()
+
+
+def cut(whole, base, size, way):
     return pl.pallas_call(
-        functools.partial(cut_kernel, base),
-        out_shape=[jax.ShapeDtypeStruct((PLANE, size, SLOTS, LANES), jnp.float32)] * 2,
+        functools.partial(cut_kernel, base, way),
+        out_shape=jax.ShapeDtypeStruct((PLANE, size, SLOTS, LANES), jnp.float32),
         in_specs=[pl.BlockSpec(memory_space=pl.ANY)],
-        out_specs=[pl.BlockSpec(memory_space=pltpu.VMEM)] * 2,
-        scratch_shapes=[pltpu.SemaphoreType.DMA((2,))],
+        out_specs=pl.BlockSpec(memory_space=pltpu.VMEM),
+        scratch_shapes=[pltpu.SemaphoreType.DMA],
         compiler_params=pltpu.CompilerParams(vmem_limit_bytes=8 * 1024 * 1024),
-        cost_estimate=pl.CostEstimate(flops=0, bytes_accessed=3_200_000, transcendentals=0),
+        cost_estimate=pl.CostEstimate(flops=0, bytes_accessed=1_600_000, transcendentals=0),
     )(whole)
 
 
@@ -374,9 +368,9 @@
     kept = arrange(side, parts, early, (0,))
     kept, weights = fence((kept, weights))
     ahead, rest, weights = fence((ahead, rest, settle(weights, [ahead], 50.0)))
-    one = cut(rest, 0, 4 * len(late[0]))
-    two = cut(rest, 4 * len(late[0]), 4 * len(late[1]))
-    one, two = (one[0], move(one[1])), (two[0], move(two[1]))
+    place, sizes = (0, 4 * len(late[0])), [4 * len(pairs) for pairs in late]
+    one, two = (move(cut(rest, base, size, 1)) for base, size in zip(place, sizes))
+    one, two = ((cut(rest, base, size, 0), part) for base, size, part in zip(place, sizes, (one, two)))
     zero = spread(join(kept, ahead, landed))
     one, zero, weights = fence((one, zero, settle(weights, one[1:], 50.0)))
     partial, sigma = work([zero], partial, weights, spilled=True)

time: 153 us -> 152 us (level)
    unnamed x18 -> x20, local copies, waits for them, and re-layouts: 3.04 us -> 3.97 us
where the time goes in v14:
time: 152 us
  waiting for transfers between devices  59.1 us (39%)
  blocking collectives  33.6 us (22%)
  Pallas kernels  28.6 us (19%)
  starting transfers between devices  24 us (16%)
  local copies, waits for them, and re-layouts  5.05 us (3%)
    all_to_all x2, waiting for transfers between devices, spread(): return lax.all_to_all(value, ('y', 'x'), split_axis=0, concat_axis=0)  44.7 us
    all_to_all x1, blocking collectives, spread(): return lax.all_to_all(value, ('y', 'x'), split_axis=0, concat_axis=0)  20 us
    pallas_call x3, Pallas kernels, collide(): pl.pallas_call(functools.partial(kernel, count, stacked, joined, spilled)...  16.7 us
    ppermute x4, waiting for transfers between devices, move(): return lax.ppermute(value, 'zh', [(0, 1), (1, 0)])  14.4 us
    all_to_all x1, blocking collectives, per_device(): lax.all_to_all(shares, ('zh', 'zl', 'core'), split_axis=0, concat_axis=0)  13.6 us
    ppermute x4, starting transfers between devices, move(): return lax.ppermute(value, 'zh', [(0, 1), (1, 0)])  13.5 us
    all_to_all x2, starting transfers between devices, spread(): return lax.all_to_all(value, ('y', 'x'), split_axis=0, concat_axis=0)  10.5 us
    pallas_call x4, Pallas kernels, arrange(): pl.pallas_call(functools.partial(arrange_kernel, blocks, ways), out_shape...  9.77 us
  transfers between devices with their start and end apart: 6, of which 4 were waited for; matrix products, arithmetic and copies ran while one was open for 0% of the time, Pallas kernels for 14%

profile of v14, /device:TPU:1, one launch (start us, length us, event | category | flops | bytes accessed | tf_op | source)
XLA Modules:
  0.0 151.5 jit_solution(9648224663918322556)
XLA Ops:
  0.0 1.9 %shard_map.55 = f32[16,8,8,128]{3,2,1,0:T(8,128)} custom-call(s32[1]{0:T(128)} %bitcast.first.turn, f32[12,3,2,16,8,128]{5,4,3,2,1,0:T(8,128)} %bitcast.32), custom_call_target="tpu_custom_call" | custom-call | bytes 3200000 | tf_op jit(solution)/shard_map/pallas_call | solution.py:261
  1.9 7.8 %collective-permute-start = (f32[16,8,8,128]{3,2,1,0:T(8,128)}, f32[16,8,8,128]{3,2,1,0:T(8,128)S(1)}, u32[]{:S(2)}, u32[]{:S(2)}) collective-permute-start(f32[16,8,8,128]{3,2,1,0:T(8,128)} %shard_map.55), channel_id=1, source_target_pairs={{0,32},{32,0},{1,33},{33,1},{2,34},{34,2},{3,35},{35,3},{4,36},{36... | collective-permute-start | bytes 1572872 | tf_op jit(solution)/shard_map/ppermute | solution.py:348
  9.8 3.5 %shard_map.56 = f32[16,2,20,8,128]{4,3,2,1,0:T(8,128)} custom-call(s32[1]{0:T(128)} %bitcast.first.turn, f32[12,3,2,16,8,128]{5,4,3,2,1,0:T(8,128)} %bitcast.33), custom_call_target="tpu_custom_call" | custom-call | bytes 3200000 | tf_op jit(solution)/shard_map/pallas_call | solution.py:261
  13.3 6.8 %all-to-all-start = ((f32[16,2,20,8,128]{4,3,2,1,0:T(8,128)}), f32[16,2,20,8,128]{4,3,2,1,0:T(8,128)S(1)}, u32[]{:S(2)}, u32[]{:S(2)}) async-start(f32[16,2,20,8,128]{4,3,2,1,0:T(8,128)} %shard_map.56), calls=%async_computation | async-start | bytes 5242880 | tf_op jit(solution)/shard_map/all_to_all | solution.py:345
  20.1 1.9 %shard_map.61 = f32[16,8,8,128]{3,2,1,0:T(8,128)} custom-call(s32[1]{0:T(128)} %bitcast.first.turn, f32[12,3,2,16,8,128]{5,4,3,2,1,0:T(8,128)} %bitcast.34), custom_call_target="tpu_custom_call" | custom-call | bytes 3200000 | tf_op jit(solution)/shard_map/pallas_call | solution.py:261
  22.0 0.1 collective-permute-start.2
  22.1 2.4 %shard_map.57.kept = f32[16,16,8,128]{3,2,1,0:T(8,128)} custom-call(s32[1]{0:T(128)} %bitcast.first.turn, f32[12,3,2,16,8,128]{5,4,3,2,1,0:T(8,128)} %bitcast.35), custom_call_target="tpu_custom_call" | custom-call | bytes 3200000 | tf_op jit(solution)/shard_map/pallas_call | solution.py:261
  25.2 0.1 broadcast_in_dim.19.given
  25.3 0.0 collective-permute-done.refs_0_.ahead
  25.3 0.0 copy-start.5
  25.3 0.8 copy-done.5
  26.1 31.8 %all-to-all-done.whole = f32[16,2,20,8,128]{4,3,2,1,0:T(8,128)S(1)} async-done(((f32[16,2,20,8,128]{4,3,2,1,0:T(8,128)}), f32[16,2,20,8,128]{4,3,2,1,0:T(8,128)S(1)}, u32[]{:S(2)}, u32[]{:S(2)}) %all-to-all-start) | async-done | bytes 2621472 | tf_op jit(solution)/shard_map/all_to_all | solution.py:345
  57.8 0.8 shard_map.60
  58.7 1.3 collective-permute-start.1
  60.0 0.0 copy-start.1
  60.0 0.0 copy-start.6
  60.0 0.1 shard_map.67
  60.1 0.0 copy-start.4
  60.1 0.9 copy-done.4
  61.0 0.1 shard_map.66.refs_0_
  61.1 0.0 copy-start.2
  61.1 0.9 copy-done.2
  62.0 0.0 collective-permute-done.2.landed
  62.0 0.0 copy-done.1
  62.0 0.0 copy-done.6
  62.0 1.2 shard_map.62
  63.2 0.0 copy-start
  63.2 1.4 copy-done
  64.5 3.7 %all-to-all-start.1 = ((f32[16,2,16,8,128]{4,3,2,1,0:T(8,128)}), f32[16,2,16,8,128]{4,3,2,1,0:T(8,128)S(1)}, u32[]{:S(2)}, u32[]{:S(2)}) async-start(f32[16,2,16,8,128]{4,3,2,1,0:T(8,128)} %copy-done), calls=%async_computation.1 | async-start | bytes 4194304 | tf_op jit(solution)/shard_map/all_to_all | solution.py:345
  68.3 0.0 copy-start.7
  68.3 0.0 copy-start.8
  68.3 0.0 copy-start.9
  68.3 4.3 %collective-permute-start.3 = (f32[16,12,8,128]{3,2,1,0:T(8,128)}, f32[16,12,8,128]{3,2,1,0:T(8,128)}, u32[]{:S(2)}, u32[]{:S(2)}) collective-permute-start(f32[16,12,8,128]{3,2,1,0:T(8,128)} %copy-done.4), channel_id=1, source_target_pairs={{0,32},{32,0},{1,33},{33,1},{2,34},{34,2},{3,35},{35,3},{4,36},{36... | collective-permute-start | bytes 2359304 | tf_op jit(solution)/shard_map/ppermute | solution.py:348
  72.6 9.8 %collective-permute-done.1.refs_0_.refs_1_ = f32[16,8,8,128]{3,2,1,0:T(8,128)} collective-permute-done((f32[16,8,8,128]{3,2,1,0:T(8,128)}, f32[16,8,8,128]{3,2,1,0:T(8,128)}, u32[]{:S(2)}, u32[]{:S(2)}) %collective-permute-start.1) | collective-permute-done | bytes 524320 | tf_op jit(solution)/shard_map/ppermute | solution.py:348
  82.4 12.9 %all-to-all-done.1.refs_0_.refs_2_ = f32[16,2,16,8,128]{4,3,2,1,0:T(8,128)S(1)} async-done(((f32[16,2,16,8,128]{4,3,2,1,0:T(8,128)}), f32[16,2,16,8,128]{4,3,2,1,0:T(8,128)S(1)}, u32[]{:S(2)}, u32[]{:S(2)}) %all-to-all-start.1) | async-done | bytes 2097184 | tf_op jit(solution)/shard_map/all_to_all | solution.py:345
  95.3 0.0 copy-done.7
  95.3 0.0 copy-done.8
  95.3 0.0 copy-done.9
  95.3 6.1 %shard_map.64 = (f32[32,9,128]{2,1,0:T(8,128)S(1)}, f32[32,16,256]{2,1,0:T(8,128)S(1)}) custom-call(s32[1]{0:T(128)} %bitcast.first.turn, f32[16,2,16,8,128]{4,3,2,1,0:T(8,128)S(1)} %all-to-all-done.1.refs_0_.refs_2_, f32[8,128]{1,0:T(8,128)S(1)} %shard_map.63.refs_1_.refs_4_.refs_2_, bf16[256,256]{1,0:T(8,128)(2,1)S(1)} %copy-done.8, ...), custom_call_target="tpu_custom_call" | custom-call | flops 1000000000 | tf_op jit(solution)/shard_map/pallas_call | solution.py:228
  101.5 0.0 copy-start.3
  101.5 4.6 %shard_map.65.refs_6_ = f32[32,9,128]{2,1,0:T(8,128)S(1)} custom-call(s32[1]{0:T(128)} %bitcast.first.turn, f32[16,8,8,128]{3,2,1,0:T(8,128)S(1)} %shard_map.59.refs_0_, f32[16,8,8,128]{3,2,1,0:T(8,128)} %collective-permute-done.1.refs_0_.refs_1_, f32[16,2,16,8,128]{4,3,2,1,0:T(8,128)S(1)} %all-to-all-done.1.refs_0_.refs_2_, ...), custom_call_target="tpu_custom_call" | custom-call | flops 1000000000 | tf_op jit(solution)/shard_map/pallas_call | solution.py:228
  106.1 4.6 %collective-permute-done.3.refs_1_ = f32[16,12,8,128]{3,2,1,0:T(8,128)} collective-permute-done((f32[16,12,8,128]{3,2,1,0:T(8,128)}, f32[16,12,8,128]{3,2,1,0:T(8,128)}, u32[]{:S(2)}, u32[]{:S(2)}) %collective-permute-start.3) | collective-permute-done | bytes 786464 | tf_op jit(solution)/shard_map/ppermute | solution.py:348
  110.7 0.0 copy-done.3
  110.7 5.9 %shard_map.68 = f32[32,9,128]{2,1,0:T(8,128)S(1)} custom-call(s32[1]{0:T(128)} %bitcast.first.turn, f32[16,12,8,128]{3,2,1,0:T(8,128)S(1)} %copy-done.3, f32[16,12,8,128]{3,2,1,0:T(8,128)} %collective-permute-done.3.refs_1_, f32[8,128]{1,0:T(8,128)S(1)} %shard_map.63.refs_1_.refs_4_.refs_2_, bf16[256,256]{1,0:T(8,128)(2,1)S(1)} %copy-done.8, ...), custom_call_target="tpu_custom_call" | custom-call | flops 1000000000 | tf_op jit(solution)/shard_map/pallas_call | solution.py:228
  116.7 0.1 copy.9
  116.7 20.0 %all_to_all.20 = f32[16,2,9,128]{3,1,2,0:T(2,128)S(1)} all-to-all(f32[16,2,9,128]{3,1,2,0:T(2,128)S(1)} %copy.9), channel_id=1, replica_groups=mesh['y'=4,'zh'=2,'x'=4,'zl'=4,'core'=2] {'y','x'}, dimensions={0} | all-to-all | bytes 294912 | tf_op jit(solution)/shard_map/all_to_all | solution.py:345
  136.8 0.1 reduce_sum.18
  136.8 0.1 reshape.69
  137.0 0.1 reshape.72
  137.1 13.6 %all_to_all.21 = f32[16,1,144]{2,1,0:T(1,128)S(1)} all-to-all(f32[16,1,144]{2,1,0:T(1,128)S(1)} %reshape.72), channel_id=1, replica_groups=mesh['y'=4,'zh'=2,'x'=4,'zl'=4,'core'=2] {'zh','zl','core'}, dimensions={0} | all-to-all | bytes 18432 | tf_op jit(solution)/shard_map/all_to_all | solution.py:384
  150.7 0.1 negate_bitcast_fusion
  150.8 0.1 stack.2
  150.9 0.6 copy.14
  (9 shorter events, 0.2 us)
Async XLA Ops:
  1.9 23.3 %collective-permute-start = (f32[16,8,8,128]{3,2,1,0:T(8,128)}, f32[16,8,8,128]{3,2,1,0:T(8,128)S(1)}, u32[]{:S(2)}, u32[]{:S(2)}) collective-permute-start(f32[16,8,8,128]{3,2,1,0:T(8,128)} %shard_map.55), channel_id=1, source_target_pairs={{0,32},{32,0},{1,33},{33,1},{2,34},{34,2},{3,35},{35,3},{4,36},{36... | collective-permute-start | bytes 1572872 | tf_op jit(solution)/shard_map/ppermute | solution.py:348
  13.3 44.5 %all-to-all-start = ((f32[16,2,20,8,128]{4,3,2,1,0:T(8,128)}), f32[16,2,20,8,128]{4,3,2,1,0:T(8,128)S(1)}, u32[]{:S(2)}, u32[]{:S(2)}) async-start(f32[16,2,20,8,128]{4,3,2,1,0:T(8,128)} %shard_map.56), calls=%async_computation | async-start | bytes 5242880 | tf_op jit(solution)/shard_map/all_to_all | solution.py:345
  22.0 39.9 %collective-permute-start.2 = (f32[16,8,8,128]{3,2,1,0:T(8,128)}, f32[16,8,8,128]{3,2,1,0:T(8,128)}, u32[]{:S(2)}, u32[]{:S(2)}) collective-permute-start(f32[16,8,8,128]{3,2,1,0:T(8,128)} %shard_map.61), channel_id=1, source_target_pairs={{0,32},{32,0},{1,33},{33,1},{2,34},{34,2},{3,35},{35,3},{4,36},{36... | collective-permute-start | bytes 1572872 | tf_op jit(solution)/shard_map/ppermute | solution.py:348
  25.3 0.8 copy-start.5
  58.7 23.7 %collective-permute-start.1 = (f32[16,8,8,128]{3,2,1,0:T(8,128)}, f32[16,8,8,128]{3,2,1,0:T(8,128)}, u32[]{:S(2)}, u32[]{:S(2)}) collective-permute-start(f32[16,8,8,128]{3,2,1,0:T(8,128)} %shard_map.60), channel_id=1, source_target_pairs={{0,32},{32,0},{1,33},{33,1},{2,34},{34,2},{3,35},{35,3},{4,36},{36... | collective-permute-start | bytes 1572872 | tf_op jit(solution)/shard_map/ppermute | solution.py:348
  60.0 2.0 %copy-start.1 = (f32[16,16,8,128]{3,2,1,0:T(8,128)S(1)}, f32[16,16,8,128]{3,2,1,0:T(8,128)}, u32[]{:S(2)}) copy-start(f32[16,16,8,128]{3,2,1,0:T(8,128)} %shard_map.57.kept) | copy-start | bytes 3145732
  60.0 1.9 %copy-start.6 = (f32[16,8,8,128]{3,2,1,0:T(8,128)S(1)}, f32[16,8,8,128]{3,2,1,0:T(8,128)}, u32[]{:S(2)}) copy-start(f32[16,8,8,128]{3,2,1,0:T(8,128)} %copy-done.5) | copy-start | bytes 1572868
  60.1 0.9 copy-start.4
  61.1 0.9 copy-start.2
  63.2 1.4 copy-start
  64.5 30.7 %all-to-all-start.1 = ((f32[16,2,16,8,128]{4,3,2,1,0:T(8,128)}), f32[16,2,16,8,128]{4,3,2,1,0:T(8,128)S(1)}, u32[]{:S(2)}, u32[]{:S(2)}) async-start(f32[16,2,16,8,128]{4,3,2,1,0:T(8,128)} %copy-done), calls=%async_computation.1 | async-start | bytes 4194304 | tf_op jit(solution)/shard_map/all_to_all | solution.py:345
  68.3 27.0 %copy-start.7 = (bf16[256,256]{1,0:T(8,128)(2,1)S(1)}, bf16[256,256]{1,0:T(8,128)(2,1)}, u32[]{:S(2)}) copy-start(bf16[256,256]{1,0:T(8,128)(2,1)} %constant.75.clone.refs_3_.refs_6_.refs_4_) | copy-start | bytes 393220
  68.3 27.0 %copy-start.8 = (bf16[256,256]{1,0:T(8,128)(2,1)S(1)}, bf16[256,256]{1,0:T(8,128)(2,1)}, u32[]{:S(2)}) copy-start(bf16[256,256]{1,0:T(8,128)(2,1)} %constant.74.clone.refs_2_.refs_5_.refs_3_) | copy-start | bytes 393220
  68.3 27.0 %copy-start.9 = (f32[32,2,128]{2,1,0:T(2,128)S(1)}, f32[32,2,128]{2,1,0:T(2,128)}, u32[]{:S(2)}) copy-start(f32[32,2,128]{2,1,0:T(2,128)} %constant.76.clone.refs_4_.refs_7_.refs_5_) | copy-start | bytes 98308
  68.3 42.4 %collective-permute-start.3 = (f32[16,12,8,128]{3,2,1,0:T(8,128)}, f32[16,12,8,128]{3,2,1,0:T(8,128)}, u32[]{:S(2)}, u32[]{:S(2)}) collective-permute-start(f32[16,12,8,128]{3,2,1,0:T(8,128)} %copy-done.4), channel_id=1, source_target_pairs={{0,32},{32,0},{1,33},{33,1},{2,34},{34,2},{3,35},{35,3},{4,36},{36... | collective-permute-start | bytes 2359304 | tf_op jit(solution)/shard_map/ppermute | solution.py:348
  101.5 9.3 %copy-start.3 = (f32[16,12,8,128]{3,2,1,0:T(8,128)S(1)}, f32[16,12,8,128]{3,2,1,0:T(8,128)}, u32[]{:S(2)}) copy-start(f32[16,12,8,128]{3,2,1,0:T(8,128)} %copy-done.2) | copy-start | bytes 2359300

commit v15 on v14

--- a/solution.py
+++ b/solution.py
@@ -203,8 +203,8 @@
             one, two = memory(a, b), memory(b, a)
             results += [one[0] + two[0], two[1] - one[1]]
         for i, result in enumerate(results):
-            spot_out, row = plane * 2 + half, pl.ds(i, 1)
-            out[spot_out, row, :] = before[spot_out, row, :] + jnp.sum(result * scale, axis=0, keepdims=True)
+            row = pl.ds(half * PAIRS + i, 1)
+            out[plane, row, :] = before[plane, row, :] + jnp.sum(result * scale, axis=0, keepdims=True)
         if spilled:
             refs[6][m] = field[m, ORB]
 
@@ -221,7 +221,7 @@
 def collide(turn, fields, weights, high, low, twiddle, before, older=(), spilled=False):
     stacked, joined = len(fields) == 1, int(len(older) > 0)
     count = ORB + 1 if stacked else ORB - joined
-    shapes = [jax.ShapeDtypeStruct((ROWS, PAIRS, LANES), jnp.float32)]
+    shapes = [jax.ShapeDtypeStruct((PLANE, 2 * PAIRS, LANES), jnp.float32)]
     if spilled:
         shapes.append(jax.ShapeDtypeStruct((ROWS, 2 * SLOTS, 2 * LANES), jnp.float32))
     inputs = (*fields, *older, weights, high, low, twiddle, before)
@@ -351,7 +351,7 @@
         return collide(turn_flag, fields, weights, high, low, twiddle, partial, **more)
 
     turn_flag = zh.reshape(1).astype(jnp.int32)
-    partial = jnp.zeros((ROWS, PAIRS, LANES), jnp.float32)
+    partial = jnp.zeros((PLANE, 2 * PAIRS, LANES), jnp.float32)
     fence = lax.optimization_barrier
     early = [[(0, 0), (1, 0)], [(2, 0), (0, 1)]]
     late = [[(1, 1), (2, 1)], [(0, 2), (1, 2), (2, 2)]]
@@ -377,8 +377,7 @@
     (partial,) = work(one, partial, weights, older=(zero, sigma))
     partial, two = fence((partial, two))
     (partial,) = work(two, partial, weights)
-    blocks = partial.reshape(PLANE, 2, PAIRS, LANES)
-    owned = jnp.sum(spread(blocks), axis=0)
+    owned = jnp.sum(spread(partial), axis=0)
     share = LANES // 8
     shares = owned.reshape(2, PAIRS, 8, share).transpose(0, 2, 1, 3).reshape(PLANE, 1, PAIRS * share)
     shares = lax.all_to_all(shares, ("zh", "zl", "core"), split_axis=0, concat_axis=0)

time: 152 us -> 152 us (level)
  no operation moved by 1% of the time
where the time goes in v15:
time: 152 us
  waiting for transfers between devices  59.1 us (39%)
  blocking collectives  33.9 us (22%)
  Pallas kernels  28.6 us (19%)
  starting transfers between devices  24 us (16%)
  local copies, waits for them, and re-layouts  4.96 us (3%)
    all_to_all x2, waiting for transfers between devices, spread(): return lax.all_to_all(value, ('y', 'x'), split_axis=0, concat_axis=0)  44.7 us
    all_to_all x1, blocking collectives, spread(): return lax.all_to_all(value, ('y', 'x'), split_axis=0, concat_axis=0)  20.3 us
    pallas_call x3, Pallas kernels, collide(): pl.pallas_call(functools.partial(kernel, count, stacked, joined, spilled)...  16.7 us
    ppermute x4, waiting for transfers between devices, move(): return lax.ppermute(value, 'zh', [(0, 1), (1, 0)])  14.4 us
    all_to_all x1, blocking collectives, per_device(): lax.all_to_all(shares, ('zh', 'zl', 'core'), split_axis=0, concat_axis=0)  13.6 us
    ppermute x4, starting transfers between devices, move(): return lax.ppermute(value, 'zh', [(0, 1), (1, 0)])  13.5 us
    all_to_all x2, starting transfers between devices, spread(): return lax.all_to_all(value, ('y', 'x'), split_axis=0, concat_axis=0)  10.5 us
    pallas_call x4, Pallas kernels, arrange(): pl.pallas_call(functools.partial(arrange_kernel, blocks, ways), out_shape...  9.77 us
  transfers between devices with their start and end apart: 6, of which 4 were waited for; matrix products, arithmetic and copies ran while one was open for 0% of the time, Pallas kernels for 14%

profile of v15, /device:TPU:1, one launch (start us, length us, event | category | flops | bytes accessed | tf_op | source)
XLA Modules:
  0.0 151.6 jit_solution(15811507909703739503)
XLA Ops:
  0.0 1.9 %shard_map.55 = f32[16,8,8,128]{3,2,1,0:T(8,128)} custom-call(s32[1]{0:T(128)} %bitcast.first.turn, f32[12,3,2,16,8,128]{5,4,3,2,1,0:T(8,128)} %bitcast.28), custom_call_target="tpu_custom_call" | custom-call | bytes 3200000 | tf_op jit(solution)/shard_map/pallas_call | solution.py:261
  1.9 7.8 %collective-permute-start = (f32[16,8,8,128]{3,2,1,0:T(8,128)}, f32[16,8,8,128]{3,2,1,0:T(8,128)S(1)}, u32[]{:S(2)}, u32[]{:S(2)}) collective-permute-start(f32[16,8,8,128]{3,2,1,0:T(8,128)} %shard_map.55), channel_id=1, source_target_pairs={{0,32},{32,0},{1,33},{33,1},{2,34},{34,2},{3,35},{35,3},{4,36},{36... | collective-permute-start | bytes 1572872 | tf_op jit(solution)/shard_map/ppermute | solution.py:348
  9.8 3.5 %shard_map.56 = f32[16,2,20,8,128]{4,3,2,1,0:T(8,128)} custom-call(s32[1]{0:T(128)} %bitcast.first.turn, f32[12,3,2,16,8,128]{5,4,3,2,1,0:T(8,128)} %bitcast.29), custom_call_target="tpu_custom_call" | custom-call | bytes 3200000 | tf_op jit(solution)/shard_map/pallas_call | solution.py:261
  13.3 6.8 %all-to-all-start = ((f32[16,2,20,8,128]{4,3,2,1,0:T(8,128)}), f32[16,2,20,8,128]{4,3,2,1,0:T(8,128)S(1)}, u32[]{:S(2)}, u32[]{:S(2)}) async-start(f32[16,2,20,8,128]{4,3,2,1,0:T(8,128)} %shard_map.56), calls=%async_computation | async-start | bytes 5242880 | tf_op jit(solution)/shard_map/all_to_all | solution.py:345
  20.1 1.9 %shard_map.61 = f32[16,8,8,128]{3,2,1,0:T(8,128)} custom-call(s32[1]{0:T(128)} %bitcast.first.turn, f32[12,3,2,16,8,128]{5,4,3,2,1,0:T(8,128)} %bitcast.30), custom_call_target="tpu_custom_call" | custom-call | bytes 3200000 | tf_op jit(solution)/shard_map/pallas_call | solution.py:261
  22.0 0.1 collective-permute-start.2
  22.1 2.4 %shard_map.57.kept = f32[16,16,8,128]{3,2,1,0:T(8,128)} custom-call(s32[1]{0:T(128)} %bitcast.first.turn, f32[12,3,2,16,8,128]{5,4,3,2,1,0:T(8,128)} %bitcast.31), custom_call_target="tpu_custom_call" | custom-call | bytes 3200000 | tf_op jit(solution)/shard_map/pallas_call | solution.py:261
  25.2 0.1 broadcast_in_dim.19.given
  25.3 0.0 collective-permute-done.refs_0_.ahead
  25.3 0.0 copy-start.5
  25.3 0.8 copy-done.5
  26.1 31.8 %all-to-all-done.whole = f32[16,2,20,8,128]{4,3,2,1,0:T(8,128)S(1)} async-done(((f32[16,2,20,8,128]{4,3,2,1,0:T(8,128)}), f32[16,2,20,8,128]{4,3,2,1,0:T(8,128)S(1)}, u32[]{:S(2)}, u32[]{:S(2)}) %all-to-all-start) | async-done | bytes 2621472 | tf_op jit(solution)/shard_map/all_to_all | solution.py:345
  57.8 0.8 shard_map.60
  58.7 1.3 collective-permute-start.1
  60.0 0.0 copy-start.1
  60.0 0.0 copy-start.6
  60.0 0.1 shard_map.67
  60.1 0.0 copy-start.4
  60.1 0.9 copy-done.4
  61.0 0.1 shard_map.66.refs_0_
  61.1 0.0 copy-start.2
  61.1 0.9 copy-done.2
  62.0 0.0 collective-permute-done.2.landed
  62.0 0.0 copy-done.1
  62.0 0.0 copy-done.6
  62.0 1.2 shard_map.62
  63.2 0.0 copy-start
  63.2 1.4 copy-done
  64.5 3.7 %all-to-all-start.1 = ((f32[16,2,16,8,128]{4,3,2,1,0:T(8,128)}), f32[16,2,16,8,128]{4,3,2,1,0:T(8,128)S(1)}, u32[]{:S(2)}, u32[]{:S(2)}) async-start(f32[16,2,16,8,128]{4,3,2,1,0:T(8,128)} %copy-done), calls=%async_computation.1 | async-start | bytes 4194304 | tf_op jit(solution)/shard_map/all_to_all | solution.py:345
  68.3 0.0 copy-start.7
  68.3 0.0 copy-start.8
  68.3 0.0 copy-start.9
  68.3 4.3 %collective-permute-start.3 = (f32[16,12,8,128]{3,2,1,0:T(8,128)}, f32[16,12,8,128]{3,2,1,0:T(8,128)}, u32[]{:S(2)}, u32[]{:S(2)}) collective-permute-start(f32[16,12,8,128]{3,2,1,0:T(8,128)} %copy-done.4), channel_id=1, source_target_pairs={{0,32},{32,0},{1,33},{33,1},{2,34},{34,2},{3,35},{35,3},{4,36},{36... | collective-permute-start | bytes 2359304 | tf_op jit(solution)/shard_map/ppermute | solution.py:348
  72.6 9.8 %collective-permute-done.1.refs_0_.refs_1_ = f32[16,8,8,128]{3,2,1,0:T(8,128)} collective-permute-done((f32[16,8,8,128]{3,2,1,0:T(8,128)}, f32[16,8,8,128]{3,2,1,0:T(8,128)}, u32[]{:S(2)}, u32[]{:S(2)}) %collective-permute-start.1) | collective-permute-done | bytes 524320 | tf_op jit(solution)/shard_map/ppermute | solution.py:348
  82.4 12.9 %all-to-all-done.1.refs_0_.refs_2_ = f32[16,2,16,8,128]{4,3,2,1,0:T(8,128)S(1)} async-done(((f32[16,2,16,8,128]{4,3,2,1,0:T(8,128)}), f32[16,2,16,8,128]{4,3,2,1,0:T(8,128)S(1)}, u32[]{:S(2)}, u32[]{:S(2)}) %all-to-all-start.1) | async-done | bytes 2097184 | tf_op jit(solution)/shard_map/all_to_all | solution.py:345
  95.3 0.0 copy-done.7
  95.3 0.0 copy-done.8
  95.3 0.0 copy-done.9
  95.3 6.1 %shard_map.64 = (f32[16,18,128]{2,1,0:T(8,128)S(1)}, f32[32,16,256]{2,1,0:T(8,128)S(1)}) custom-call(s32[1]{0:T(128)} %bitcast.first.turn, f32[16,2,16,8,128]{4,3,2,1,0:T(8,128)S(1)} %all-to-all-done.1.refs_0_.refs_2_, f32[8,128]{1,0:T(8,128)S(1)} %shard_map.63.refs_1_.refs_4_.refs_2_, bf16[256,256]{1,0:T(8,128)(2,1)S(1)} %copy-done.8, ...), custom_call_target="tpu_custom_call" | custom-call | flops 1000000000 | tf_op jit(solution)/shard_map/pallas_call | solution.py:228
  101.5 0.0 copy-start.3
  101.5 4.6 %shard_map.65.refs_6_ = f32[16,18,128]{2,1,0:T(8,128)S(1)} custom-call(s32[1]{0:T(128)} %bitcast.first.turn, f32[16,8,8,128]{3,2,1,0:T(8,128)S(1)} %shard_map.59.refs_0_, f32[16,8,8,128]{3,2,1,0:T(8,128)} %collective-permute-done.1.refs_0_.refs_1_, f32[16,2,16,8,128]{4,3,2,1,0:T(8,128)S(1)} %all-to-all-done.1.refs_0_.refs_2_, ...), custom_call_target="tpu_custom_call" | custom-call | flops 1000000000 | tf_op jit(solution)/shard_map/pallas_call | solution.py:228
  106.1 4.6 %collective-permute-done.3.refs_1_ = f32[16,12,8,128]{3,2,1,0:T(8,128)} collective-permute-done((f32[16,12,8,128]{3,2,1,0:T(8,128)}, f32[16,12,8,128]{3,2,1,0:T(8,128)}, u32[]{:S(2)}, u32[]{:S(2)}) %collective-permute-start.3) | collective-permute-done | bytes 786464 | tf_op jit(solution)/shard_map/ppermute | solution.py:348
  110.7 0.0 copy-done.3
  110.7 5.9 %shard_map.68 = f32[16,18,128]{2,1,0:T(8,128)S(1)} custom-call(s32[1]{0:T(128)} %bitcast.first.turn, f32[16,12,8,128]{3,2,1,0:T(8,128)S(1)} %copy-done.3, f32[16,12,8,128]{3,2,1,0:T(8,128)} %collective-permute-done.3.refs_1_, f32[8,128]{1,0:T(8,128)S(1)} %shard_map.63.refs_1_.refs_4_.refs_2_, bf16[256,256]{1,0:T(8,128)(2,1)S(1)} %copy-done.8, ...), custom_call_target="tpu_custom_call" | custom-call | flops 1000000000 | tf_op jit(solution)/shard_map/pallas_call | solution.py:228
  116.7 20.3 %all_to_all.20 = f32[16,18,128]{2,1,0:T(8,128)S(1)} all-to-all(f32[16,18,128]{2,1,0:T(8,128)S(1)} %shard_map.68), channel_id=1, replica_groups=mesh['y'=4,'zh'=2,'x'=4,'zl'=4,'core'=2] {'y','x'}, dimensions={0} | all-to-all | bytes 294912 | tf_op jit(solution)/shard_map/all_to_all | solution.py:345
  137.0 0.1 reshape.65
  137.1 0.1 reshape.68
  137.2 13.6 %all_to_all.21 = f32[16,1,144]{2,1,0:T(1,128)S(1)} all-to-all(f32[16,1,144]{2,1,0:T(1,128)S(1)} %reshape.68), channel_id=1, replica_groups=mesh['y'=4,'zh'=2,'x'=4,'zl'=4,'core'=2] {'zh','zl','core'}, dimensions={0} | all-to-all | bytes 18432 | tf_op jit(solution)/shard_map/all_to_all | solution.py:383
  150.9 0.1 negate_bitcast_fusion
  150.9 0.1 stack.2
  151.0 0.6 copy.12
  (10 shorter events, 0.2 us)
Async XLA Ops:
  1.9 23.3 %collective-permute-start = (f32[16,8,8,128]{3,2,1,0:T(8,128)}, f32[16,8,8,128]{3,2,1,0:T(8,128)S(1)}, u32[]{:S(2)}, u32[]{:S(2)}) collective-permute-start(f32[16,8,8,128]{3,2,1,0:T(8,128)} %shard_map.55), channel_id=1, source_target_pairs={{0,32},{32,0},{1,33},{33,1},{2,34},{34,2},{3,35},{35,3},{4,36},{36... | collective-permute-start | bytes 1572872 | tf_op jit(solution)/shard_map/ppermute | solution.py:348
  13.3 44.5 %all-to-all-start = ((f32[16,2,20,8,128]{4,3,2,1,0:T(8,128)}), f32[16,2,20,8,128]{4,3,2,1,0:T(8,128)S(1)}, u32[]{:S(2)}, u32[]{:S(2)}) async-start(f32[16,2,20,8,128]{4,3,2,1,0:T(8,128)} %shard_map.56), calls=%async_computation | async-start | bytes 5242880 | tf_op jit(solution)/shard_map/all_to_all | solution.py:345
  22.0 39.9 %collective-permute-start.2 = (f32[16,8,8,128]{3,2,1,0:T(8,128)}, f32[16,8,8,128]{3,2,1,0:T(8,128)}, u32[]{:S(2)}, u32[]{:S(2)}) collective-permute-start(f32[16,8,8,128]{3,2,1,0:T(8,128)} %shard_map.61), channel_id=1, source_target_pairs={{0,32},{32,0},{1,33},{33,1},{2,34},{34,2},{3,35},{35,3},{4,36},{36... | collective-permute-start | bytes 1572872 | tf_op jit(solution)/shard_map/ppermute | solution.py:348
  25.3 0.8 copy-start.5
  58.7 23.7 %collective-permute-start.1 = (f32[16,8,8,128]{3,2,1,0:T(8,128)}, f32[16,8,8,128]{3,2,1,0:T(8,128)}, u32[]{:S(2)}, u32[]{:S(2)}) collective-permute-start(f32[16,8,8,128]{3,2,1,0:T(8,128)} %shard_map.60), channel_id=1, source_target_pairs={{0,32},{32,0},{1,33},{33,1},{2,34},{34,2},{3,35},{35,3},{4,36},{36... | collective-permute-start | bytes 1572872 | tf_op jit(solution)/shard_map/ppermute | solution.py:348
  60.0 2.0 %copy-start.1 = (f32[16,16,8,128]{3,2,1,0:T(8,128)S(1)}, f32[16,16,8,128]{3,2,1,0:T(8,128)}, u32[]{:S(2)}) copy-start(f32[16,16,8,128]{3,2,1,0:T(8,128)} %shard_map.57.kept) | copy-start | bytes 3145732
  60.0 1.9 %copy-start.6 = (f32[16,8,8,128]{3,2,1,0:T(8,128)S(1)}, f32[16,8,8,128]{3,2,1,0:T(8,128)}, u32[]{:S(2)}) copy-start(f32[16,8,8,128]{3,2,1,0:T(8,128)} %copy-done.5) | copy-start | bytes 1572868
  60.1 0.9 copy-start.4
  61.1 0.9 copy-start.2
  63.2 1.4 copy-start
  64.5 30.7 %all-to-all-start.1 = ((f32[16,2,16,8,128]{4,3,2,1,0:T(8,128)}), f32[16,2,16,8,128]{4,3,2,1,0:T(8,128)S(1)}, u32[]{:S(2)}, u32[]{:S(2)}) async-start(f32[16,2,16,8,128]{4,3,2,1,0:T(8,128)} %copy-done), calls=%async_computation.1 | async-start | bytes 4194304 | tf_op jit(solution)/shard_map/all_to_all | solution.py:345
  68.3 27.0 %copy-start.7 = (bf16[256,256]{1,0:T(8,128)(2,1)S(1)}, bf16[256,256]{1,0:T(8,128)(2,1)}, u32[]{:S(2)}) copy-start(bf16[256,256]{1,0:T(8,128)(2,1)} %constant.75.clone.refs_3_.refs_6_.refs_4_) | copy-start | bytes 393220
  68.3 27.0 %copy-start.8 = (bf16[256,256]{1,0:T(8,128)(2,1)S(1)}, bf16[256,256]{1,0:T(8,128)(2,1)}, u32[]{:S(2)}) copy-start(bf16[256,256]{1,0:T(8,128)(2,1)} %constant.74.clone.refs_2_.refs_5_.refs_3_) | copy-start | bytes 393220
  68.3 27.0 %copy-start.9 = (f32[32,2,128]{2,1,0:T(2,128)S(1)}, f32[32,2,128]{2,1,0:T(2,128)}, u32[]{:S(2)}) copy-start(f32[32,2,128]{2,1,0:T(2,128)} %constant.76.clone.refs_4_.refs_7_.refs_5_) | copy-start | bytes 98308
  68.3 42.4 %collective-permute-start.3 = (f32[16,12,8,128]{3,2,1,0:T(8,128)}, f32[16,12,8,128]{3,2,1,0:T(8,128)}, u32[]{:S(2)}, u32[]{:S(2)}) collective-permute-start(f32[16,12,8,128]{3,2,1,0:T(8,128)} %copy-done.4), channel_id=1, source_target_pairs={{0,32},{32,0},{1,33},{33,1},{2,34},{34,2},{3,35},{35,3},{4,36},{36... | collective-permute-start | bytes 2359304 | tf_op jit(solution)/shard_map/ppermute | solution.py:348
  101.5 9.3 %copy-start.3 = (f32[16,12,8,128]{3,2,1,0:T(8,128)S(1)}, f32[16,12,8,128]{3,2,1,0:T(8,128)}, u32[]{:S(2)}) copy-start(f32[16,12,8,128]{3,2,1,0:T(8,128)} %copy-done.2) | copy-start | bytes 2359300
